TPU v7x, 128 devices: a whole 4x4x4 slice. The times are simulated.
128 devices in a mesh: fsdp: 16 (over y, x_lo, core), seq: 8 (over x_hi, z).
Axes of the slice: x: 4 (x_hi: 2, x_lo: 2; x = x_hi * 2 + x_lo), y: 4, z: 4, core: 2. Of those that a mesh axis runs over, the one named last changes fastest.
Arguments:
- query_raw: bfloat16 [16384, 3072], P(('fsdp', 'seq')), may hold values from -200 to 200
- key_raw: bfloat16 [16384, 3072], P(('fsdp', 'seq')), may hold values from -200 to 200
- value_in: bfloat16 [16384, 3072], P(('fsdp', 'seq')), may hold values from -6 to 6
- query_dot: bfloat16 [16384, 3072], P(('fsdp', 'seq')), may hold values from -6 to 6
- key_dot: bfloat16 [16384, 3072], P(('fsdp', 'seq')), may hold values from -6 to 6
- value_dot: bfloat16 [16384, 3072], P(('fsdp', 'seq')), may hold values from -6 to 6
- gain_query: float32 [3072], replicated, may hold values from 1 to 2
- gain_key: float32 [3072], replicated, may hold values from 1 to 2
- out_weight: bfloat16 [3072, 5120], P(None, 'fsdp'), may hold values from -0.109375 to 0.109375
- gate_table: float32 [64, 5120], replicated, may hold values from 0.5 to 2
- gate_dot_table: float32 [64, 5120], replicated, may hold values from -6 to 6
- time_index: int32 [16], P('fsdp'), may hold values from 0 to 63
Outputs:
- gated_branch: bfloat16 [16384, 5120], P(('fsdp', 'seq'))
- branch_tangent: bfloat16 [16384, 5120], P(('fsdp', 'seq'))
All inputs are finite; a program needn't handle non-finite values.
Results may differ from a plain program's by a relative error of at most 0.012.
Values may be sent and summed in bfloat16 or wider, within the bound.
No kernel may reach another device: no remote copies, remote signals or barrier semaphores. Data moves between devices by JAX's collectives and lax.ppermute only.
A program may use at most 128 MiB of HBM per device.

v0:
```python
import math

import jax
import jax.numpy as jnp
from jax import lax
from jax.sharding import PartitionSpec as P

HD = 128


eps = 1e-06


def normalize(raw, raw_dot, gain):
    signal = raw.astype(jnp.float32)
    signal_dot = raw_dot.astype(jnp.float32)
    inverse = lax.rsqrt(jnp.mean(signal * signal, axis=-1, keepdims=True) + eps)
    inner = jnp.mean(signal * signal_dot, axis=-1, keepdims=True)
    normed = gain * signal * inverse
    normed_dot = gain * (signal_dot * inverse - signal * inverse**3 * inner)
    return (normed.astype(jnp.bfloat16), normed_dot.astype(jnp.bfloat16))


def block_step(inputs, key_rows, value_rows, key_tan, value_tan, scale):
    query_block, query_block_tan = inputs
    scores = (
        jnp.einsum("qnd,knd->nqk", query_block, key_rows, preferred_element_type=jnp.float32)
        * scale
    )
    scores_dot = (
        jnp.einsum("qnd,knd->nqk", query_block_tan, key_rows, preferred_element_type=jnp.float32)
        + jnp.einsum("qnd,knd->nqk", query_block, key_tan, preferred_element_type=jnp.float32)
    ) * scale
    row_peak = jnp.max(scores, axis=-1, keepdims=True)
    weights = jnp.exp(scores - row_peak)
    prob = weights / jnp.sum(weights, axis=-1, keepdims=True)
    prob_dot = prob * (scores_dot - jnp.sum(prob * scores_dot, axis=-1, keepdims=True))
    prob_low = prob.astype(jnp.bfloat16)
    prob_dot_low = prob_dot.astype(jnp.bfloat16)
    attn = jnp.einsum("nqk,knd->qnd", prob_low, value_rows, preferred_element_type=jnp.float32)
    attn_dot = jnp.einsum(
        "nqk,knd->qnd", prob_dot_low, value_rows, preferred_element_type=jnp.float32
    ) + jnp.einsum("nqk,knd->qnd", prob_low, value_tan, preferred_element_type=jnp.float32)
    return (attn.astype(jnp.bfloat16), attn_dot.astype(jnp.bfloat16))


def attend(pieces):
    length = pieces[0].shape[0]
    head_count = pieces[0].shape[2]
    width = pieces[0].shape[3]
    query_rows, key_rows, value_rows, query_tan, key_tan, value_tan = [
        a.reshape(length, head_count, width) for a in pieces
    ]
    block = math.gcd(length, 512)
    scale = width ** (-0.5)
    shaped = (
        query_rows.reshape(length // block, block, head_count, width),
        query_tan.reshape(length // block, block, head_count, width),
    )

    def one_block(inputs):
        return block_step(inputs, key_rows, value_rows, key_tan, value_tan, scale)

    attn, attn_dot = lax.map(one_block, shaped)
    return (
        attn.reshape(length, 1, head_count, width),
        attn_dot.reshape(length, 1, head_count, width),
    )


def local(
    query_raw,
    key_raw,
    value_in,
    query_dot,
    key_dot,
    value_dot,
    gain_query,
    gain_key,
    out_weight,
    gate_table,
    gate_dot_table,
    time_index,
):
    tokens = query_raw.shape[0]
    head_width = query_raw.shape[1]
    groups = lax.axis_size("seq")
    layout = (tokens, groups, head_width // (HD * groups), HD)
    query_hat, query_hat_dot = normalize(query_raw, query_dot, gain_query)
    key_hat, key_hat_dot = normalize(key_raw, key_dot, gain_key)
    attn, attn_dot = attend(
        (
            lax.all_to_all(
                query_hat.reshape(layout), "seq", split_axis=1, concat_axis=0, tiled=True
            ),
            lax.all_to_all(key_hat.reshape(layout), "seq", split_axis=1, concat_axis=0, tiled=True),
            lax.all_to_all(
                value_in.reshape(layout), "seq", split_axis=1, concat_axis=0, tiled=True
            ),
            lax.all_to_all(
                query_hat_dot.reshape(layout), "seq", split_axis=1, concat_axis=0, tiled=True
            ),
            lax.all_to_all(
                key_hat_dot.reshape(layout), "seq", split_axis=1, concat_axis=0, tiled=True
            ),
            lax.all_to_all(
                value_dot.reshape(layout), "seq", split_axis=1, concat_axis=0, tiled=True
            ),
        )
    )
    attn, attn_dot = (
        lax.all_to_all(attn, "seq", split_axis=0, concat_axis=1, tiled=True),
        lax.all_to_all(attn_dot, "seq", split_axis=0, concat_axis=1, tiled=True),
    )
    stacked = jnp.stack((attn.reshape(tokens, head_width), attn_dot.reshape(tokens, head_width)))
    flat = stacked.reshape(2 * tokens, head_width)
    projected = jnp.dot(
        flat,
        lax.all_gather(out_weight, "fsdp", axis=1, tiled=True),
        preferred_element_type=jnp.float32,
    )
    primal_proj = projected[:tokens]
    tangent_proj = projected[tokens:]
    gate = lax.dynamic_index_in_dim(gate_table, time_index[0], 0, keepdims=False)
    gate_dot = lax.dynamic_index_in_dim(gate_dot_table, time_index[0], 0, keepdims=False)
    gated_branch = (gate * primal_proj).astype(jnp.bfloat16)
    branch_tangent = (gate_dot * primal_proj + gate * tangent_proj).astype(jnp.bfloat16)
    return (gated_branch, branch_tangent)


def solution(mesh):
    return jax.shard_map(
        local,
        mesh=mesh,
        in_specs=(
            P(("fsdp", "seq"), None),
            P(("fsdp", "seq"), None),
            P(("fsdp", "seq"), None),
            P(("fsdp", "seq"), None),
            P(("fsdp", "seq"), None),
            P(("fsdp", "seq"), None),
            P(),
            P(),
            P(None, "fsdp"),
            P(),
            P(),
            P("fsdp"),
        ),
        out_specs=(P(("fsdp", "seq"), None), P(("fsdp", "seq"), None)),
        check_vma=False,
    )
```

profile of v0, /device:TPU:1, one launch (start us, length us, event | category | flops | bytes accessed | tf_op | source)
XLA Modules:
  0.0 268.5 jit_solution(13331645894202685754)
XLA Ops:
  12.2 8.3 %all-to-all-start.1 = ((bf16[128,8,3,128]{0,3,2,1:T(8,128)(2,1)}), bf16[128,8,3,128]{0,3,2,1:T(8,128)(2,1)S(1)}, u32[]{:S(2)}, u32[]{:S(2)}) async-start(bf16[128,8,3,128]{0,3,2,1:T(8,128)(2,1)} %bitcast.12), calls=%async_computation.1 | async-start | bytes 1572864 | tf_op jit(solution)/shard_map/all_to_all | solution.py:96
  22.9 16.4 %all-to-all-done.1 = bf16[128,8,3,128]{0,3,2,1:T(8,128)(2,1)S(1)} async-done(((bf16[128,8,3,128]{0,3,2,1:T(8,128)(2,1)}), bf16[128,8,3,128]{0,3,2,1:T(8,128)(2,1)S(1)}, u32[]{:S(2)}, u32[]{:S(2)}) %all-to-all-start.1) | async-done | bytes 786464 | tf_op jit(solution)/shard_map/all_to_all | solution.py:96
  39.3 3.5 %all-to-all-start.4 = ((bf16[128,8,3,128]{0,3,2,1:T(8,128)(2,1)}), bf16[128,8,3,128]{0,3,2,1:T(8,128)(2,1)S(1)}, u32[]{:S(2)}, u32[]{:S(2)}) async-start(bf16[128,8,3,128]{0,3,2,1:T(8,128)(2,1)} %bitcast.128), calls=%async_computation.4 | async-start | bytes 1572864 | tf_op jit(solution)/shard_map/all_to_all | solution.py:103
  44.7 17.9 %all-to-all-done.4 = bf16[128,8,3,128]{0,3,2,1:T(8,128)(2,1)S(1)} async-done(((bf16[128,8,3,128]{0,3,2,1:T(8,128)(2,1)}), bf16[128,8,3,128]{0,3,2,1:T(8,128)(2,1)S(1)}, u32[]{:S(2)}, u32[]{:S(2)}) %all-to-all-start.4) | async-done | bytes 786464 | tf_op jit(solution)/shard_map/all_to_all | solution.py:103
  62.6 24.2 %all_to_all.120 = bf16[128,8,3,128]{0,3,2,1:T(8,128)(2,1)S(1)} all-to-all(bf16[128,8,3,128]{0,3,2,1:T(8,128)(2,1)} %bitcast.130), channel_id=1, replica_groups=mesh['fsdp'=16,'seq'=8] {'seq'}, dimensions={1} | all-to-all | bytes 1572864 | tf_op jit(solution)/shard_map/all_to_all | solution.py:93
  86.8 3.5 %all-to-all-start.3 = ((bf16[128,8,3,128]{0,3,2,1:T(8,128)(2,1)}), bf16[128,8,3,128]{0,3,2,1:T(8,128)(2,1)S(1)}, u32[]{:S(2)}, u32[]{:S(2)}) async-start(bf16[128,8,3,128]{0,3,2,1:T(8,128)(2,1)} %bitcast.129), calls=%async_computation.3 | async-start | bytes 1572864 | tf_op jit(solution)/shard_map/all_to_all | solution.py:100
  90.4 2.4 copy.76
  92.7 16.7 %all-to-all-done.3 = bf16[128,8,3,128]{0,3,2,1:T(8,128)(2,1)S(1)} async-done(((bf16[128,8,3,128]{0,3,2,1:T(8,128)(2,1)}), bf16[128,8,3,128]{0,3,2,1:T(8,128)(2,1)S(1)}, u32[]{:S(2)}, u32[]{:S(2)}) %all-to-all-start.3) | async-done | bytes 786464 | tf_op jit(solution)/shard_map/all_to_all | solution.py:100
  109.4 4.2 %all-to-all-start.2 = ((bf16[128,8,3,128]{0,3,2,1:T(8,128)(2,1)}), bf16[128,8,3,128]{0,3,2,1:T(8,128)(2,1)}, u32[]{:S(2)}, u32[]{:S(2)}) async-start(bf16[128,8,3,128]{0,3,2,1:T(8,128)(2,1)} %bitcast.127), calls=%async_computation.2 | async-start | bytes 1572864 | tf_op jit(solution)/shard_map/all_to_all | solution.py:97
  113.6 2.3 copy.82
  115.9 16.4 %all-to-all-done.2 = bf16[128,8,3,128]{0,3,2,1:T(8,128)(2,1)} async-done(((bf16[128,8,3,128]{0,3,2,1:T(8,128)(2,1)}), bf16[128,8,3,128]{0,3,2,1:T(8,128)(2,1)}, u32[]{:S(2)}, u32[]{:S(2)}) %all-to-all-start.2) | async-done | bytes 786464 | tf_op jit(solution)/shard_map/all_to_all | solution.py:97
  132.4 4.4 %all-to-all-start.5 = ((bf16[128,8,3,128]{0,3,2,1:T(8,128)(2,1)}), bf16[128,8,3,128]{0,3,2,1:T(8,128)(2,1)}, u32[]{:S(2)}, u32[]{:S(2)}) async-start(bf16[128,8,3,128]{0,3,2,1:T(8,128)(2,1)} %bitcast.126), calls=%async_computation.5 | async-start | bytes 1572864 | tf_op jit(solution)/shard_map/all_to_all | solution.py:106
  140.0 2.4 copy.77
  142.4 12.4 %all-to-all-done.5 = bf16[128,8,3,128]{0,3,2,1:T(8,128)(2,1)} async-done(((bf16[128,8,3,128]{0,3,2,1:T(8,128)(2,1)}), bf16[128,8,3,128]{0,3,2,1:T(8,128)(2,1)}, u32[]{:S(2)}, u32[]{:S(2)}) %all-to-all-start.5) | async-done | bytes 786464 | tf_op jit(solution)/shard_map/all_to_all | solution.py:106
  157.0 31.3 %while.12 = (s32[]{:T(128)}, bf16[2,512,3,128]{3,1,0,2:T(8,128)(2,1)S(1)}, bf16[2,512,3,128]{3,1,0,2:T(8,128)(2,1)S(1)}, bf16[2,512,3,128]{3,1,0,2:T(8,128)(2,1)...) while((s32[]{:T(128)}, ...), condition=%wide.region_8.9_spmd, body=%wide.region_4.8_spmd.sunk | while | flops 2441674240 | bytes 96387864 | solution.py:64
  157.0 5.7 %fusion.115 = (f32[3,512]{1,0:T(4,128)S(1)}, f32[3,512,1024]{2,1,0:T(8,128)}) fusion(bf16[1024,3,128]{2,0,1:T(8,128)(2,1)S(1)} %get-tuple-element.215, bf16[2,512,3,128]{3,1,0,2:T(8,128)(2,1)} %get-tuple-element.214, s32[]{:T(128)} %get-tuple-element.201), kind=kOutput, calls=%fused_computation.77.clone.1 | convolution fusion | flops 407372800 | bytes 7477760 | tf_op jit(solution)/shard_map/while/body/eval_jaxpr/sub | solution.py:35
  164.3 4.2 %multiply_reduce_fusion.3 = (f32[3,512]{1,0:T(4,128)S(1)}, f32[3,512,1024]{2,1,0:T(8,128)S(1)}) fusion(f32[3,512,1024]{2,1,0:T(8,128)} %get-tuple-element.187, f32[3,512]{1,0:T(4,128)S(1)} %get-tuple-element.188, f32[3,512,1024]{2,1,0:T(8,128)S(1)} %fusion.117, bf16[1024,3,128]{2,0,1:T(8,128)(2,1)S(1)} %copy-done.7, ...), kind=kOutput, calls=%fused_computation.2.clone.1 | convolution fusion | flops 410515968 | bytes 20068356 | tf_op jit(solution)/shard_map/while/body/eval_jaxpr/qnd,knd->nqk/dot_general | solution.py:32
  172.7 5.7 %fusion.115 = (f32[3,512]{1,0:T(4,128)S(1)}, f32[3,512,1024]{2,1,0:T(8,128)}) fusion(bf16[1024,3,128]{2,0,1:T(8,128)(2,1)S(1)} %get-tuple-element.215, bf16[2,512,3,128]{3,1,0,2:T(8,128)(2,1)} %get-tuple-element.214, s32[]{:T(128)} %get-tuple-element.201), kind=kOutput, calls=%fused_computation.77.clone.1 | convolution fusion | flops 407372800 | bytes 7477760 | tf_op jit(solution)/shard_map/while/body/eval_jaxpr/sub | solution.py:35
  179.9 4.2 %multiply_reduce_fusion.3 = (f32[3,512]{1,0:T(4,128)S(1)}, f32[3,512,1024]{2,1,0:T(8,128)S(1)}) fusion(f32[3,512,1024]{2,1,0:T(8,128)} %get-tuple-element.187, f32[3,512]{1,0:T(4,128)S(1)} %get-tuple-element.188, f32[3,512,1024]{2,1,0:T(8,128)S(1)} %fusion.117, bf16[1024,3,128]{2,0,1:T(8,128)(2,1)S(1)} %copy-done.7, ...), kind=kOutput, calls=%fused_computation.2.clone.1 | convolution fusion | flops 410515968 | bytes 20068356 | tf_op jit(solution)/shard_map/while/body/eval_jaxpr/qnd,knd->nqk/dot_general | solution.py:32
  190.0 4.3 %all-to-all-start.6 = ((bf16[1024,1,3,128]{3,2,1,0:T(4,128)(2,1)}), bf16[1024,1,3,128]{3,2,1,0:T(4,128)(2,1)S(1)}, u32[]{:S(2)}, u32[]{:S(2)}) async-start(bf16[1024,1,3,128]{3,2,1,0:T(4,128)(2,1)} %copy.87), calls=%async_computation.6 | async-start | bytes 2097152 | tf_op jit(solution)/shard_map/all_to_all | solution.py:112
  195.9 22.0 %all-to-all-done.6 = bf16[1024,1,3,128]{3,2,1,0:T(4,128)(2,1)S(1)} async-done(((bf16[1024,1,3,128]{3,2,1,0:T(4,128)(2,1)}), bf16[1024,1,3,128]{3,2,1,0:T(4,128)(2,1)S(1)}, u32[]{:S(2)}, u32[]{:S(2)}) %all-to-all-start.6) | async-done | bytes 786464 | tf_op jit(solution)/shard_map/all_to_all | solution.py:112
  217.9 4.0 %all-to-all-start.7 = ((bf16[1024,1,3,128]{3,2,1,0:T(4,128)(2,1)}), bf16[1024,1,3,128]{3,2,1,0:T(4,128)(2,1)S(1)}, u32[]{:S(2)}, u32[]{:S(2)}) async-start(bf16[1024,1,3,128]{3,2,1,0:T(4,128)(2,1)} %copy.91), calls=%async_computation.7 | async-start | bytes 2097152 | tf_op jit(solution)/shard_map/all_to_all | solution.py:113
  224.9 16.7 %all-to-all-done.7 = bf16[1024,1,3,128]{3,2,1,0:T(4,128)(2,1)S(1)} async-done(((bf16[1024,1,3,128]{3,2,1,0:T(4,128)(2,1)}), bf16[1024,1,3,128]{3,2,1,0:T(4,128)(2,1)S(1)}, u32[]{:S(2)}, u32[]{:S(2)}) %all-to-all-start.7) | async-done | bytes 786464 | tf_op jit(solution)/shard_map/all_to_all | solution.py:113
  245.7 13.9 %fusion.80 = f32[256,5120]{1,0:T(8,128)S(1)} fusion(bf16[256,3072]{1,0:T(8,128)(2,1)} %bitcast.133, bf16[3072,5120]{0,1:T(8,128)(2,1)} %all-gather.2.cloned.1.call-done), kind=kOutput, calls=%fused_computation.78 | convolution fusion | flops 8053063680 | bytes 38273024 | tf_op jit(solution)/shard_map/dot_general | solution.py:117
  (82 shorter events, 37.8 us)
Async XLA Ops:
  7.2 2.3 copy-start.5
  7.2 238.6 %all-gather.2.cloned.1.call-start = ((), (), s32[]{:S(2)}) async-start(), calls=%async_computation.8 | async-start | bytes 33423360 | tf_op jit(solution)/shard_map/all_gather | solution.py:119
  7.9 2.4 copy-start.11
  10.3 10.2 %copy-start.6 = (bf16[128,3072]{1,0:T(8,128)(2,1)S(1)}, bf16[128,3072]{1,0:T(8,128)(2,1)}, u32[]{:S(2)}) copy-start(bf16[128,3072]{1,0:T(8,128)(2,1)} %param.14) | copy-start | bytes 2359300
  12.2 27.1 %all-to-all-start.1 = ((bf16[128,8,3,128]{0,3,2,1:T(8,128)(2,1)}), bf16[128,8,3,128]{0,3,2,1:T(8,128)(2,1)S(1)}, u32[]{:S(2)}, u32[]{:S(2)}) async-start(bf16[128,8,3,128]{0,3,2,1:T(8,128)(2,1)} %bitcast.12), calls=%async_computation.1 | async-start | bytes 1572864 | tf_op jit(solution)/shard_map/all_to_all | solution.py:96
  20.9 21.9 %copy-start.12 = (f32[3072]{0:T(1024)S(1)}, f32[3072]{0:T(1024)}, u32[]{:S(2)}) copy-start(f32[3072]{0:T(1024)} %param.20) | copy-start | bytes 36868
  39.3 23.3 %all-to-all-start.4 = ((bf16[128,8,3,128]{0,3,2,1:T(8,128)(2,1)}), bf16[128,8,3,128]{0,3,2,1:T(8,128)(2,1)S(1)}, u32[]{:S(2)}, u32[]{:S(2)}) async-start(bf16[128,8,3,128]{0,3,2,1:T(8,128)(2,1)} %bitcast.128), calls=%async_computation.4 | async-start | bytes 1572864 | tf_op jit(solution)/shard_map/all_to_all | solution.py:103
  86.8 22.6 %all-to-all-start.3 = ((bf16[128,8,3,128]{0,3,2,1:T(8,128)(2,1)}), bf16[128,8,3,128]{0,3,2,1:T(8,128)(2,1)S(1)}, u32[]{:S(2)}, u32[]{:S(2)}) async-start(bf16[128,8,3,128]{0,3,2,1:T(8,128)(2,1)} %bitcast.129), calls=%async_computation.3 | async-start | bytes 1572864 | tf_op jit(solution)/shard_map/all_to_all | solution.py:100
  109.4 27.4 %copy-start = (bf16[128,8,3,128]{0,3,2,1:T(8,128)(2,1)}, bf16[128,8,3,128]{0,3,2,1:T(8,128)(2,1)S(1)}, u32[]{:S(2)}) copy-start(bf16[128,8,3,128]{0,3,2,1:T(8,128)(2,1)S(1)} %all-to-all-done.3) | copy-start | bytes 2359300
  109.4 23.0 %all-to-all-start.2 = ((bf16[128,8,3,128]{0,3,2,1:T(8,128)(2,1)}), bf16[128,8,3,128]{0,3,2,1:T(8,128)(2,1)}, u32[]{:S(2)}, u32[]{:S(2)}) async-start(bf16[128,8,3,128]{0,3,2,1:T(8,128)(2,1)} %bitcast.127), calls=%async_computation.2 | async-start | bytes 1572864 | tf_op jit(solution)/shard_map/all_to_all | solution.py:97
  132.4 22.4 %all-to-all-start.5 = ((bf16[128,8,3,128]{0,3,2,1:T(8,128)(2,1)}), bf16[128,8,3,128]{0,3,2,1:T(8,128)(2,1)}, u32[]{:S(2)}, u32[]{:S(2)}) async-start(bf16[128,8,3,128]{0,3,2,1:T(8,128)(2,1)} %bitcast.126), calls=%async_computation.5 | async-start | bytes 1572864 | tf_op jit(solution)/shard_map/all_to_all | solution.py:106
  137.2 2.4 copy-start.1
  139.5 17.5 %copy-start.3 = (bf16[2,512,3,128]{3,1,0,2:T(8,128)(2,1)S(1)}, bf16[2,512,3,128]{3,1,0,2:T(8,128)(2,1)}, u32[]{:S(2)}) copy-start(bf16[2,512,3,128]{3,1,0,2:T(8,128)(2,1)} %custom-call) | copy-start | bytes 2359300
  139.9 17.1 %copy-start.4 = (bf16[2,512,3,128]{3,1,0,2:T(8,128)(2,1)S(1)}, bf16[2,512,3,128]{3,1,0,2:T(8,128)(2,1)}, u32[]{:S(2)}) copy-start(bf16[2,512,3,128]{3,1,0,2:T(8,128)(2,1)} %custom-call.1) | copy-start | bytes 2359300
  162.7 5.8 %slice-start = ((s8[6291456]{0:T(1024)(128)(4,1)}), s8[4194304]{0:T(1024)(128)(4,1)S(1)}, s32[]{:S(2)}) async-start(s8[6291456]{0:T(1024)(128)(4,1)} %bitcast.142), calls=%async_computation.9 | async-start | bytes 8388608 | tf_op jit(solution)/shard_map/while
  164.3 4.3 %copy-start.9 = (bf16[1024,3,128]{2,0,1:T(8,128)(2,1)S(1)}, bf16[1024,3,128]{2,0,1:T(8,128)(2,1)}, u32[]{:S(2)}) copy-start(bf16[1024,3,128]{2,0,1:T(8,128)(2,1)} %get-tuple-element.216) | copy-start | bytes 2359300 | tf_op jit(solution)/shard_map/while
  164.3 4.3 %slice-start.1 = ((s8[6291456]{0:T(1024)(128)(4,1)}), s8[2097152]{0:T(1024)(128)(4,1)S(1)}, s32[]{:S(2)}) async-start(s8[6291456]{0:T(1024)(128)(4,1)} %bitcast.142), calls=%async_computation.10 | async-start | bytes 4194304 | tf_op jit(solution)/shard_map/while
  178.4 5.8 %slice-start = ((s8[6291456]{0:T(1024)(128)(4,1)}), s8[4194304]{0:T(1024)(128)(4,1)S(1)}, s32[]{:S(2)}) async-start(s8[6291456]{0:T(1024)(128)(4,1)} %bitcast.142), calls=%async_computation.9 | async-start | bytes 8388608 | tf_op jit(solution)/shard_map/while
  179.9 4.3 %copy-start.9 = (bf16[1024,3,128]{2,0,1:T(8,128)(2,1)S(1)}, bf16[1024,3,128]{2,0,1:T(8,128)(2,1)}, u32[]{:S(2)}) copy-start(bf16[1024,3,128]{2,0,1:T(8,128)(2,1)} %get-tuple-element.216) | copy-start | bytes 2359300 | tf_op jit(solution)/shard_map/while
  179.9 4.4 %slice-start.1 = ((s8[6291456]{0:T(1024)(128)(4,1)}), s8[2097152]{0:T(1024)(128)(4,1)S(1)}, s32[]{:S(2)}) async-start(s8[6291456]{0:T(1024)(128)(4,1)} %bitcast.142), calls=%async_computation.10 | async-start | bytes 4194304 | tf_op jit(solution)/shard_map/while
  184.3 1.6 copy-start.10
  190.0 28.0 %all-to-all-start.6 = ((bf16[1024,1,3,128]{3,2,1,0:T(4,128)(2,1)}), bf16[1024,1,3,128]{3,2,1,0:T(4,128)(2,1)S(1)}, u32[]{:S(2)}, u32[]{:S(2)}) async-start(bf16[1024,1,3,128]{3,2,1,0:T(4,128)(2,1)} %copy.87), calls=%async_computation.6 | async-start | bytes 2097152 | tf_op jit(solution)/shard_map/all_to_all | solution.py:112
  217.9 23.6 %all-to-all-start.7 = ((bf16[1024,1,3,128]{3,2,1,0:T(4,128)(2,1)}), bf16[1024,1,3,128]{3,2,1,0:T(4,128)(2,1)S(1)}, u32[]{:S(2)}, u32[]{:S(2)}) async-start(bf16[1024,1,3,128]{3,2,1,0:T(4,128)(2,1)} %copy.91), calls=%async_computation.7 | async-start | bytes 2097152 | tf_op jit(solution)/shard_map/all_to_all | solution.py:113
  224.9 18.0 %copy-start.2 = (bf16[128,8,1,3,128]{0,4,3,1,2:T(8,128)(2,1)S(1)}, bf16[128,8,1,3,128]{0,4,3,1,2:T(8,128)(2,1)}, u32[]{:S(2)}) copy-start(bf16[128,8,1,3,128]{0,4,3,1,2:T(8,128)(2,1)} %copy.89) | copy-start | bytes 2359300
  (5 other events, 7.1 us)
Sparse Core Ops, SparseCore 0:
  9.7 227.8 all-gather.1
where the time goes:
time: 273 us; the launch traced here: 269 us
  waiting for transfers between devices  119 us (44%)
  matrix products  43.7 us (16%)
  starting transfers between devices  32.3 us (12%)
  local copies, waits for them, and re-layouts  26.1 us (10%)
  blocking collectives  24.2 us (9%)
  between operations  14.9 us (5%)
  other arithmetic  8.05 us (3%)
    all_to_all x1, blocking collectives, local(): lax.all_to_all(query_hat.reshape(layout), 'seq', split_axis=1, concat_axi...  24.2 us
    all_to_all x1, waiting for transfers between devices, local(): lax.all_to_all(attn, 'seq', split_axis=0, concat_axis=1, tiled=True)  22 us
    all_to_all x1, waiting for transfers between devices, local(): lax.all_to_all(key_hat_dot.reshape(layout), 'seq', split_axis=1, concat_a...  17.9 us
    all_to_all x1, waiting for transfers between devices, local(): lax.all_to_all(attn_dot, 'seq', split_axis=0, concat_axis=1, tiled=True)  16.7 us
    all_to_all x1, waiting for transfers between devices, local(): lax.all_to_all(query_hat_dot.reshape(layout), 'seq', split_axis=1, concat...  16.7 us
    all_to_all x1, waiting for transfers between devices, local(): lax.all_to_all(value_in.reshape(layout), 'seq', split_axis=1, concat_axis...  16.4 us
    all_to_all x1, waiting for transfers between devices, local(): lax.all_to_all(key_hat.reshape(layout), 'seq', split_axis=1, concat_axis=...  16.4 us
    dot_general x1, matrix products, local(): jnp.dot(flat, lax.all_gather(out_weight, 'fsdp', axis=1, tiled=True), pre...  13.9 us
  transfers between devices with their start and end apart: 8, of which 7 were waited for; matrix products, arithmetic and copies ran while one was open for 23% of the time, Pallas kernels for 0%

commit v1 on v0

v1 whole, which is shorter than its diff:
```python
import functools
import math

import jax
import jax.numpy as jnp
from jax import lax
from jax.experimental import pallas as pl
from jax.experimental.pallas import tpu as pltpu
from jax.sharding import PartitionSpec as P

HD = 128
EPS = 1e-06
F32 = jnp.float32
BF16 = jnp.bfloat16
MIB = 1 << 20
VMEM_ALL = 60 * MIB
PIECE = 320
NO_COST = pl.CostEstimate(flops=0, bytes_accessed=0, transcendentals=0)

NY, NXL, NC, NXH, NZ = 4, 2, 2, 2, 4
NX = NXL * NXH


def place(y, x, core, z):
    x_hi, x_lo = divmod(x % NX, NXL)
    return (((y % NY) * NXL + x_lo) * NC + core) * (NXH * NZ) + x_hi * NZ + z


def chips():
    return [(y, x, z) for y in range(NY) for x in range(NX) for z in range(NZ)]


def along_y(step):
    return [(place(y, x, c, z), place(y + step, x, c, z)) for y, x, z in chips() for c in range(NC)]


def core_swap():
    return [(place(y, x, c, z), place(y, x, 1 - c, z)) for y, x, z in chips() for c in range(NC)]


def beside():
    return [(place(y, x, c, z), place(y, x + 1 - 2 * c, c, z)) for y, x, z in chips() for c in range(NC)]


def move(a, perm):
    return lax.ppermute(a, ("fsdp", "seq"), perm)


def norm_body(q_ref, qd_ref, k_ref, kd_ref, v_ref, vd_ref, gq_ref, gk_ref, *out_refs):
    def normed(raw_ref, dot_ref, gain_ref):
        signal = raw_ref[...].astype(F32)
        signal_dot = dot_ref[...].astype(F32)
        gain = gain_ref[...]
        inverse = lax.rsqrt(jnp.mean(signal * signal, axis=-1, keepdims=True) + EPS)
        inner = jnp.mean(signal * signal_dot, axis=-1, keepdims=True)
        hat = gain * signal * inverse
        hat_dot = gain * (signal_dot * inverse - signal * (inverse * inverse * inverse * inner))
        return hat.astype(BF16), hat_dot.astype(BF16)

    groups = out_refs[0].shape[0]
    counts = [ref.shape[2] // (6 * HD) for ref in out_refs]
    heads = sum(counts)
    target = [(ref, j) for ref, count in zip(out_refs, counts) for j in range(count)]
    q, qd = normed(q_ref, qd_ref, gq_ref)
    k, kd = normed(k_ref, kd_ref, gk_ref)
    pieces = (qd, q, k, kd, v_ref[...], vd_ref[...])
    for g in range(groups):
        for h in range(heads):
            src = (g * heads + h) * HD
            ref, j = target[h]
            for i, piece in enumerate(pieces):
                dst = (6 * j + i) * HD
                ref[g, :, dst : dst + HD] = piece[:, src : src + HD]


def norm_pack(q, qd, k, kd, v, vd, gq, gk, groups, counts):
    tokens, width = q.shape
    rows = 64
    wide = pl.BlockSpec((rows, width), lambda i: (i, 0))
    gain = pl.BlockSpec((1, width), lambda i: (0, 0))
    return pl.pallas_call(
        norm_body,
        grid=(tokens // rows,),
        in_specs=[wide] * 6 + [gain] * 2,
        out_specs=[pl.BlockSpec((groups, rows, n * 6 * HD), lambda i: (0, i, 0)) for n in counts],
        out_shape=[jax.ShapeDtypeStruct((groups, tokens, n * 6 * HD), BF16) for n in counts],
        compiler_params=pltpu.CompilerParams(vmem_limit_bytes=VMEM_ALL),
        cost_estimate=NO_COST,
        name="norm_pack",
    )(q, qd, k, kd, v, vd, gq.reshape(1, width), gk.reshape(1, width))


NT = (((1,), (1,)), ((), ()))
NN = (((1,), (0,)), ((), ()))


def attn_body(in_ref, *refs):
    out_ref = refs[-1]
    groups, tokens, _ = in_ref.shape
    length = groups * tokens
    blocks = 4
    rows = blocks * tokens
    scale = HD**-0.5

    def columns(first, count):
        return in_ref[:, :, first * HD : (first + count) * HD].reshape(length, count * HD)

    k, kk = columns(2, 1), columns(2, 2)
    v, vv = columns(4, 1), columns(4, 2)
    for b in range(0, groups, blocks):
        both = in_ref[b : b + blocks, :, 0 : 2 * HD].reshape(rows, 2 * HD)
        q = in_ref[b : b + blocks, :, HD : 2 * HD].reshape(rows, HD)
        s = lax.dot_general(q, k, NT, preferred_element_type=F32)
        sd = lax.dot_general(both, kk, NT, preferred_element_type=F32)
        peak = jnp.max(s, axis=-1, keepdims=True)
        w = jnp.exp2((s - peak) * (scale * math.log2(math.e)))
        inv = 1.0 / jnp.sum(w, axis=-1, keepdims=True)
        mean = jnp.sum(w * sd, axis=-1, keepdims=True) * inv
        w_dot = (w * (sd - mean)).astype(BF16)
        first = lax.dot_general(w.astype(BF16), vv, NN, preferred_element_type=F32)
        second = lax.dot_general(w_dot, v, NN, preferred_element_type=F32)
        attn = (first[:, :HD] * inv).astype(BF16)
        attn_dot = ((second * scale + first[:, HD:]) * inv).astype(BF16)
        out_ref[b : b + blocks, :, 0:HD] = attn.reshape(blocks, tokens, HD)
        out_ref[b : b + blocks, :, HD : 2 * HD] = attn_dot.reshape(blocks, tokens, HD)


def attend(packed, first, heads, earlier=None):
    groups, tokens, width = packed.shape
    return pl.pallas_call(
        attn_body,
        grid=(width // (6 * HD),),
        in_specs=[pl.BlockSpec((groups, tokens, 6 * HD), lambda h: (0, 0, h))]
        + ([] if earlier is None else [pl.BlockSpec(memory_space=pl.ANY)]),
        out_specs=pl.BlockSpec((groups, tokens, 2 * HD), lambda h: (0, 0, first + h)),
        out_shape=jax.ShapeDtypeStruct((groups, tokens, heads * 2 * HD), BF16),
        input_output_aliases={} if earlier is None else {1: 0},
        compiler_params=pltpu.CompilerParams(vmem_limit_bytes=VMEM_ALL),
        cost_estimate=NO_COST,
        name="attend",
    )(packed, *(() if earlier is None else (earlier,)))


def gates_body(info_ref, gate_hbm, gate_dot_hbm, out_ref, wide, sem):
    copies = []
    for who in range(2):
        row = pl.multiple_of(info_ref[who] // 8 * 8, 8)
        for t, table in enumerate((gate_hbm, gate_dot_hbm)):
            copies.append(pltpu.make_async_copy(table.at[pl.ds(row, 8), :], wide.at[who, t], sem.at[who, t]))
    for c in copies:
        c.start()
    for c in copies:
        c.wait()
    for who in range(2):
        for t in range(2):
            out_ref[2 * who + t : 2 * who + t + 1] = wide[who, t, pl.ds(info_ref[who] % 8, 1), :]


def pick_gates(times, gate_table, gate_dot_table):
    width = gate_table.shape[1]
    hbm = pl.BlockSpec(memory_space=pltpu.HBM)
    return pl.pallas_call(
        gates_body,
        in_specs=[pl.BlockSpec(memory_space=pltpu.SMEM), hbm, hbm],
        out_specs=pl.BlockSpec(memory_space=pltpu.VMEM),
        out_shape=jax.ShapeDtypeStruct((4, width), F32),
        scratch_shapes=[pltpu.VMEM((2, 2, 8, width), F32), pltpu.SemaphoreType.DMA((2, 2))],
        compiler_params=pltpu.CompilerParams(vmem_limit_bytes=VMEM_ALL),
        cost_estimate=NO_COST,
        name="pick_gates",
    )(times, gate_table, gate_dot_table)


def gates_body(info_ref, gate_hbm, gate_dot_hbm, out_ref, wide, sem):
    copies = []
    for who in range(2):
        row = pl.multiple_of(info_ref[who] // 8 * 8, 8)
        for t, table in enumerate((gate_hbm, gate_dot_hbm)):
            copies.append(pltpu.make_async_copy(table.at[pl.ds(row, 8), :], wide.at[who, t], sem.at[who, t]))
    for c in copies:
        c.start()
    for c in copies:
        c.wait()
    for who in range(2):
        for t in range(2):
            out_ref[2 * who + t : 2 * who + t + 1] = wide[who, t, pl.ds(info_ref[who] % 8, 1), :]


def pick_gates(times, gate_table, gate_dot_table):
    width = gate_table.shape[1]
    hbm = pl.BlockSpec(memory_space=pltpu.HBM)
    return pl.pallas_call(
        gates_body,
        in_specs=[pl.BlockSpec(memory_space=pltpu.SMEM), hbm, hbm],
        out_specs=pl.BlockSpec(memory_space=pltpu.VMEM),
        out_shape=jax.ShapeDtypeStruct((4, width), F32),
        scratch_shapes=[pltpu.VMEM((2, 2, 8, width), F32), pltpu.SemaphoreType.DMA((2, 2))],
        compiler_params=pltpu.CompilerParams(vmem_limit_bytes=VMEM_ALL),
        cost_estimate=NO_COST,
        name="pick_gates",
    )(times, gate_table, gate_dot_table)


def round_up(n, unit):
    return -(-n // unit) * unit


def project_body(n, first, info_ref, gates_ref, own_ref, peer_ref, *rest):
    weights = rest[:n]
    mine_ref, send_ref = rest[n : n + 2]
    x, w, w_sem = rest[n + 2 :]
    groups, tokens, _ = own_ref.shape
    heads = own_ref.shape[2] // (2 * HD)

    at, ends, w_copies = 0, [], []
    for i, weight in enumerate(weights):
        rows = weight.shape[0]
        w_copies.append(pltpu.make_async_copy(weight, w.at[pl.ds(at, rows), :], w_sem.at[i]))
        at += rows
        ends.append(at)
    for c in w_copies:
        c.start()

    pieces = ends[-1] // PIECE

    def gate_rows(line):
        parts = []
        for i in range(pieces):
            column = info_ref[first + i] * PIECE
            base = pl.multiple_of(column // HD * HD, HD)
            wide = gates_ref[line : line + 1, pl.ds(base, 3 * HD)]
            parts.append(jnp.where(column % HD != 0, wide[:, HD // 2 : HD // 2 + PIECE], wide[:, :PIECE]))
        return jnp.concatenate(parts, axis=1)

    lines = [gate_rows(line) for line in range(4)]
    for who, ref in enumerate((own_ref, peer_ref)):
        for g in range(groups):
            for h in range(heads):
                at = (g * heads + h) * HD
                for t in range(2):
                    row = (2 * who + t) * tokens
                    src = (2 * h + t) * HD
                    x[row : row + tokens, at : at + HD] = ref[g, :, src : src + HD]
    for c in w_copies:
        c.wait()
    y = lax.dot_general(x[...], w[...], NT, preferred_element_type=F32)
    for who, ref in enumerate((mine_ref, send_ref)):
        gate, gate_dot = lines[2 * who], lines[2 * who + 1]
        primal = y[2 * who * tokens : (2 * who + 1) * tokens]
        tangent = y[(2 * who + 1) * tokens : (2 * who + 2) * tokens]
        ref[0] = (gate * primal).astype(BF16)
        ref[1] = (gate_dot * primal + gate * tangent).astype(BF16)


def project(info, first, own, peer, gates, weights):
    groups, tokens, _ = own.shape
    n = len(weights)
    total = sum(a.shape[0] for a in weights)
    depth = weights[0].shape[1]
    hbm = pl.BlockSpec(memory_space=pltpu.HBM)
    vmem = pl.BlockSpec(memory_space=pltpu.VMEM)
    half = jax.ShapeDtypeStruct((2, tokens, total), BF16)
    return pl.pallas_call(
        functools.partial(project_body, n, first),
        in_specs=[pl.BlockSpec(memory_space=pltpu.SMEM)] + [vmem] * 3 + [hbm] * n,
        out_specs=[vmem, vmem],
        out_shape=[half, half],
        scratch_shapes=[
            pltpu.VMEM((4 * tokens, depth), BF16),
            pltpu.VMEM((total, depth), BF16),
            pltpu.SemaphoreType.DMA((n,)),
        ],
        compiler_params=pltpu.CompilerParams(vmem_limit_bytes=36 * MIB),
        cost_estimate=NO_COST,
        name="project",
    )(info, gates, own, peer, *weights)


def merge_body(spots, info_ref, *refs):
    parts = (len(refs) - 2) // 2
    out_refs = refs[2 * parts :]
    first = info_ref[8] == 0
    for i, (part, at) in enumerate(spots):
        own_ref, got_ref = refs[part], refs[parts + part]
        cols = 2 * PIECE
        column = pl.multiple_of(info_ref[9 + i] * cols, cols)
        here = slice(at * PIECE, (at + 1) * PIECE)
        for t in range(2):
            own, got = own_ref[t, :, here], got_ref[t, :, here]
            low = jnp.where(first, own, got)
            high = jnp.where(first, got, own)
            out_refs[t][:, pl.ds(column, cols)] = jnp.concatenate([low, high], axis=1)


def merge(info, spots, owns, gots, width):
    tokens = owns[0].shape[1]
    vmem = pl.BlockSpec(memory_space=pltpu.VMEM)
    out = jax.ShapeDtypeStruct((tokens, width), BF16)
    return pl.pallas_call(
        functools.partial(merge_body, spots),
        in_specs=[pl.BlockSpec(memory_space=pltpu.SMEM)] + [vmem] * (2 * len(owns)),
        out_specs=[vmem, vmem],
        out_shape=[out, out],
        compiler_params=pltpu.CompilerParams(vmem_limit_bytes=12 * MIB),
        cost_estimate=NO_COST,
        name="merge",
    )(info, *owns, *gots)


def local(
    query_raw,
    key_raw,
    value_in,
    query_dot,
    key_dot,
    value_dot,
    gain_query,
    gain_key,
    out_weight,
    gate_table,
    gate_dot_table,
    time_index,
):
    groups = lax.axis_size("seq")
    fsdp = lax.axis_index("fsdp")
    core = fsdp % NC
    x_lo = fsdp // NC % NXL
    y = fsdp // (NC * NXL)
    up, down, swap = along_y(1), along_y(-1), core_swap()

    def exchange(a):
        return lax.all_to_all(a, "seq", split_axis=0, concat_axis=0, tiled=True)

    other = 1 - x_lo
    steps = (0, -1, 1, 2)
    block = [(y + step) % NY * NXL + low for low in (x_lo, other) for step in steps]
    source = [index * NC + core for index in block]
    info = jnp.stack([jnp.asarray(v, jnp.int32) for v in (*source, core, *block)])

    weight = out_weight.T
    half = PIECE // 2
    near = move(weight, beside())
    w1 = weight[:half]
    a1 = move(w1, up)
    b1 = move(w1, down)
    peer_time = move(time_index, swap)
    (packed,) = norm_pack(
        query_raw, query_dot, key_raw, key_dot, value_in, value_dot, gain_query, gain_key, groups, (3,)
    )
    times = jnp.concatenate([time_index, peer_time])
    packed, weight, near, a1, b1, times, info = lax.optimization_barrier(
        (packed, weight, near, a1, b1, times, info)
    )

    received = exchange(packed)
    w2 = weight[half:]
    a2 = move(w2, up)
    b2 = move(w2, down)
    c1 = move(a1, up)
    c2 = move(b2, down)
    near_a = move(near, up)
    near_b = move(near, down)
    received, a2, b2, c1, c2 = lax.optimization_barrier((received, a2, b2, c1, c2))

    attn = attend(received, 0, 3)
    own = exchange(attn)
    gates = pick_gates(times, gate_table, gate_dot_table)
    own, near_a, near_b, gates, c2 = lax.optimization_barrier((own, near_a, near_b, gates, c2))

    peer = move(own, swap)
    near_c1 = move(near_a[: half // 2], up)
    near_c2 = move(near_b[half // 2 : half], down)
    near_c3 = move(c2, beside())

    mine_a, sent_a = project(info, 0, own, peer, gates, (weight, a1, a2, b1, b2, c1, c2))
    got_a = move(sent_a, swap)
    mine_b, sent_b = project(info, 4, own, peer, gates, (near, near_a, near_b, near_c1, near_c2, near_c3))
    got_b = move(sent_b, swap)
    spots = [(part, i) for part in range(2) for i in range(4)]
    return tuple(merge(info, spots, (mine_a, mine_b), (got_a, got_b), gate_table.shape[1]))


def solution(mesh):
    return jax.shard_map(
        local,
        mesh=mesh,
        in_specs=(
            P(("fsdp", "seq"), None),
            P(("fsdp", "seq"), None),
            P(("fsdp", "seq"), None),
            P(("fsdp", "seq"), None),
            P(("fsdp", "seq"), None),
            P(("fsdp", "seq"), None),
            P(),
            P(),
            P(None, "fsdp"),
            P(),
            P(),
            P("fsdp"),
        ),
        out_specs=(P(("fsdp", "seq"), None), P(("fsdp", "seq"), None)),
        check_vma=False,
    )
```

time: 273 us -> 160 us (0.59); the launches traced: 269 us -> 160 us
  matrix products: 43.7 us -> 0 us
  waiting for transfers between devices: 119 us -> 77.3 us
  Pallas kernels: 0 us -> 37.6 us
  blocking collectives: 24.2 us -> 0 us
  local copies, waits for them, and re-layouts: 26.1 us -> 10.7 us
  between operations: 14.9 us -> 1.55 us
  other arithmetic: 8.05 us -> 1.21 us
    all_to_all x7 -> x2, waiting for transfers between devices: 118 us -> 9.69 us  [exchange(): return lax.all_to_all(a, 'seq', split_axis=0, concat_axis=0, tiled=True)]
    ppermute x0 -> x16, waiting for transfers between devices: none -> 67.6 us  [move(): return lax.ppermute(a, ('fsdp', 'seq'), perm)]
    pallas_call x0 -> x6, Pallas kernels: none -> 37.6 us  [the longest x2 15.3 us: project(): pl.pallas_call(functools.partial(project_body, n, first), in_specs=[pl.Bl...]
    dot_general x11 -> x0, matrix products: 32.4 us -> none  [the longest x1 13.9 us: local(): jnp.dot(flat, lax.all_gather(out_weight, 'fsdp', axis=1, tiled=True), pre...]
    all_to_all x1 -> x0, blocking collectives: 24.2 us -> none  [local(): lax.all_to_all(query_hat.reshape(layout), 'seq', split_axis=1, concat_axi...]
    all_to_all x7 -> x2, starting transfers between devices: 32.3 us -> 9.48 us  [exchange(): return lax.all_to_all(a, 'seq', split_axis=0, concat_axis=0, tiled=True)]
    ppermute x0 -> x16, starting transfers between devices: none -> 21.7 us  [move(): return lax.ppermute(a, ('fsdp', 'seq'), perm)]
    sub x2 -> x0, matrix products: 11.4 us -> none  [block_step(): weights = jnp.exp(scores - row_peak)]
  transfers between devices with their start and end apart: 8 -> 18, of which waited for: 7 -> 7; matrix products, arithmetic and copies ran while one was open for 23% -> 4% of each run, Pallas kernels for 0% -> 22%
where the time goes in v1:
time: 160 us
  waiting for transfers between devices  77.3 us (48%)
  Pallas kernels  37.6 us (24%)
  starting transfers between devices  31.2 us (20%)
  local copies, waits for them, and re-layouts  10.7 us (7%)
    ppermute x16, waiting for transfers between devices, move(): return lax.ppermute(a, ('fsdp', 'seq'), perm)  67.6 us
    ppermute x16, starting transfers between devices, move(): return lax.ppermute(a, ('fsdp', 'seq'), perm)  21.7 us
    pallas_call x2, Pallas kernels, project(): pl.pallas_call(functools.partial(project_body, n, first), in_specs=[pl.Bl...  15.3 us
    pallas_call x1, Pallas kernels, attend(): pl.pallas_call(attn_body, grid=(width // (6 * HD),), in_specs=[pl.BlockSp...  11.4 us
    all_to_all x2, waiting for transfers between devices, exchange(): return lax.all_to_all(a, 'seq', split_axis=0, concat_axis=0, tiled=True)  9.69 us
    all_to_all x2, starting transfers between devices, exchange(): return lax.all_to_all(a, 'seq', split_axis=0, concat_axis=0, tiled=True)  9.48 us
    unnamed x20, local copies, waits for them, and re-layouts  6.19 us
    pallas_call x1, Pallas kernels, norm_pack(): pl.pallas_call(norm_body, grid=(tokens // rows,), in_specs=[wide] * 6 + [...  5.84 us
  transfers between devices with their start and end apart: 18, of which 7 were waited for; matrix products, arithmetic and copies ran while one was open for 4% of the time, Pallas kernels for 22%

profile of v1, /device:TPU:1, one launch (start us, length us, event | category | flops | bytes accessed | tf_op | source)
XLA Modules:
  0.0 159.5 jit_solution(18044440023313004049)
XLA Ops:
  0.6 3.4 %collective-permute-start = (bf16[320,3072]{1,0:T(8,128)(2,1)}, bf16[320,3072]{1,0:T(8,128)(2,1)}, u32[]{:S(2)}, u32[]{:S(2)}) collective-permute-start(bf16[320,3072]{1,0:T(8,128)(2,1)} %bitcast.20), channel_id=1, source_target_pairs={{0,16},{8,28},{1,17},{9,29},{2,18},{10,30},{3,19},{11,31},{16,4},{... | collective-permute-start | bytes 5898248 | tf_op jit(solution)/shard_map/ppermute | solution.py:46
  4.0 2.2 %slice.16 = bf16[160,3072]{1,0:T(8,128)(2,1)} slice(bf16[320,3072]{1,0:T(8,128)(2,1)} %bitcast.21), slice={[0:160], [0:3072]} | slice | bytes 1966080 | tf_op jit(solution)/shard_map/slice | solution.py:343
  6.2 1.3 collective-permute-start.1
  7.5 1.4 collective-permute-start.2
  10.0 5.8 %norm_pack.1 = bf16[8,128,2304]{2,1,0:T(8,128)(2,1)} custom-call(bf16[128,3072]{1,0:T(8,128)(2,1)} %q_ref.1, bf16[128,3072]{1,0:T(8,128)(2,1)} %qd_ref.1, bf16[128,3072]{1,0:T(8,128)(2,1)} %k_ref.1, bf16[128,3072]{1,0:T(8,128)(2,1)} %kd_ref.1, bf16[128,3072]{1,0:T(8,128)(2,1)} %v_ref.1, bf16[128,3072]{1,0:T(8,128)(2,1)} %vd_ref.1, f32[1,3072]{1,0:T(1,128)} %bitcast.24, ...), custom_call_target="tpu_custom_call" | custom-call | tf_op jit(solution)/shard_map/norm_pack/pallas_call | solution.py:81
  17.1 14.3 %collective-permute-done.1.rest_1_ = bf16[160,3072]{1,0:T(8,128)(2,1)S(1)} collective-permute-done((bf16[160,3072]{1,0:T(8,128)(2,1)}, bf16[160,3072]{1,0:T(8,128)(2,1)S(1)}, u32[]{:S(2)}, u32[]{:S(2)}) %collective-permute-start.1) | collective-permute-done | bytes 983072 | tf_op jit(solution)/shard_map/ppermute | solution.py:46
  31.4 5.0 %all-to-all-start = ((bf16[8,128,2304]{2,1,0:T(8,128)(2,1)}), bf16[8,128,2304]{2,1,0:T(8,128)(2,1)}, u32[]{:S(2)}, u32[]{:S(2)}) async-start(bf16[8,128,2304]{2,1,0:T(8,128)(2,1)} %norm_pack.1), calls=%async_computation | async-start | bytes 9437184 | tf_op jit(solution)/shard_map/all_to_all | solution.py:332
  36.5 2.6 %collective-permute-start.5 = (bf16[160,3072]{1,0:T(8,128)(2,1)S(1)}, bf16[160,3072]{1,0:T(8,128)(2,1)S(1)}, u32[]{:S(2)}, u32[]{:S(2)}) collective-permute-start(bf16[160,3072]{1,0:T(8,128)(2,1)S(1)} %slice.13), channel_id=1, source_target_pairs={{0,96},{8,104},{1,97},{9,105},{2,98},{10,106},{3,99},{11,107},{16,... | collective-permute-start | bytes 2949128 | tf_op jit(solution)/shard_map/ppermute | solution.py:46
  39.2 19.8 %collective-permute-done.5.rest_4_ = bf16[160,3072]{1,0:T(8,128)(2,1)S(1)} collective-permute-done((bf16[160,3072]{1,0:T(8,128)(2,1)S(1)}, bf16[160,3072]{1,0:T(8,128)(2,1)S(1)}, u32[]{:S(2)}, u32[]{:S(2)}) %collective-permute-start.5) | collective-permute-done | bytes 983072 | tf_op jit(solution)/shard_map/ppermute | solution.py:46
  59.1 3.5 %collective-permute-start.7 = (bf16[160,3072]{1,0:T(8,128)(2,1)S(1)}, bf16[160,3072]{1,0:T(8,128)(2,1)}, u32[]{:S(2)}, u32[]{:S(2)}) collective-permute-start(bf16[160,3072]{1,0:T(8,128)(2,1)S(1)} %collective-permute-done.5.rest_4_), channel_id=1, source_target_pairs={{0,96},{8,104},{1,97},{9,105},{2,98},{10,106},{3,99},{11,107},{16,... | collective-permute-start | bytes 2949128 | tf_op jit(solution)/shard_map/ppermute | solution.py:46
  63.6 2.7 %collective-permute-start.9 = (bf16[320,3072]{1,0:T(8,128)(2,1)}, bf16[320,3072]{1,0:T(8,128)(2,1)}, u32[]{:S(2)}, u32[]{:S(2)}) collective-permute-start(bf16[320,3072]{1,0:T(8,128)(2,1)} %collective-permute-done.rest_0_), channel_id=1, source_target_pairs={{0,96},{8,104},{1,97},{9,105},{2,98},{10,106},{3,99},{11,107},{16,... | collective-permute-start | bytes 5898248 | tf_op jit(solution)/shard_map/ppermute | solution.py:46
  67.2 16.2 %collective-permute-done.6.rest_5_ = bf16[160,3072]{1,0:T(8,128)(2,1)S(1)} collective-permute-done((bf16[160,3072]{1,0:T(8,128)(2,1)S(1)}, bf16[160,3072]{1,0:T(8,128)(2,1)S(1)}, u32[]{:S(2)}, u32[]{:S(2)}) %collective-permute-start.6) | collective-permute-done | bytes 983072 | tf_op jit(solution)/shard_map/ppermute | solution.py:46
  84.3 7.3 %all-to-all-done.in_ref = bf16[8,128,2304]{2,1,0:T(8,128)(2,1)} async-done(((bf16[8,128,2304]{2,1,0:T(8,128)(2,1)}), bf16[8,128,2304]{2,1,0:T(8,128)(2,1)}, u32[]{:S(2)}, u32[]{:S(2)}) %all-to-all-start) | async-done | bytes 4718624 | tf_op jit(solution)/shard_map/all_to_all | solution.py:332
  91.6 11.4 %attend.1 = bf16[8,128,768]{2,1,0:T(8,128)(2,1)} custom-call(bf16[8,128,2304]{2,1,0:T(8,128)(2,1)} %all-to-all-done.in_ref), custom_call_target="tpu_custom_call" | custom-call | tf_op jit(solution)/shard_map/attend/pallas_call | solution.py:130
  102.9 4.4 %all-to-all-start.1 = ((bf16[8,128,768]{2,1,0:T(8,128)(2,1)}), bf16[8,128,768]{2,1,0:T(8,128)(2,1)S(1)}, u32[]{:S(2)}, u32[]{:S(2)}) async-start(bf16[8,128,768]{2,1,0:T(8,128)(2,1)} %attend.1), calls=%async_computation.1 | async-start | bytes 3145728 | tf_op jit(solution)/shard_map/all_to_all | solution.py:332
  107.4 2.5 %pick_gates.1.gates_ref = f32[4,5120]{1,0:T(4,128)} custom-call(s32[2]{0:T(128)} %pad_add_fusion.info_ref, f32[64,5120]{1,0:T(8,128)} %gate_hbm.1, f32[64,5120]{1,0:T(8,128)} %gate_dot_hbm.1), custom_call_target="tpu_custom_call" | custom-call | tf_op jit(solution)/shard_map/pick_gates/pallas_call | solution.py:192
  109.9 15.6 %collective-permute-done.8.rest_1_ = bf16[320,3072]{1,0:T(8,128)(2,1)} collective-permute-done((bf16[320,3072]{1,0:T(8,128)(2,1)}, bf16[320,3072]{1,0:T(8,128)(2,1)}, u32[]{:S(2)}, u32[]{:S(2)}) %collective-permute-start.8) | collective-permute-done | bytes 1966112 | tf_op jit(solution)/shard_map/ppermute | solution.py:46
  125.5 2.4 %all-to-all-done.1.own_ref = bf16[8,128,768]{2,1,0:T(8,128)(2,1)S(1)} async-done(((bf16[8,128,768]{2,1,0:T(8,128)(2,1)}), bf16[8,128,768]{2,1,0:T(8,128)(2,1)S(1)}, u32[]{:S(2)}, u32[]{:S(2)}) %all-to-all-start.1) | async-done | bytes 1572896 | tf_op jit(solution)/shard_map/all_to_all | solution.py:332
  129.1 1.7 %collective-permute-start.13 = (bf16[160,3072]{1,0:T(8,128)(2,1)}, bf16[160,3072]{1,0:T(8,128)(2,1)S(1)}, u32[]{:S(2)}, u32[]{:S(2)}) collective-permute-start(bf16[160,3072]{1,0:T(8,128)(2,1)} %collective-permute-done.7.rest_6_), channel_id=1, source_target_pairs={{0,16},{8,28},{1,17},{9,29},{2,18},{10,30},{3,19},{11,31},{16,4},{... | collective-permute-start | bytes 2949128 | tf_op jit(solution)/shard_map/ppermute | solution.py:46
  134.0 1.9 %collective-permute-start.12 = (bf16[80,3072]{1,0:T(8,128)(2,1)S(1)}, bf16[80,3072]{1,0:T(8,128)(2,1)S(1)}, u32[]{:S(2)}, u32[]{:S(2)}) collective-permute-start(bf16[80,3072]{1,0:T(8,128)(2,1)S(1)} %slice.15), channel_id=1, source_target_pairs={{0,96},{8,104},{1,97},{9,105},{2,98},{10,106},{3,99},{11,107},{16,... | collective-permute-start | bytes 1474568 | tf_op jit(solution)/shard_map/ppermute | solution.py:46
  139.2 7.7 %project.2 = (bf16[2,128,1280]{2,1,0:T(8,128)(2,1)S(1)}, bf16[2,128,1280]{2,1,0:T(8,128)(2,1)S(1)}) custom-call(s32[17]{0:T(128)S(1)} %stack.71.info_ref, f32[4,5120]{1,0:T(4,128)S(1)} %copy-done.9, bf16[8,128,768]{2,1,0:T(8,128)(2,1)S(1)} %all-to-all-done.1.own_ref, bf16[8,128,768]{2,1,0:T(8,128)(2,1)S(1)} %collective-permute-done.10.peer_ref, ...), custom_call_target="tpu_custom_call" | custom-call | tf_op jit(solution)/shard_map/project/pallas_call | solution.py:263
  147.1 7.6 %project.3 = (bf16[2,128,1280]{2,1,0:T(8,128)(2,1)S(1)}, bf16[2,128,1280]{2,1,0:T(8,128)(2,1)S(1)}) custom-call(s32[17]{0:T(128)S(1)} %stack.71.info_ref, f32[4,5120]{1,0:T(4,128)S(1)} %copy-done.9, bf16[8,128,768]{2,1,0:T(8,128)(2,1)S(1)} %all-to-all-done.1.own_ref, bf16[8,128,768]{2,1,0:T(8,128)(2,1)S(1)} %collective-permute-done.10.peer_ref, ...), custom_call_target="tpu_custom_call" | custom-call | tf_op jit(solution)/shard_map/project/pallas_call | solution.py:263
  155.2 1.7 %collective-permute-done.15.refs_3_ = bf16[2,128,1280]{2,1,0:T(8,128)(2,1)S(1)} collective-permute-done((bf16[2,128,1280]{2,1,0:T(8,128)(2,1)S(1)}, bf16[2,128,1280]{2,1,0:T(8,128)(2,1)S(1)}, u32[]{:S(2)}, u32[]{:S(2)}) %collective-permute-start.15) | collective-permute-done | bytes 655392 | tf_op jit(solution)/shard_map/ppermute | solution.py:46
  157.0 2.6 %merge.1 = (bf16[128,5120]{1,0:T(8,128)(2,1)}, bf16[128,5120]{1,0:T(8,128)(2,1)}) custom-call(s32[17]{0:T(128)S(1)} %stack.71.info_ref, bf16[2,128,1280]{2,1,0:T(8,128)(2,1)S(1)} %get-tuple-element.38.refs_0_, bf16[2,128,1280]{2,1,0:T(8,128)(2,1)S(1)} %get-tuple-element.41.refs_1_, bf16[2,128,1280]{2,1,0:T(8,128)(2,1)S(1)} %collective-permute-done.14.refs_2_, ...), custom_call_target="tpu_custom_call" | custom-call | tf_op jit(solution)/shard_map/merge/pallas_call | solution.py:299
  (44 shorter events, 12.9 us)
Async XLA Ops:
  0.6 30.8 %collective-permute-start = (bf16[320,3072]{1,0:T(8,128)(2,1)}, bf16[320,3072]{1,0:T(8,128)(2,1)}, u32[]{:S(2)}, u32[]{:S(2)}) collective-permute-start(bf16[320,3072]{1,0:T(8,128)(2,1)} %bitcast.20), channel_id=1, source_target_pairs={{0,16},{8,28},{1,17},{9,29},{2,18},{10,30},{3,19},{11,31},{16,4},{... | collective-permute-start | bytes 5898248 | tf_op jit(solution)/shard_map/ppermute | solution.py:46
  6.2 25.2 %collective-permute-start.1 = (bf16[160,3072]{1,0:T(8,128)(2,1)}, bf16[160,3072]{1,0:T(8,128)(2,1)S(1)}, u32[]{:S(2)}, u32[]{:S(2)}) collective-permute-start(bf16[160,3072]{1,0:T(8,128)(2,1)} %slice.16), channel_id=1, source_target_pairs={{0,32},{8,40},{1,33},{9,41},{2,34},{10,42},{3,35},{11,43},{16,48},... | collective-permute-start | bytes 2949128 | tf_op jit(solution)/shard_map/ppermute | solution.py:46
  7.5 23.9 %collective-permute-start.2 = (bf16[160,3072]{1,0:T(8,128)(2,1)}, bf16[160,3072]{1,0:T(8,128)(2,1)}, u32[]{:S(2)}, u32[]{:S(2)}) collective-permute-start(bf16[160,3072]{1,0:T(8,128)(2,1)} %slice.16), channel_id=1, source_target_pairs={{0,96},{8,104},{1,97},{9,105},{2,98},{10,106},{3,99},{11,107},{16,... | collective-permute-start | bytes 2949128 | tf_op jit(solution)/shard_map/ppermute | solution.py:46
  9.0 6.9 %collective-permute-start.3 = (s32[1]{0:T(128)}, s32[1]{0:T(128)}, u32[]{:S(2)}, u32[]{:S(2)}) collective-permute-start(s32[1]{0:T(128)} %param.23), channel_id=1, source_target_pairs={{0,8},{8,0},{1,9},{9,1},{2,10},{10,2},{3,11},{11,3},{16,24},{24,16... | collective-permute-start | bytes 20 | tf_op jit(solution)/shard_map/ppermute | solution.py:46
  17.1 19.3 %copy-start = (bf16[3072,320]{0,1:T(8,128)(2,1)S(1)}, bf16[3072,320]{0,1:T(8,128)(2,1)}, u32[]{:S(2)}) copy-start(bf16[3072,320]{0,1:T(8,128)(2,1)} %param.20) | copy-start | bytes 5898244
  31.4 7.8 %copy-start.1 = (bf16[160,3072]{1,0:T(8,128)(2,1)}, bf16[160,3072]{1,0:T(8,128)(2,1)S(1)}, u32[]{:S(2)}) copy-start(bf16[160,3072]{1,0:T(8,128)(2,1)S(1)} %collective-permute-done.1.rest_1_) | copy-start | bytes 2949124
  31.4 60.1 %all-to-all-start = ((bf16[8,128,2304]{2,1,0:T(8,128)(2,1)}), bf16[8,128,2304]{2,1,0:T(8,128)(2,1)}, u32[]{:S(2)}, u32[]{:S(2)}) async-start(bf16[8,128,2304]{2,1,0:T(8,128)(2,1)} %norm_pack.1), calls=%async_computation | async-start | bytes 9437184 | tf_op jit(solution)/shard_map/all_to_all | solution.py:332
  36.5 22.5 %collective-permute-start.5 = (bf16[160,3072]{1,0:T(8,128)(2,1)S(1)}, bf16[160,3072]{1,0:T(8,128)(2,1)S(1)}, u32[]{:S(2)}, u32[]{:S(2)}) collective-permute-start(bf16[160,3072]{1,0:T(8,128)(2,1)S(1)} %slice.13), channel_id=1, source_target_pairs={{0,96},{8,104},{1,97},{9,105},{2,98},{10,106},{3,99},{11,107},{16,... | collective-permute-start | bytes 2949128 | tf_op jit(solution)/shard_map/ppermute | solution.py:46
  39.2 27.1 %collective-permute-start.4 = (bf16[160,3072]{1,0:T(8,128)(2,1)S(1)}, bf16[160,3072]{1,0:T(8,128)(2,1)S(1)}, u32[]{:S(2)}, u32[]{:S(2)}) collective-permute-start(bf16[160,3072]{1,0:T(8,128)(2,1)S(1)} %slice.13), channel_id=1, source_target_pairs={{0,32},{8,40},{1,33},{9,41},{2,34},{10,42},{3,35},{11,43},{16,48},... | collective-permute-start | bytes 2949128 | tf_op jit(solution)/shard_map/ppermute | solution.py:46
  39.2 44.2 %collective-permute-start.6 = (bf16[160,3072]{1,0:T(8,128)(2,1)S(1)}, bf16[160,3072]{1,0:T(8,128)(2,1)S(1)}, u32[]{:S(2)}, u32[]{:S(2)}) collective-permute-start(bf16[160,3072]{1,0:T(8,128)(2,1)S(1)} %collective-permute-done.1.rest_1_), channel_id=1, source_target_pairs={{0,32},{8,40},{1,33},{9,41},{2,34},{10,42},{3,35},{11,43},{16,48},... | collective-permute-start | bytes 2949128 | tf_op jit(solution)/shard_map/ppermute | solution.py:46
  59.1 25.3 %collective-permute-start.7 = (bf16[160,3072]{1,0:T(8,128)(2,1)S(1)}, bf16[160,3072]{1,0:T(8,128)(2,1)}, u32[]{:S(2)}, u32[]{:S(2)}) collective-permute-start(bf16[160,3072]{1,0:T(8,128)(2,1)S(1)} %collective-permute-done.5.rest_4_), channel_id=1, source_target_pairs={{0,96},{8,104},{1,97},{9,105},{2,98},{10,106},{3,99},{11,107},{16,... | collective-permute-start | bytes 2949128 | tf_op jit(solution)/shard_map/ppermute | solution.py:46
  63.6 61.9 %collective-permute-start.8 = (bf16[320,3072]{1,0:T(8,128)(2,1)}, bf16[320,3072]{1,0:T(8,128)(2,1)}, u32[]{:S(2)}, u32[]{:S(2)}) collective-permute-start(bf16[320,3072]{1,0:T(8,128)(2,1)} %collective-permute-done.rest_0_), channel_id=1, source_target_pairs={{0,32},{8,40},{1,33},{9,41},{2,34},{10,42},{3,35},{11,43},{16,48},... | collective-permute-start | bytes 5898248 | tf_op jit(solution)/shard_map/ppermute | solution.py:46
  63.6 61.9 %collective-permute-start.9 = (bf16[320,3072]{1,0:T(8,128)(2,1)}, bf16[320,3072]{1,0:T(8,128)(2,1)}, u32[]{:S(2)}, u32[]{:S(2)}) collective-permute-start(bf16[320,3072]{1,0:T(8,128)(2,1)} %collective-permute-done.rest_0_), channel_id=1, source_target_pairs={{0,96},{8,104},{1,97},{9,105},{2,98},{10,106},{3,99},{11,107},{16,... | collective-permute-start | bytes 5898248 | tf_op jit(solution)/shard_map/ppermute | solution.py:46
  102.9 25.0 %all-to-all-start.1 = ((bf16[8,128,768]{2,1,0:T(8,128)(2,1)}), bf16[8,128,768]{2,1,0:T(8,128)(2,1)S(1)}, u32[]{:S(2)}, u32[]{:S(2)}) async-start(bf16[8,128,768]{2,1,0:T(8,128)(2,1)} %attend.1), calls=%async_computation.1 | async-start | bytes 3145728 | tf_op jit(solution)/shard_map/all_to_all | solution.py:332
  127.9 8.0 %copy-start.2 = (bf16[160,3072]{1,0:T(8,128)(2,1)S(1)}, bf16[160,3072]{1,0:T(8,128)(2,1)}, u32[]{:S(2)}) copy-start(bf16[160,3072]{1,0:T(8,128)(2,1)} %copy-done.1) | copy-start | bytes 2949124
  127.9 8.0 %copy-start.4 = (bf16[160,3072]{1,0:T(8,128)(2,1)S(1)}, bf16[160,3072]{1,0:T(8,128)(2,1)}, u32[]{:S(2)}) copy-start(bf16[160,3072]{1,0:T(8,128)(2,1)} %copy-done.3) | copy-start | bytes 2949124
  127.9 8.0 %collective-permute-start.10 = (bf16[8,128,768]{2,1,0:T(8,128)(2,1)S(1)}, bf16[8,128,768]{2,1,0:T(8,128)(2,1)S(1)}, u32[]{:S(2)}, u32[]{:S(2)}) collective-permute-start(bf16[8,128,768]{2,1,0:T(8,128)(2,1)S(1)} %all-to-all-done.1.own_ref), channel_id=1, source_target_pairs={{0,8},{8,0},{1,9},{9,1},{2,10},{10,2},{3,11},{11,3},{16,24},{24,16... | collective-permute-start | bytes 4718600 | tf_op jit(solution)/shard_map/ppermute | solution.py:46
  129.1 17.9 %collective-permute-start.13 = (bf16[160,3072]{1,0:T(8,128)(2,1)}, bf16[160,3072]{1,0:T(8,128)(2,1)S(1)}, u32[]{:S(2)}, u32[]{:S(2)}) collective-permute-start(bf16[160,3072]{1,0:T(8,128)(2,1)} %collective-permute-done.7.rest_6_), channel_id=1, source_target_pairs={{0,16},{8,28},{1,17},{9,29},{2,18},{10,30},{3,19},{11,31},{16,4},{... | collective-permute-start | bytes 2949128 | tf_op jit(solution)/shard_map/ppermute | solution.py:46
  131.9 15.2 %collective-permute-start.11 = (bf16[80,3072]{1,0:T(8,128)(2,1)S(1)}, bf16[80,3072]{1,0:T(8,128)(2,1)S(1)}, u32[]{:S(2)}, u32[]{:S(2)}) collective-permute-start(bf16[80,3072]{1,0:T(8,128)(2,1)S(1)} %slice.14), channel_id=1, source_target_pairs={{0,32},{8,40},{1,33},{9,41},{2,34},{10,42},{3,35},{11,43},{16,48},... | collective-permute-start | bytes 1474568 | tf_op jit(solution)/shard_map/ppermute | solution.py:46
  134.0 13.0 %collective-permute-start.12 = (bf16[80,3072]{1,0:T(8,128)(2,1)S(1)}, bf16[80,3072]{1,0:T(8,128)(2,1)S(1)}, u32[]{:S(2)}, u32[]{:S(2)}) collective-permute-start(bf16[80,3072]{1,0:T(8,128)(2,1)S(1)} %slice.15), channel_id=1, source_target_pairs={{0,96},{8,104},{1,97},{9,105},{2,98},{10,106},{3,99},{11,107},{16,... | collective-permute-start | bytes 1474568 | tf_op jit(solution)/shard_map/ppermute | solution.py:46
  135.9 1.2 copy-start.6
  137.1 1.2 copy-start.8
  146.9 8.3 %collective-permute-start.14 = (bf16[2,128,1280]{2,1,0:T(8,128)(2,1)S(1)}, bf16[2,128,1280]{2,1,0:T(8,128)(2,1)S(1)}, u32[]{:S(2)}, u32[]{:S(2)}) collective-permute-start(bf16[2,128,1280]{2,1,0:T(8,128)(2,1)S(1)} %get-tuple-element.42), channel_id=1, source_target_pairs={{0,8},{8,0},{1,9},{9,1},{2,10},{10,2},{3,11},{11,3},{16,24},{24,16... | collective-permute-start | bytes 1966088 | tf_op jit(solution)/shard_map/ppermute | solution.py:46
  154.7 2.3 %collective-permute-start.15 = (bf16[2,128,1280]{2,1,0:T(8,128)(2,1)S(1)}, bf16[2,128,1280]{2,1,0:T(8,128)(2,1)S(1)}, u32[]{:S(2)}, u32[]{:S(2)}) collective-permute-start(bf16[2,128,1280]{2,1,0:T(8,128)(2,1)S(1)} %get-tuple-element.43), channel_id=1, source_target_pairs={{0,8},{8,0},{1,9},{9,1},{2,10},{10,2},{3,11},{11,3},{16,24},{24,16... | collective-permute-start | bytes 1966088 | tf_op jit(solution)/shard_map/ppermute | solution.py:46
  (4 other events, 3.8 us)

commit v2 on v1

--- a/solution.py
+++ b/solution.py
@@ -141,98 +141,81 @@
     )(packed, *(() if earlier is None else (earlier,)))
 
 
-def gates_body(info_ref, gate_hbm, gate_dot_hbm, out_ref, wide, sem):
-    copies = []
+def prepare_body(n, info_ref, gate_hbm, gate_dot_hbm, *rest):
+    weights = rest[:n]
+    gates_ref, w_ref, wide, sem, w_sem = rest[n:]
+    copies, at = [], 0
     for who in range(2):
         row = pl.multiple_of(info_ref[who] // 8 * 8, 8)
         for t, table in enumerate((gate_hbm, gate_dot_hbm)):
             copies.append(pltpu.make_async_copy(table.at[pl.ds(row, 8), :], wide.at[who, t], sem.at[who, t]))
+    for i, weight in enumerate(weights):
+        rows = weight.shape[0]
+        copies.append(pltpu.make_async_copy(weight, w_ref.at[pl.ds(at, rows), :], w_sem.at[i]))
+        at += rows
     for c in copies:
         c.start()
     for c in copies:
         c.wait()
     for who in range(2):
         for t in range(2):
-            out_ref[2 * who + t : 2 * who + t + 1] = wide[who, t, pl.ds(info_ref[who] % 8, 1), :]
-
-
-def pick_gates(times, gate_table, gate_dot_table):
+            gates_ref[2 * who + t : 2 * who + t + 1] = wide[who, t, pl.ds(info_ref[who] % 8, 1), :]
+
+
+def prepare(times, gate_table, gate_dot_table, weights):
     width = gate_table.shape[1]
-    hbm = pl.BlockSpec(memory_space=pltpu.HBM)
-    return pl.pallas_call(
-        gates_body,
-        in_specs=[pl.BlockSpec(memory_space=pltpu.SMEM), hbm, hbm],
-        out_specs=pl.BlockSpec(memory_space=pltpu.VMEM),
-        out_shape=jax.ShapeDtypeStruct((4, width), F32),
-        scratch_shapes=[pltpu.VMEM((2, 2, 8, width), F32), pltpu.SemaphoreType.DMA((2, 2))],
-        compiler_params=pltpu.CompilerParams(vmem_limit_bytes=VMEM_ALL),
-        cost_estimate=NO_COST,
-        name="pick_gates",
-    )(times, gate_table, gate_dot_table)
-
-
-def gates_body(info_ref, gate_hbm, gate_dot_hbm, out_ref, wide, sem):
-    copies = []
-    for who in range(2):
-        row = pl.multiple_of(info_ref[who] // 8 * 8, 8)
-        for t, table in enumerate((gate_hbm, gate_dot_hbm)):
-            copies.append(pltpu.make_async_copy(table.at[pl.ds(row, 8), :], wide.at[who, t], sem.at[who, t]))
-    for c in copies:
-        c.start()
-    for c in copies:
-        c.wait()
-    for who in range(2):
-        for t in range(2):
-            out_ref[2 * who + t : 2 * who + t + 1] = wide[who, t, pl.ds(info_ref[who] % 8, 1), :]
-
-
-def pick_gates(times, gate_table, gate_dot_table):
-    width = gate_table.shape[1]
-    hbm = pl.BlockSpec(memory_space=pltpu.HBM)
-    return pl.pallas_call(
-        gates_body,
-        in_specs=[pl.BlockSpec(memory_space=pltpu.SMEM), hbm, hbm],
-        out_specs=pl.BlockSpec(memory_space=pltpu.VMEM),
-        out_shape=jax.ShapeDtypeStruct((4, width), F32),
-        scratch_shapes=[pltpu.VMEM((2, 2, 8, width), F32), pltpu.SemaphoreType.DMA((2, 2))],
-        compiler_params=pltpu.CompilerParams(vmem_limit_bytes=VMEM_ALL),
-        cost_estimate=NO_COST,
-        name="pick_gates",
-    )(times, gate_table, gate_dot_table)
+    n = len(weights)
+    total = sum(a.shape[0] for a in weights)
+    anywhere = pl.BlockSpec(memory_space=pl.ANY)
+    vmem = pl.BlockSpec(memory_space=pltpu.VMEM)
+    return pl.pallas_call(
+        functools.partial(prepare_body, n),
+        in_specs=[pl.BlockSpec(memory_space=pltpu.SMEM)] + [anywhere] * (2 + n),
+        out_specs=[vmem, vmem],
+        out_shape=[
+            jax.ShapeDtypeStruct((4, width), F32),
+            jax.ShapeDtypeStruct((total, weights[0].shape[1]), BF16),
+        ],
+        scratch_shapes=[
+            pltpu.VMEM((2, 2, 8, width), F32),
+            pltpu.SemaphoreType.DMA((2, 2)),
+            pltpu.SemaphoreType.DMA((n,)),
+        ],
+        compiler_params=pltpu.CompilerParams(vmem_limit_bytes=36 * MIB),
+        cost_estimate=NO_COST,
+        name="prepare",
+    )(times, gate_table, gate_dot_table, *weights)
 
 
 def round_up(n, unit):
     return -(-n // unit) * unit
 
 
-def project_body(n, first, info_ref, gates_ref, own_ref, peer_ref, *rest):
+def project_body(n, first, ready_rows, info_ref, gates_ref, own_ref, peer_ref, *rest):
+    ready = rest[0] if ready_rows else None
+    rest = rest[1:] if ready_rows else rest
     weights = rest[:n]
-    mine_ref, send_ref = rest[n : n + 2]
-    x, w, w_sem = rest[n + 2 :]
+    mine_ref, send_ref, x, w, w_sem = rest[n:]
     groups, tokens, _ = own_ref.shape
     heads = own_ref.shape[2] // (2 * HD)
 
-    at, ends, w_copies = 0, [], []
+    at, w_copies = 0, []
     for i, weight in enumerate(weights):
         rows = weight.shape[0]
         w_copies.append(pltpu.make_async_copy(weight, w.at[pl.ds(at, rows), :], w_sem.at[i]))
         at += rows
-        ends.append(at)
     for c in w_copies:
         c.start()
 
-    pieces = ends[-1] // PIECE
-
-    def gate_rows(line):
+    def gate_rows(line, begin, end):
         parts = []
-        for i in range(pieces):
+        for i in range(begin // PIECE, end // PIECE):
             column = info_ref[first + i] * PIECE
             base = pl.multiple_of(column // HD * HD, HD)
             wide = gates_ref[line : line + 1, pl.ds(base, 3 * HD)]
             parts.append(jnp.where(column % HD != 0, wide[:, HD // 2 : HD // 2 + PIECE], wide[:, :PIECE]))
         return jnp.concatenate(parts, axis=1)
 
-    lines = [gate_rows(line) for line in range(4)]
     for who, ref in enumerate((own_ref, peer_ref)):
         for g in range(groups):
             for h in range(heads):
@@ -241,39 +224,47 @@
                     row = (2 * who + t) * tokens
                     src = (2 * h + t) * HD
                     x[row : row + tokens, at : at + HD] = ref[g, :, src : src + HD]
+
+    def part(weight_ref, begin):
+        end = begin + weight_ref.shape[0]
+        y = lax.dot_general(x[...], weight_ref[...], NT, preferred_element_type=F32)
+        for who, ref in enumerate((mine_ref, send_ref)):
+            gate, gate_dot = (gate_rows(2 * who + t, begin, end) for t in range(2))
+            primal = y[2 * who * tokens : (2 * who + 1) * tokens]
+            tangent = y[(2 * who + 1) * tokens : (2 * who + 2) * tokens]
+            ref[0, :, begin:end] = (gate * primal).astype(BF16)
+            ref[1, :, begin:end] = (gate_dot * primal + gate * tangent).astype(BF16)
+
+    if ready_rows:
+        part(ready, 0)
     for c in w_copies:
         c.wait()
-    y = lax.dot_general(x[...], w[...], NT, preferred_element_type=F32)
-    for who, ref in enumerate((mine_ref, send_ref)):
-        gate, gate_dot = lines[2 * who], lines[2 * who + 1]
-        primal = y[2 * who * tokens : (2 * who + 1) * tokens]
-        tangent = y[(2 * who + 1) * tokens : (2 * who + 2) * tokens]
-        ref[0] = (gate * primal).astype(BF16)
-        ref[1] = (gate_dot * primal + gate * tangent).astype(BF16)
-
-
-def project(info, first, own, peer, gates, weights):
+    part(w, ready_rows)
+
+
+def project(info, first, own, peer, gates, ready, weights):
     groups, tokens, _ = own.shape
     n = len(weights)
-    total = sum(a.shape[0] for a in weights)
+    rows = sum(a.shape[0] for a in weights)
+    ready_rows = 0 if ready is None else ready.shape[0]
     depth = weights[0].shape[1]
     hbm = pl.BlockSpec(memory_space=pltpu.HBM)
     vmem = pl.BlockSpec(memory_space=pltpu.VMEM)
-    half = jax.ShapeDtypeStruct((2, tokens, total), BF16)
-    return pl.pallas_call(
-        functools.partial(project_body, n, first),
-        in_specs=[pl.BlockSpec(memory_space=pltpu.SMEM)] + [vmem] * 3 + [hbm] * n,
+    half = jax.ShapeDtypeStruct((2, tokens, round_up(ready_rows + rows, HD)), BF16)
+    return pl.pallas_call(
+        functools.partial(project_body, n, first, ready_rows),
+        in_specs=[pl.BlockSpec(memory_space=pltpu.SMEM)] + [vmem] * (3 if ready is None else 4) + [hbm] * n,
         out_specs=[vmem, vmem],
         out_shape=[half, half],
         scratch_shapes=[
             pltpu.VMEM((4 * tokens, depth), BF16),
-            pltpu.VMEM((total, depth), BF16),
+            pltpu.VMEM((rows, depth), BF16),
             pltpu.SemaphoreType.DMA((n,)),
         ],
         compiler_params=pltpu.CompilerParams(vmem_limit_bytes=36 * MIB),
         cost_estimate=NO_COST,
         name="project",
-    )(info, gates, own, peer, *weights)
+    )(info, gates, own, peer, *(() if ready is None else (ready,)), *weights)
 
 
 def merge_body(spots, info_ref, *refs):
@@ -364,19 +355,20 @@
 
     attn = attend(received, 0, 3)
     own = exchange(attn)
-    gates = pick_gates(times, gate_table, gate_dot_table)
-    own, near_a, near_b, gates, c2 = lax.optimization_barrier((own, near_a, near_b, gates, c2))
+    gates, here = prepare(times, gate_table, gate_dot_table, (weight, a1, a2, b1, b2, c1, c2))
+    own, near_a, near_b, gates, here, c2 = lax.optimization_barrier((own, near_a, near_b, gates, here, c2))
 
     peer = move(own, swap)
     near_c1 = move(near_a[: half // 2], up)
     near_c2 = move(near_b[half // 2 : half], down)
     near_c3 = move(c2, beside())
 
-    mine_a, sent_a = project(info, 0, own, peer, gates, (weight, a1, a2, b1, b2, c1, c2))
+    mine_a, sent_a = project(info, 0, own, peer, gates, here, (near, near_a, near_b))
+    mine_a, sent_a, near_c1, near_c2, near_c3 = lax.optimization_barrier((mine_a, sent_a, near_c1, near_c2, near_c3))
     got_a = move(sent_a, swap)
-    mine_b, sent_b = project(info, 4, own, peer, gates, (near, near_a, near_b, near_c1, near_c2, near_c3))
+    mine_b, sent_b = project(info, 7, own, peer, gates, None, (near_c1, near_c2, near_c3))
     got_b = move(sent_b, swap)
-    spots = [(part, i) for part in range(2) for i in range(4)]
+    spots = [(0, i) for i in range(7)] + [(1, 0)]
     return tuple(merge(info, spots, (mine_a, mine_b), (got_a, got_b), gate_table.shape[1]))
 
 

time: 160 us -> 157 us (0.981)
  waiting for transfers between devices: 77.3 us -> 62.8 us
  local copies, waits for them, and re-layouts: 10.7 us -> 20.7 us
    ppermute x16, waiting for transfers between devices: 67.6 us -> 54.1 us  [move(): return lax.ppermute(a, ('fsdp', 'seq'), perm)]
    unnamed x20 -> x32, local copies, waits for them, and re-layouts: 6.19 us -> 16.2 us
  transfers between devices with their start and end apart: 18 -> 18, of which waited for: 7 -> 7; matrix products, arithmetic and copies ran while one was open for 4% -> 3% of each run, Pallas kernels for 22% -> 23%
where the time goes in v2:
time: 157 us; the launch traced here: 156 us
  waiting for transfers between devices  62.8 us (40%)
  Pallas kernels  39 us (25%)
  starting transfers between devices  31.2 us (20%)
  local copies, waits for them, and re-layouts  20.7 us (13%)
    ppermute x16, waiting for transfers between devices, move(): return lax.ppermute(a, ('fsdp', 'seq'), perm)  54.1 us
    ppermute x16, starting transfers between devices, move(): return lax.ppermute(a, ('fsdp', 'seq'), perm)  21.7 us
    unnamed x32, local copies, waits for them, and re-layouts  16.2 us
    pallas_call x2, Pallas kernels, project(): pl.pallas_call(functools.partial(project_body, n, first, ready_rows), in_...  15.5 us
    pallas_call x1, Pallas kernels, attend(): pl.pallas_call(attn_body, grid=(width // (6 * HD),), in_specs=[pl.BlockSp...  11.4 us
    all_to_all x2, starting transfers between devices, exchange(): return lax.all_to_all(a, 'seq', split_axis=0, concat_axis=0, tiled=True)  9.5 us
    all_to_all x2, waiting for transfers between devices, exchange(): return lax.all_to_all(a, 'seq', split_axis=0, concat_axis=0, tiled=True)  8.68 us
    pallas_call x1, Pallas kernels, norm_pack(): pl.pallas_call(norm_body, grid=(tokens // rows,), in_specs=[wide] * 6 + [...  5.85 us
  transfers between devices with their start and end apart: 18, of which 7 were waited for; matrix products, arithmetic and copies ran while one was open for 3% of the time, Pallas kernels for 23%

profile of v2, /device:TPU:1, one launch (start us, length us, event | category | flops | bytes accessed | tf_op | source)
XLA Modules:
  0.0 155.8 jit_solution(3313088925328159097)
XLA Ops:
  0.6 3.4 %collective-permute-start = (bf16[320,3072]{1,0:T(8,128)(2,1)}, bf16[320,3072]{1,0:T(8,128)(2,1)}, u32[]{:S(2)}, u32[]{:S(2)}) collective-permute-start(bf16[320,3072]{1,0:T(8,128)(2,1)} %bitcast.20), channel_id=1, source_target_pairs={{0,16},{8,28},{1,17},{9,29},{2,18},{10,30},{3,19},{11,31},{16,4},{... | collective-permute-start | bytes 5898248 | tf_op jit(solution)/shard_map/ppermute | solution.py:46
  4.0 2.2 %slice.16 = bf16[160,3072]{1,0:T(8,128)(2,1)} slice(bf16[320,3072]{1,0:T(8,128)(2,1)} %bitcast.21), slice={[0:160], [0:3072]} | slice | bytes 1966080 | tf_op jit(solution)/shard_map/slice | solution.py:334
  7.5 1.4 collective-permute-start.2
  9.9 5.8 %norm_pack.1 = bf16[8,128,2304]{2,1,0:T(8,128)(2,1)} custom-call(bf16[128,3072]{1,0:T(8,128)(2,1)} %q_ref.1, bf16[128,3072]{1,0:T(8,128)(2,1)} %qd_ref.1, bf16[128,3072]{1,0:T(8,128)(2,1)} %k_ref.1, bf16[128,3072]{1,0:T(8,128)(2,1)} %kd_ref.1, bf16[128,3072]{1,0:T(8,128)(2,1)} %v_ref.1, bf16[128,3072]{1,0:T(8,128)(2,1)} %vd_ref.1, f32[1,3072]{1,0:T(1,128)} %bitcast.24, ...), custom_call_target="tpu_custom_call" | custom-call | tf_op jit(solution)/shard_map/norm_pack/pallas_call | solution.py:81
  16.5 14.9 %collective-permute-done.1.rest_1_ = bf16[160,3072]{1,0:T(8,128)(2,1)S(1)} collective-permute-done((bf16[160,3072]{1,0:T(8,128)(2,1)}, bf16[160,3072]{1,0:T(8,128)(2,1)S(1)}, u32[]{:S(2)}, u32[]{:S(2)}) %collective-permute-start.1) | collective-permute-done | bytes 983072 | tf_op jit(solution)/shard_map/ppermute | solution.py:46
  31.4 5.0 %all-to-all-start = ((bf16[8,128,2304]{2,1,0:T(8,128)(2,1)}), bf16[8,128,2304]{2,1,0:T(8,128)(2,1)}, u32[]{:S(2)}, u32[]{:S(2)}) async-start(bf16[8,128,2304]{2,1,0:T(8,128)(2,1)} %norm_pack.1), calls=%async_computation | async-start | bytes 9437184 | tf_op jit(solution)/shard_map/all_to_all | solution.py:323
  36.5 2.6 %collective-permute-start.5 = (bf16[160,3072]{1,0:T(8,128)(2,1)S(1)}, bf16[160,3072]{1,0:T(8,128)(2,1)S(1)}, u32[]{:S(2)}, u32[]{:S(2)}) collective-permute-start(bf16[160,3072]{1,0:T(8,128)(2,1)S(1)} %slice.13), channel_id=1, source_target_pairs={{0,96},{8,104},{1,97},{9,105},{2,98},{10,106},{3,99},{11,107},{16,... | collective-permute-start | bytes 2949128 | tf_op jit(solution)/shard_map/ppermute | solution.py:46
  39.2 19.8 %collective-permute-done.5.rest_4_ = bf16[160,3072]{1,0:T(8,128)(2,1)S(1)} collective-permute-done((bf16[160,3072]{1,0:T(8,128)(2,1)S(1)}, bf16[160,3072]{1,0:T(8,128)(2,1)S(1)}, u32[]{:S(2)}, u32[]{:S(2)}) %collective-permute-start.5) | collective-permute-done | bytes 983072 | tf_op jit(solution)/shard_map/ppermute | solution.py:46
  59.1 3.5 %collective-permute-start.7 = (bf16[160,3072]{1,0:T(8,128)(2,1)S(1)}, bf16[160,3072]{1,0:T(8,128)(2,1)S(1)}, u32[]{:S(2)}, u32[]{:S(2)}) collective-permute-start(bf16[160,3072]{1,0:T(8,128)(2,1)S(1)} %collective-permute-done.5.rest_4_), channel_id=1, source_target_pairs={{0,96},{8,104},{1,97},{9,105},{2,98},{10,106},{3,99},{11,107},{16,... | collective-permute-start | bytes 2949128 | tf_op jit(solution)/shard_map/ppermute | solution.py:46
  63.6 2.7 %collective-permute-start.9 = (bf16[320,3072]{1,0:T(8,128)(2,1)}, bf16[320,3072]{1,0:T(8,128)(2,1)}, u32[]{:S(2)}, u32[]{:S(2)}) collective-permute-start(bf16[320,3072]{1,0:T(8,128)(2,1)} %collective-permute-done.rest_1_), channel_id=1, source_target_pairs={{0,96},{8,104},{1,97},{9,105},{2,98},{10,106},{3,99},{11,107},{16,... | collective-permute-start | bytes 5898248 | tf_op jit(solution)/shard_map/ppermute | solution.py:46
  67.2 16.2 %collective-permute-done.6.rest_5_ = bf16[160,3072]{1,0:T(8,128)(2,1)S(1)} collective-permute-done((bf16[160,3072]{1,0:T(8,128)(2,1)S(1)}, bf16[160,3072]{1,0:T(8,128)(2,1)S(1)}, u32[]{:S(2)}, u32[]{:S(2)}) %collective-permute-start.6) | collective-permute-done | bytes 983072 | tf_op jit(solution)/shard_map/ppermute | solution.py:46
  85.3 6.2 %all-to-all-done.in_ref = bf16[8,128,2304]{2,1,0:T(8,128)(2,1)} async-done(((bf16[8,128,2304]{2,1,0:T(8,128)(2,1)}), bf16[8,128,2304]{2,1,0:T(8,128)(2,1)}, u32[]{:S(2)}, u32[]{:S(2)}) %all-to-all-start) | async-done | bytes 4718624 | tf_op jit(solution)/shard_map/all_to_all | solution.py:323
  91.6 11.4 %attend.1 = bf16[8,128,768]{2,1,0:T(8,128)(2,1)} custom-call(bf16[8,128,2304]{2,1,0:T(8,128)(2,1)} %all-to-all-done.in_ref), custom_call_target="tpu_custom_call" | custom-call | tf_op jit(solution)/shard_map/attend/pallas_call | solution.py:130
  102.9 4.5 %all-to-all-start.1 = ((bf16[8,128,768]{2,1,0:T(8,128)(2,1)}), bf16[8,128,768]{2,1,0:T(8,128)(2,1)S(1)}, u32[]{:S(2)}, u32[]{:S(2)}) async-start(bf16[8,128,768]{2,1,0:T(8,128)(2,1)} %attend.1), calls=%async_computation.1 | async-start | bytes 3145728 | tf_op jit(solution)/shard_map/all_to_all | solution.py:323
  108.7 1.3 copy-done.3
  116.0 3.6 %prepare.1 = (f32[4,5120]{1,0:T(4,128)S(1)}, bf16[1280,3072]{1,0:T(8,128)(2,1)S(1)}) custom-call(s32[2]{0:T(128)S(1)} %pad_add_fusion.info_ref, f32[64,5120]{1,0:T(8,128)S(1)} %copy-done.2, f32[64,5120]{1,0:T(8,128)S(1)} %copy-done.3, bf16[320,3072]{1,0:T(8,128)(2,1)S(1)} %bitcast.23, bf16[160,3072]{1,0:T(8,128)(2,1)S(1)} %copy-done.5, ...), custom_call_target="tpu_custom_call" | custom-call | tf_op jit(solution)/shard_map/prepare/pallas_call | solution.py:171
  119.7 3.0 %copy-done = bf16[1280,3072]{1,0:T(8,128)(2,1)} copy-done((bf16[1280,3072]{1,0:T(8,128)(2,1)}, bf16[1280,3072]{1,0:T(8,128)(2,1)S(1)}, u32[]{:S(2)}) %copy-start) | copy-done | bytes 7864344
  123.4 2.1 %collective-permute-done.8.rest_2_ = bf16[320,3072]{1,0:T(8,128)(2,1)} collective-permute-done((bf16[320,3072]{1,0:T(8,128)(2,1)}, bf16[320,3072]{1,0:T(8,128)(2,1)}, u32[]{:S(2)}, u32[]{:S(2)}) %collective-permute-start.8) | collective-permute-done | bytes 1966112 | tf_op jit(solution)/shard_map/ppermute | solution.py:46
  125.5 2.5 %all-to-all-done.1.own_ref = bf16[8,128,768]{2,1,0:T(8,128)(2,1)S(1)} async-done(((bf16[8,128,768]{2,1,0:T(8,128)(2,1)}), bf16[8,128,768]{2,1,0:T(8,128)(2,1)S(1)}, u32[]{:S(2)}, u32[]{:S(2)}) %all-to-all-start.1) | async-done | bytes 1572896 | tf_op jit(solution)/shard_map/all_to_all | solution.py:323
  129.1 1.7 %collective-permute-start.13 = (bf16[160,3072]{1,0:T(8,128)(2,1)}, bf16[160,3072]{1,0:T(8,128)(2,1)S(1)}, u32[]{:S(2)}, u32[]{:S(2)}) collective-permute-start(bf16[160,3072]{1,0:T(8,128)(2,1)} %copy-done.6), channel_id=1, source_target_pairs={{0,16},{8,28},{1,17},{9,29},{2,18},{10,30},{3,19},{11,31},{16,4},{... | collective-permute-start | bytes 2949128 | tf_op jit(solution)/shard_map/ppermute | solution.py:46
  134.0 1.9 %collective-permute-start.12 = (bf16[80,3072]{1,0:T(8,128)(2,1)S(1)}, bf16[80,3072]{1,0:T(8,128)(2,1)S(1)}, u32[]{:S(2)}, u32[]{:S(2)}) collective-permute-start(bf16[80,3072]{1,0:T(8,128)(2,1)S(1)} %slice.15), channel_id=1, source_target_pairs={{0,96},{8,104},{1,97},{9,105},{2,98},{10,106},{3,99},{11,107},{16,... | collective-permute-start | bytes 1474568 | tf_op jit(solution)/shard_map/ppermute | solution.py:46
  135.9 11.1 %project.2 = (bf16[2,128,2304]{2,1,0:T(8,128)(2,1)S(1)}, bf16[2,128,2304]{2,1,0:T(8,128)(2,1)S(1)}) custom-call(s32[17]{0:T(128)S(1)} %stack.71.info_ref, f32[4,5120]{1,0:T(4,128)S(1)} %copy-done.15, bf16[8,128,768]{2,1,0:T(8,128)(2,1)S(1)} %all-to-all-done.1.own_ref, bf16[8,128,768]{2,1,0:T(8,128)(2,1)S(1)} %collective-permute-done.10.peer_ref, ...), custom_call_target="tpu_custom_call" | custom-call | tf_op jit(solution)/shard_map/project/pallas_call | solution.py:254
  147.2 4.4 %project.3 = (bf16[2,128,384]{2,1,0:T(8,128)(2,1)S(1)}, bf16[2,128,384]{2,1,0:T(8,128)(2,1)S(1)}) custom-call(s32[17]{0:T(128)S(1)} %stack.71.info_ref, f32[4,5120]{1,0:T(4,128)S(1)} %copy-done.15, bf16[8,128,768]{2,1,0:T(8,128)(2,1)S(1)} %all-to-all-done.1.own_ref, bf16[8,128,768]{2,1,0:T(8,128)(2,1)S(1)} %collective-permute-done.10.peer_ref, ...), custom_call_target="tpu_custom_call" | custom-call | tf_op jit(solution)/shard_map/project/pallas_call | solution.py:254
  153.3 2.6 %merge.1 = (bf16[128,5120]{1,0:T(8,128)(2,1)}, bf16[128,5120]{1,0:T(8,128)(2,1)}) custom-call(s32[17]{0:T(128)S(1)} %stack.71.info_ref, bf16[2,128,2304]{2,1,0:T(8,128)(2,1)S(1)} %get-tuple-element.53.refs_0_, bf16[2,128,384]{2,1,0:T(8,128)(2,1)S(1)} %get-tuple-element.57.refs_1_, bf16[2,128,2304]{2,1,0:T(8,128)(2,1)S(1)} %collective-permute-done.14.refs_2_, ...), custom_call_target="tpu_custom_call" | custom-call | tf_op jit(solution)/shard_map/merge/pallas_call | solution.py:290
  (56 shorter events, 20.4 us)
Async XLA Ops:
  0.6 30.8 %collective-permute-start = (bf16[320,3072]{1,0:T(8,128)(2,1)}, bf16[320,3072]{1,0:T(8,128)(2,1)}, u32[]{:S(2)}, u32[]{:S(2)}) collective-permute-start(bf16[320,3072]{1,0:T(8,128)(2,1)} %bitcast.20), channel_id=1, source_target_pairs={{0,16},{8,28},{1,17},{9,29},{2,18},{10,30},{3,19},{11,31},{16,4},{... | collective-permute-start | bytes 5898248 | tf_op jit(solution)/shard_map/ppermute | solution.py:46
  6.2 25.2 %collective-permute-start.1 = (bf16[160,3072]{1,0:T(8,128)(2,1)}, bf16[160,3072]{1,0:T(8,128)(2,1)S(1)}, u32[]{:S(2)}, u32[]{:S(2)}) collective-permute-start(bf16[160,3072]{1,0:T(8,128)(2,1)} %slice.16), channel_id=1, source_target_pairs={{0,32},{8,40},{1,33},{9,41},{2,34},{10,42},{3,35},{11,43},{16,48},... | collective-permute-start | bytes 2949128 | tf_op jit(solution)/shard_map/ppermute | solution.py:46
  7.5 23.9 %collective-permute-start.2 = (bf16[160,3072]{1,0:T(8,128)(2,1)}, bf16[160,3072]{1,0:T(8,128)(2,1)}, u32[]{:S(2)}, u32[]{:S(2)}) collective-permute-start(bf16[160,3072]{1,0:T(8,128)(2,1)} %slice.16), channel_id=1, source_target_pairs={{0,96},{8,104},{1,97},{9,105},{2,98},{10,106},{3,99},{11,107},{16,... | collective-permute-start | bytes 2949128 | tf_op jit(solution)/shard_map/ppermute | solution.py:46
  9.0 6.8 %collective-permute-start.3 = (s32[1]{0:T(128)}, s32[1]{0:T(128)}, u32[]{:S(2)}, u32[]{:S(2)}) collective-permute-start(s32[1]{0:T(128)} %param.23), channel_id=1, source_target_pairs={{0,8},{8,0},{1,9},{9,1},{2,10},{10,2},{3,11},{11,3},{16,24},{24,16... | collective-permute-start | bytes 20 | tf_op jit(solution)/shard_map/ppermute | solution.py:46
  16.5 20.0 %copy-start.1 = (bf16[3072,320]{0,1:T(8,128)(2,1)S(1)}, bf16[3072,320]{0,1:T(8,128)(2,1)}, u32[]{:S(2)}) copy-start(bf16[3072,320]{0,1:T(8,128)(2,1)} %param.20) | copy-start | bytes 5898244
  31.4 7.8 %copy-start.4 = (bf16[160,3072]{1,0:T(8,128)(2,1)}, bf16[160,3072]{1,0:T(8,128)(2,1)S(1)}, u32[]{:S(2)}) copy-start(bf16[160,3072]{1,0:T(8,128)(2,1)S(1)} %collective-permute-done.1.rest_1_) | copy-start | bytes 2949124
  31.4 60.1 %all-to-all-start = ((bf16[8,128,2304]{2,1,0:T(8,128)(2,1)}), bf16[8,128,2304]{2,1,0:T(8,128)(2,1)}, u32[]{:S(2)}, u32[]{:S(2)}) async-start(bf16[8,128,2304]{2,1,0:T(8,128)(2,1)} %norm_pack.1), calls=%async_computation | async-start | bytes 9437184 | tf_op jit(solution)/shard_map/all_to_all | solution.py:323
  36.5 22.5 %collective-permute-start.5 = (bf16[160,3072]{1,0:T(8,128)(2,1)S(1)}, bf16[160,3072]{1,0:T(8,128)(2,1)S(1)}, u32[]{:S(2)}, u32[]{:S(2)}) collective-permute-start(bf16[160,3072]{1,0:T(8,128)(2,1)S(1)} %slice.13), channel_id=1, source_target_pairs={{0,96},{8,104},{1,97},{9,105},{2,98},{10,106},{3,99},{11,107},{16,... | collective-permute-start | bytes 2949128 | tf_op jit(solution)/shard_map/ppermute | solution.py:46
  39.2 27.0 %collective-permute-start.4 = (bf16[160,3072]{1,0:T(8,128)(2,1)S(1)}, bf16[160,3072]{1,0:T(8,128)(2,1)S(1)}, u32[]{:S(2)}, u32[]{:S(2)}) collective-permute-start(bf16[160,3072]{1,0:T(8,128)(2,1)S(1)} %slice.13), channel_id=1, source_target_pairs={{0,32},{8,40},{1,33},{9,41},{2,34},{10,42},{3,35},{11,43},{16,48},... | collective-permute-start | bytes 2949128 | tf_op jit(solution)/shard_map/ppermute | solution.py:46
  39.2 44.2 %collective-permute-start.6 = (bf16[160,3072]{1,0:T(8,128)(2,1)S(1)}, bf16[160,3072]{1,0:T(8,128)(2,1)S(1)}, u32[]{:S(2)}, u32[]{:S(2)}) collective-permute-start(bf16[160,3072]{1,0:T(8,128)(2,1)S(1)} %collective-permute-done.1.rest_1_), channel_id=1, source_target_pairs={{0,32},{8,40},{1,33},{9,41},{2,34},{10,42},{3,35},{11,43},{16,48},... | collective-permute-start | bytes 2949128 | tf_op jit(solution)/shard_map/ppermute | solution.py:46
  59.1 25.3 %collective-permute-start.7 = (bf16[160,3072]{1,0:T(8,128)(2,1)S(1)}, bf16[160,3072]{1,0:T(8,128)(2,1)S(1)}, u32[]{:S(2)}, u32[]{:S(2)}) collective-permute-start(bf16[160,3072]{1,0:T(8,128)(2,1)S(1)} %collective-permute-done.5.rest_4_), channel_id=1, source_target_pairs={{0,96},{8,104},{1,97},{9,105},{2,98},{10,106},{3,99},{11,107},{16,... | collective-permute-start | bytes 2949128 | tf_op jit(solution)/shard_map/ppermute | solution.py:46
  63.6 61.9 %collective-permute-start.8 = (bf16[320,3072]{1,0:T(8,128)(2,1)}, bf16[320,3072]{1,0:T(8,128)(2,1)}, u32[]{:S(2)}, u32[]{:S(2)}) collective-permute-start(bf16[320,3072]{1,0:T(8,128)(2,1)} %collective-permute-done.rest_1_), channel_id=1, source_target_pairs={{0,32},{8,40},{1,33},{9,41},{2,34},{10,42},{3,35},{11,43},{16,48},... | collective-permute-start | bytes 5898248 | tf_op jit(solution)/shard_map/ppermute | solution.py:46
  63.6 61.9 %collective-permute-start.9 = (bf16[320,3072]{1,0:T(8,128)(2,1)}, bf16[320,3072]{1,0:T(8,128)(2,1)}, u32[]{:S(2)}, u32[]{:S(2)}) collective-permute-start(bf16[320,3072]{1,0:T(8,128)(2,1)} %collective-permute-done.rest_1_), channel_id=1, source_target_pairs={{0,96},{8,104},{1,97},{9,105},{2,98},{10,106},{3,99},{11,107},{16,... | collective-permute-start | bytes 5898248 | tf_op jit(solution)/shard_map/ppermute | solution.py:46
  102.9 25.0 %all-to-all-start.1 = ((bf16[8,128,768]{2,1,0:T(8,128)(2,1)}), bf16[8,128,768]{2,1,0:T(8,128)(2,1)S(1)}, u32[]{:S(2)}, u32[]{:S(2)}) async-start(bf16[8,128,768]{2,1,0:T(8,128)(2,1)} %attend.1), calls=%async_computation.1 | async-start | bytes 3145728 | tf_op jit(solution)/shard_map/all_to_all | solution.py:323
  107.4 1.3 copy-start.2
  108.7 1.3 copy-start.3
  119.7 3.1 %copy-start = (bf16[1280,3072]{1,0:T(8,128)(2,1)}, bf16[1280,3072]{1,0:T(8,128)(2,1)S(1)}, u32[]{:S(2)}) copy-start(bf16[1280,3072]{1,0:T(8,128)(2,1)S(1)} %get-tuple-element.47.rest_0_) | copy-start | bytes 23592964
  125.5 10.5 %copy-start.15 = (f32[4,5120]{1,0:T(4,128)S(1)}, f32[4,5120]{1,0:T(4,128)}, u32[]{:S(2)}) copy-start(f32[4,5120]{1,0:T(4,128)} %copy-done.14) | copy-start | bytes 245764
  127.9 8.0 %collective-permute-start.10 = (bf16[8,128,768]{2,1,0:T(8,128)(2,1)S(1)}, bf16[8,128,768]{2,1,0:T(8,128)(2,1)S(1)}, u32[]{:S(2)}, u32[]{:S(2)}) collective-permute-start(bf16[8,128,768]{2,1,0:T(8,128)(2,1)S(1)} %all-to-all-done.1.own_ref), channel_id=1, source_target_pairs={{0,8},{8,0},{1,9},{9,1},{2,10},{10,2},{3,11},{11,3},{16,24},{24,16... | collective-permute-start | bytes 4718600 | tf_op jit(solution)/shard_map/ppermute | solution.py:46
  129.1 17.9 %collective-permute-start.13 = (bf16[160,3072]{1,0:T(8,128)(2,1)}, bf16[160,3072]{1,0:T(8,128)(2,1)S(1)}, u32[]{:S(2)}, u32[]{:S(2)}) collective-permute-start(bf16[160,3072]{1,0:T(8,128)(2,1)} %copy-done.6), channel_id=1, source_target_pairs={{0,16},{8,28},{1,17},{9,29},{2,18},{10,30},{3,19},{11,31},{16,4},{... | collective-permute-start | bytes 2949128 | tf_op jit(solution)/shard_map/ppermute | solution.py:46
  131.9 15.2 %collective-permute-start.11 = (bf16[80,3072]{1,0:T(8,128)(2,1)S(1)}, bf16[80,3072]{1,0:T(8,128)(2,1)S(1)}, u32[]{:S(2)}, u32[]{:S(2)}) collective-permute-start(bf16[80,3072]{1,0:T(8,128)(2,1)S(1)} %slice.14), channel_id=1, source_target_pairs={{0,32},{8,40},{1,33},{9,41},{2,34},{10,42},{3,35},{11,43},{16,48},... | collective-permute-start | bytes 1474568 | tf_op jit(solution)/shard_map/ppermute | solution.py:46
  134.0 13.0 %collective-permute-start.12 = (bf16[80,3072]{1,0:T(8,128)(2,1)S(1)}, bf16[80,3072]{1,0:T(8,128)(2,1)S(1)}, u32[]{:S(2)}, u32[]{:S(2)}) collective-permute-start(bf16[80,3072]{1,0:T(8,128)(2,1)S(1)} %slice.15), channel_id=1, source_target_pairs={{0,96},{8,104},{1,97},{9,105},{2,98},{10,106},{3,99},{11,107},{16,... | collective-permute-start | bytes 1474568 | tf_op jit(solution)/shard_map/ppermute | solution.py:46
  147.1 6.2 %collective-permute-start.14 = (bf16[2,128,2304]{2,1,0:T(8,128)(2,1)S(1)}, bf16[2,128,2304]{2,1,0:T(8,128)(2,1)S(1)}, u32[]{:S(2)}, u32[]{:S(2)}) collective-permute-start(bf16[2,128,2304]{2,1,0:T(8,128)(2,1)S(1)} %get-tuple-element.58), channel_id=1, source_target_pairs={{0,8},{8,0},{1,9},{9,1},{2,10},{10,2},{3,11},{11,3},{16,24},{24,16... | collective-permute-start | bytes 3538952 | tf_op jit(solution)/shard_map/ppermute | solution.py:46
  151.6 1.6 %collective-permute-start.15 = (bf16[2,128,384]{2,1,0:T(8,128)(2,1)S(1)}, bf16[2,128,384]{2,1,0:T(8,128)(2,1)S(1)}, u32[]{:S(2)}, u32[]{:S(2)}) collective-permute-start(bf16[2,128,384]{2,1,0:T(8,128)(2,1)S(1)} %get-tuple-element.59), channel_id=1, source_target_pairs={{0,8},{8,0},{1,9},{9,1},{2,10},{10,2},{3,11},{11,3},{16,24},{24,16... | collective-permute-start | bytes 589832 | tf_op jit(solution)/shard_map/ppermute | solution.py:46
  (10 other events, 10.6 us)

commit v3 on v2

--- a/solution.py
+++ b/solution.py
@@ -98,7 +98,7 @@
     out_ref = refs[-1]
     groups, tokens, _ = in_ref.shape
     length = groups * tokens
-    blocks = 4
+    blocks = 8
     rows = blocks * tokens
     scale = HD**-0.5
 
@@ -141,12 +141,12 @@
     )(packed, *(() if earlier is None else (earlier,)))
 
 
-def prepare_body(n, info_ref, gate_hbm, gate_dot_hbm, *rest):
+def prepare_body(n, times_ref, info_ref, gate_hbm, gate_dot_hbm, *rest):
     weights = rest[:n]
     gates_ref, w_ref, wide, sem, w_sem = rest[n:]
     copies, at = [], 0
     for who in range(2):
-        row = pl.multiple_of(info_ref[who] // 8 * 8, 8)
+        row = pl.multiple_of(times_ref[who] // 8 * 8, 8)
         for t, table in enumerate((gate_hbm, gate_dot_hbm)):
             copies.append(pltpu.make_async_copy(table.at[pl.ds(row, 8), :], wide.at[who, t], sem.at[who, t]))
     for i, weight in enumerate(weights):
@@ -158,11 +158,18 @@
     for c in copies:
         c.wait()
     for who in range(2):
+        row = times_ref[who] % 8
         for t in range(2):
-            gates_ref[2 * who + t : 2 * who + t + 1] = wide[who, t, pl.ds(info_ref[who] % 8, 1), :]
-
-
-def prepare(times, gate_table, gate_dot_table, weights):
+            parts = []
+            for i in range(gates_ref.shape[1] // PIECE):
+                column = info_ref[i] * PIECE
+                base = pl.multiple_of(column // HD * HD, HD)
+                line = wide[who, t, pl.ds(row, 1), pl.ds(base, 3 * HD)]
+                parts.append(jnp.where(column % HD != 0, line[:, HD // 2 : HD // 2 + PIECE], line[:, :PIECE]))
+            gates_ref[2 * who + t : 2 * who + t + 1] = jnp.concatenate(parts, axis=1)
+
+
+def prepare(times, info, gate_table, gate_dot_table, weights):
     width = gate_table.shape[1]
     n = len(weights)
     total = sum(a.shape[0] for a in weights)
@@ -170,10 +177,10 @@
     vmem = pl.BlockSpec(memory_space=pltpu.VMEM)
     return pl.pallas_call(
         functools.partial(prepare_body, n),
-        in_specs=[pl.BlockSpec(memory_space=pltpu.SMEM)] + [anywhere] * (2 + n),
+        in_specs=[pl.BlockSpec(memory_space=pltpu.SMEM)] * 2 + [anywhere] * (2 + n),
         out_specs=[vmem, vmem],
         out_shape=[
-            jax.ShapeDtypeStruct((4, width), F32),
+            jax.ShapeDtypeStruct((4, 8 * PIECE), F32),
             jax.ShapeDtypeStruct((total, weights[0].shape[1]), BF16),
         ],
         scratch_shapes=[
@@ -181,17 +188,17 @@
             pltpu.SemaphoreType.DMA((2, 2)),
             pltpu.SemaphoreType.DMA((n,)),
         ],
-        compiler_params=pltpu.CompilerParams(vmem_limit_bytes=36 * MIB),
+        compiler_params=pltpu.CompilerParams(vmem_limit_bytes=VMEM_ALL),
         cost_estimate=NO_COST,
         name="prepare",
-    )(times, gate_table, gate_dot_table, *weights)
+    )(times, info, gate_table, gate_dot_table, *weights)
 
 
 def round_up(n, unit):
     return -(-n // unit) * unit
 
 
-def project_body(n, first, ready_rows, info_ref, gates_ref, own_ref, peer_ref, *rest):
+def project_body(n, first, ready_rows, plan, gates_ref, own_ref, peer_ref, *rest):
     ready = rest[0] if ready_rows else None
     rest = rest[1:] if ready_rows else rest
     weights = rest[:n]
@@ -200,21 +207,12 @@
     heads = own_ref.shape[2] // (2 * HD)
 
     at, w_copies = 0, []
-    for i, weight in enumerate(weights):
-        rows = weight.shape[0]
-        w_copies.append(pltpu.make_async_copy(weight, w.at[pl.ds(at, rows), :], w_sem.at[i]))
+    for i, (which, start, rows) in enumerate(plan):
+        piece = weights[which].at[pl.ds(start, rows), :]
+        w_copies.append(pltpu.make_async_copy(piece, w.at[pl.ds(at, rows), :], w_sem.at[i]))
         at += rows
     for c in w_copies:
         c.start()
-
-    def gate_rows(line, begin, end):
-        parts = []
-        for i in range(begin // PIECE, end // PIECE):
-            column = info_ref[first + i] * PIECE
-            base = pl.multiple_of(column // HD * HD, HD)
-            wide = gates_ref[line : line + 1, pl.ds(base, 3 * HD)]
-            parts.append(jnp.where(column % HD != 0, wide[:, HD // 2 : HD // 2 + PIECE], wide[:, :PIECE]))
-        return jnp.concatenate(parts, axis=1)
 
     for who, ref in enumerate((own_ref, peer_ref)):
         for g in range(groups):
@@ -229,7 +227,8 @@
         end = begin + weight_ref.shape[0]
         y = lax.dot_general(x[...], weight_ref[...], NT, preferred_element_type=F32)
         for who, ref in enumerate((mine_ref, send_ref)):
-            gate, gate_dot = (gate_rows(2 * who + t, begin, end) for t in range(2))
+            lines = slice(first * PIECE + begin, first * PIECE + end)
+            gate, gate_dot = (gates_ref[2 * who + t : 2 * who + t + 1, lines] for t in range(2))
             primal = y[2 * who * tokens : (2 * who + 1) * tokens]
             tangent = y[(2 * who + 1) * tokens : (2 * who + 2) * tokens]
             ref[0, :, begin:end] = (gate * primal).astype(BF16)
@@ -242,29 +241,30 @@
     part(w, ready_rows)
 
 
-def project(info, first, own, peer, gates, ready, weights):
+def project(first, own, peer, gates, ready, weights, plan=None):
     groups, tokens, _ = own.shape
     n = len(weights)
-    rows = sum(a.shape[0] for a in weights)
+    plan = plan or [(i, 0, a.shape[0]) for i, a in enumerate(weights)]
+    rows = sum(count for _, _, count in plan)
     ready_rows = 0 if ready is None else ready.shape[0]
     depth = weights[0].shape[1]
     hbm = pl.BlockSpec(memory_space=pltpu.HBM)
     vmem = pl.BlockSpec(memory_space=pltpu.VMEM)
     half = jax.ShapeDtypeStruct((2, tokens, round_up(ready_rows + rows, HD)), BF16)
     return pl.pallas_call(
-        functools.partial(project_body, n, first, ready_rows),
-        in_specs=[pl.BlockSpec(memory_space=pltpu.SMEM)] + [vmem] * (3 if ready is None else 4) + [hbm] * n,
+        functools.partial(project_body, n, first, ready_rows, plan),
+        in_specs=[vmem] * (3 if ready is None else 4) + [hbm] * n,
         out_specs=[vmem, vmem],
         out_shape=[half, half],
         scratch_shapes=[
             pltpu.VMEM((4 * tokens, depth), BF16),
             pltpu.VMEM((rows, depth), BF16),
-            pltpu.SemaphoreType.DMA((n,)),
+            pltpu.SemaphoreType.DMA((len(plan),)),
         ],
         compiler_params=pltpu.CompilerParams(vmem_limit_bytes=36 * MIB),
         cost_estimate=NO_COST,
         name="project",
-    )(info, gates, own, peer, *(() if ready is None else (ready,)), *weights)
+    )(gates, own, peer, *(() if ready is None else (ready,)), *weights)
 
 
 def merge_body(spots, info_ref, *refs):
@@ -349,24 +349,37 @@
     b2 = move(w2, down)
     c1 = move(a1, up)
     c2 = move(b2, down)
-    near_a = move(near, up)
-    near_b = move(near, down)
+    quarter = half // 2
+    near_a1 = move(near[:quarter], up)
+    near_a2 = move(near[quarter:], up)
+    near_b1 = move(near[quarter:half], down)
+    near_b2 = move(jnp.concatenate([near[:quarter], near[half:]]), down)
     received, a2, b2, c1, c2 = lax.optimization_barrier((received, a2, b2, c1, c2))
 
     attn = attend(received, 0, 3)
     own = exchange(attn)
-    gates, here = prepare(times, gate_table, gate_dot_table, (weight, a1, a2, b1, b2, c1, c2))
-    own, near_a, near_b, gates, here, c2 = lax.optimization_barrier((own, near_a, near_b, gates, here, c2))
+    gates, here = prepare(times, info, gate_table, gate_dot_table, (weight, a1, a2, b1, b2, c1, c2))
+    own, near_a1, near_a2, near_b1, near_b2, gates, here, c2 = lax.optimization_barrier(
+        (own, near_a1, near_a2, near_b1, near_b2, gates, here, c2)
+    )
 
     peer = move(own, swap)
-    near_c1 = move(near_a[: half // 2], up)
-    near_c2 = move(near_b[half // 2 : half], down)
+    near_c1 = move(near_a1, up)
+    near_c2 = move(near_b1, down)
     near_c3 = move(c2, beside())
 
-    mine_a, sent_a = project(info, 0, own, peer, gates, here, (near, near_a, near_b))
+    mine_a, sent_a = project(
+        0,
+        own,
+        peer,
+        gates,
+        here,
+        (near, near_a1, near_a2, near_b1, near_b2),
+        [(0, 0, PIECE), (1, 0, quarter), (2, 0, PIECE - quarter), (4, 0, quarter), (3, 0, quarter), (4, quarter, half)],
+    )
     mine_a, sent_a, near_c1, near_c2, near_c3 = lax.optimization_barrier((mine_a, sent_a, near_c1, near_c2, near_c3))
     got_a = move(sent_a, swap)
-    mine_b, sent_b = project(info, 7, own, peer, gates, None, (near_c1, near_c2, near_c3))
+    mine_b, sent_b = project(7, own, peer, gates, None, (near_c1, near_c2, near_c3))
     got_b = move(sent_b, swap)
     spots = [(0, i) for i in range(7)] + [(1, 0)]
     return tuple(merge(info, spots, (mine_a, mine_b), (got_a, got_b), gate_table.shape[1]))

time: 157 us -> 155 us (0.987)
  local copies, waits for them, and re-layouts: 20.7 us -> 9.11 us
  waiting for transfers between devices: 62.8 us -> 66.2 us
  Pallas kernels: 39 us -> 42.3 us
  starting transfers between devices: 31.2 us -> 33.3 us
  other arithmetic: 0.7 us -> 2.56 us
    unnamed x32 -> x16, local copies, waits for them, and re-layouts: 16.2 us -> 3.75 us
    ppermute x16 -> x18, waiting for transfers between devices: 54.1 us -> 59.3 us  [move(): return lax.ppermute(a, ('fsdp', 'seq'), perm)]
    pallas_call x1, Pallas kernels: 3.63 us -> 7.3 us  [prepare(): pl.pallas_call(functools.partial(prepare_body, n), in_specs=[pl.BlockSpec...]
    ppermute x16 -> x18, starting transfers between devices: 21.7 us -> 23.8 us  [move(): return lax.ppermute(a, ('fsdp', 'seq'), perm)]
    all_to_all x2, waiting for transfers between devices: 8.68 us -> 6.99 us  [exchange(): return lax.all_to_all(a, 'seq', split_axis=0, concat_axis=0, tiled=True)]
  transfers between devices with their start and end apart: 18 -> 20, of which waited for: 7 -> 8; matrix products, arithmetic and copies ran while one was open for 3% -> 5% of each run, Pallas kernels for 23% -> 26%
where the time goes in v3:
time: 155 us
  waiting for transfers between devices  66.2 us (43%)
  Pallas kernels  42.3 us (27%)
  starting transfers between devices  33.3 us (21%)
  local copies, waits for them, and re-layouts  9.11 us (6%)
  other arithmetic  2.56 us (2%)
    ppermute x18, waiting for transfers between devices, move(): return lax.ppermute(a, ('fsdp', 'seq'), perm)  59.3 us
    ppermute x18, starting transfers between devices, move(): return lax.ppermute(a, ('fsdp', 'seq'), perm)  23.8 us
    pallas_call x2, Pallas kernels, project(): pl.pallas_call(functools.partial(project_body, n, first, ready_rows, plan...  15.5 us
    pallas_call x1, Pallas kernels, attend(): pl.pallas_call(attn_body, grid=(width // (6 * HD),), in_specs=[pl.BlockSp...  11 us
    all_to_all x2, starting transfers between devices, exchange(): return lax.all_to_all(a, 'seq', split_axis=0, concat_axis=0, tiled=True)  9.5 us
    pallas_call x1, Pallas kernels, prepare(): pl.pallas_call(functools.partial(prepare_body, n), in_specs=[pl.BlockSpec...  7.3 us
    all_to_all x2, waiting for transfers between devices, exchange(): return lax.all_to_all(a, 'seq', split_axis=0, concat_axis=0, tiled=True)  6.99 us
    pallas_call x1, Pallas kernels, norm_pack(): pl.pallas_call(norm_body, grid=(tokens // rows,), in_specs=[wide] * 6 + [...  5.86 us
  transfers between devices with their start and end apart: 20, of which 8 were waited for; matrix products, arithmetic and copies ran while one was open for 5% of the time, Pallas kernels for 26%

profile of v3, /device:TPU:1, one launch (start us, length us, event | category | flops | bytes accessed | tf_op | source)
XLA Modules:
  0.0 154.9 jit_solution(9017157481515616257)
XLA Ops:
  0.6 3.4 %collective-permute-start = (bf16[320,3072]{1,0:T(8,128)(2,1)}, bf16[320,3072]{1,0:T(8,128)(2,1)S(1)}, u32[]{:S(2)}, u32[]{:S(2)}) collective-permute-start(bf16[320,3072]{1,0:T(8,128)(2,1)} %bitcast.20), channel_id=1, source_target_pairs={{0,16},{8,28},{1,17},{9,29},{2,18},{10,30},{3,19},{11,31},{16,4},{... | collective-permute-start | bytes 5898248 | tf_op jit(solution)/shard_map/ppermute | solution.py:46
  5.3 1.4 collective-permute-start.1
  6.7 1.5 collective-permute-start.2
  9.0 5.9 %norm_pack.1 = bf16[8,128,2304]{2,1,0:T(8,128)(2,1)} custom-call(bf16[128,3072]{1,0:T(8,128)(2,1)} %q_ref.1, bf16[128,3072]{1,0:T(8,128)(2,1)} %qd_ref.1, bf16[128,3072]{1,0:T(8,128)(2,1)} %k_ref.1, bf16[128,3072]{1,0:T(8,128)(2,1)} %kd_ref.1, bf16[128,3072]{1,0:T(8,128)(2,1)} %v_ref.1, bf16[128,3072]{1,0:T(8,128)(2,1)} %vd_ref.1, f32[1,3072]{1,0:T(1,128)} %bitcast.24, ...), custom_call_target="tpu_custom_call" | custom-call | tf_op jit(solution)/shard_map/norm_pack/pallas_call | solution.py:81
  16.8 13.7 %collective-permute-done.1.rest_1_ = bf16[160,3072]{1,0:T(8,128)(2,1)} collective-permute-done((bf16[160,3072]{1,0:T(8,128)(2,1)S(1)}, bf16[160,3072]{1,0:T(8,128)(2,1)}, u32[]{:S(2)}, u32[]{:S(2)}) %collective-permute-start.1) | collective-permute-done | bytes 983072 | tf_op jit(solution)/shard_map/ppermute | solution.py:46
  30.5 5.0 %all-to-all-start = ((bf16[8,128,2304]{2,1,0:T(8,128)(2,1)}), bf16[8,128,2304]{2,1,0:T(8,128)(2,1)}, u32[]{:S(2)}, u32[]{:S(2)}) async-start(bf16[8,128,2304]{2,1,0:T(8,128)(2,1)} %norm_pack.1), calls=%async_computation | async-start | bytes 9437184 | tf_op jit(solution)/shard_map/all_to_all | solution.py:323
  36.8 2.6 %collective-permute-start.5 = (bf16[160,3072]{1,0:T(8,128)(2,1)S(1)}, bf16[160,3072]{1,0:T(8,128)(2,1)S(1)}, u32[]{:S(2)}, u32[]{:S(2)}) collective-permute-start(bf16[160,3072]{1,0:T(8,128)(2,1)S(1)} %slice.20), channel_id=1, source_target_pairs={{0,96},{8,104},{1,97},{9,105},{2,98},{10,106},{3,99},{11,107},{16,... | collective-permute-start | bytes 2949128 | tf_op jit(solution)/shard_map/ppermute | solution.py:46
  40.7 18.5 %collective-permute-done.5.rest_4_ = bf16[160,3072]{1,0:T(8,128)(2,1)S(1)} collective-permute-done((bf16[160,3072]{1,0:T(8,128)(2,1)S(1)}, bf16[160,3072]{1,0:T(8,128)(2,1)S(1)}, u32[]{:S(2)}, u32[]{:S(2)}) %collective-permute-start.5) | collective-permute-done | bytes 983072 | tf_op jit(solution)/shard_map/ppermute | solution.py:46
  59.2 3.5 %collective-permute-start.7 = (bf16[160,3072]{1,0:T(8,128)(2,1)S(1)}, bf16[160,3072]{1,0:T(8,128)(2,1)}, u32[]{:S(2)}, u32[]{:S(2)}) collective-permute-start(bf16[160,3072]{1,0:T(8,128)(2,1)S(1)} %collective-permute-done.5.rest_4_), channel_id=1, source_target_pairs={{0,96},{8,104},{1,97},{9,105},{2,98},{10,106},{3,99},{11,107},{16,... | collective-permute-start | bytes 2949128 | tf_op jit(solution)/shard_map/ppermute | solution.py:46
  65.0 1.4 collective-permute-start.9
  67.3 16.2 %collective-permute-done.6.rest_5_ = bf16[160,3072]{1,0:T(8,128)(2,1)S(1)} collective-permute-done((bf16[160,3072]{1,0:T(8,128)(2,1)}, bf16[160,3072]{1,0:T(8,128)(2,1)S(1)}, u32[]{:S(2)}, u32[]{:S(2)}) %collective-permute-start.6) | collective-permute-done | bytes 983072 | tf_op jit(solution)/shard_map/ppermute | solution.py:46
  84.5 6.1 %all-to-all-done.in_ref = bf16[8,128,2304]{2,1,0:T(8,128)(2,1)} async-done(((bf16[8,128,2304]{2,1,0:T(8,128)(2,1)}), bf16[8,128,2304]{2,1,0:T(8,128)(2,1)}, u32[]{:S(2)}, u32[]{:S(2)}) %all-to-all-start) | async-done | bytes 4718624 | tf_op jit(solution)/shard_map/all_to_all | solution.py:323
  90.6 11.0 %attend.1 = bf16[8,128,768]{2,1,0:T(8,128)(2,1)} custom-call(bf16[8,128,2304]{2,1,0:T(8,128)(2,1)} %all-to-all-done.in_ref), custom_call_target="tpu_custom_call" | custom-call | tf_op jit(solution)/shard_map/attend/pallas_call | solution.py:130
  101.6 4.5 %all-to-all-start.1 = ((bf16[8,128,768]{2,1,0:T(8,128)(2,1)}), bf16[8,128,768]{2,1,0:T(8,128)(2,1)S(1)}, u32[]{:S(2)}, u32[]{:S(2)}) async-start(bf16[8,128,768]{2,1,0:T(8,128)(2,1)} %attend.1), calls=%async_computation.1 | async-start | bytes 3145728 | tf_op jit(solution)/shard_map/all_to_all | solution.py:323
  106.1 2.5 %collective-permute-start.10 = (bf16[80,3072]{1,0:T(8,128)(2,1)}, bf16[80,3072]{1,0:T(8,128)(2,1)S(1)}, u32[]{:S(2)}, u32[]{:S(2)}) collective-permute-start(bf16[80,3072]{1,0:T(8,128)(2,1)} %get-tuple-element.64), channel_id=1, source_target_pairs={{0,96},{8,104},{1,97},{9,105},{2,98},{10,106},{3,99},{11,107},{16,... | collective-permute-start | bytes 1474568 | tf_op jit(solution)/shard_map/ppermute | solution.py:46
  108.6 7.3 %prepare.1 = (f32[4,2560]{1,0:T(4,128)}, bf16[1280,3072]{1,0:T(8,128)(2,1)}) custom-call(s32[2]{0:T(128)} %pad_add_fusion.times_ref, s32[17]{0:T(128)} %stack.71.info_ref, f32[64,5120]{1,0:T(8,128)} %gate_hbm.1, f32[64,5120]{1,0:T(8,128)} %gate_dot_hbm.1, bf16[320,3072]{1,0:T(8,128)(2,1)} %bitcast.23, bf16[160,3072]{1,0:T(8,128)(2,1)} %collective-permute-done.1.rest_1_, ...), custom_call_target="tpu_custom_call" | custom-call | tf_op jit(solution)/shard_map/prepare/pallas_call | solution.py:178
  115.9 8.1 %collective-permute-done.10.rest_4_ = bf16[80,3072]{1,0:T(8,128)(2,1)S(1)} collective-permute-done((bf16[80,3072]{1,0:T(8,128)(2,1)}, bf16[80,3072]{1,0:T(8,128)(2,1)S(1)}, u32[]{:S(2)}, u32[]{:S(2)}) %collective-permute-start.10) | collective-permute-done | bytes 491552 | tf_op jit(solution)/shard_map/ppermute | solution.py:46
  124.0 1.6 %collective-permute-done.8.rest_2_ = bf16[80,3072]{1,0:T(8,128)(2,1)} collective-permute-done((bf16[80,3072]{1,0:T(8,128)(2,1)}, bf16[80,3072]{1,0:T(8,128)(2,1)}, u32[]{:S(2)}, u32[]{:S(2)}) %collective-permute-start.8) | collective-permute-done | bytes 491552 | tf_op jit(solution)/shard_map/ppermute | solution.py:46
  126.5 1.6 %collective-permute-start.12 = (bf16[8,128,768]{2,1,0:T(8,128)(2,1)S(1)}, bf16[8,128,768]{2,1,0:T(8,128)(2,1)S(1)}, u32[]{:S(2)}, u32[]{:S(2)}) collective-permute-start(bf16[8,128,768]{2,1,0:T(8,128)(2,1)S(1)} %all-to-all-done.1.own_ref), channel_id=1, source_target_pairs={{0,8},{8,0},{1,9},{9,1},{2,10},{10,2},{3,11},{11,3},{16,24},{24,16... | collective-permute-start | bytes 4718600 | tf_op jit(solution)/shard_map/ppermute | solution.py:46
  128.2 2.3 %collective-permute-start.15 = (bf16[160,3072]{1,0:T(8,128)(2,1)}, bf16[160,3072]{1,0:T(8,128)(2,1)S(1)}, u32[]{:S(2)}, u32[]{:S(2)}) collective-permute-start(bf16[160,3072]{1,0:T(8,128)(2,1)} %collective-permute-done.7.rest_6_), channel_id=1, source_target_pairs={{0,16},{8,28},{1,17},{9,29},{2,18},{10,30},{3,19},{11,31},{16,4},{... | collective-permute-start | bytes 2949128 | tf_op jit(solution)/shard_map/ppermute | solution.py:46
  130.4 2.7 %collective-permute-start.14 = (bf16[80,3072]{1,0:T(8,128)(2,1)}, bf16[80,3072]{1,0:T(8,128)(2,1)S(1)}, u32[]{:S(2)}, u32[]{:S(2)}) collective-permute-start(bf16[80,3072]{1,0:T(8,128)(2,1)} %copy-done), channel_id=1, source_target_pairs={{0,96},{8,104},{1,97},{9,105},{2,98},{10,106},{3,99},{11,107},{16,... | collective-permute-start | bytes 1474568 | tf_op jit(solution)/shard_map/ppermute | solution.py:46
  135.0 11.6 %project.2 = (bf16[2,128,2304]{2,1,0:T(8,128)(2,1)S(1)}, bf16[2,128,2304]{2,1,0:T(8,128)(2,1)S(1)}) custom-call(f32[4,2560]{1,0:T(4,128)S(1)} %copy-done.2, bf16[8,128,768]{2,1,0:T(8,128)(2,1)S(1)} %all-to-all-done.1.own_ref, bf16[8,128,768]{2,1,0:T(8,128)(2,1)S(1)} %collective-permute-done.12.peer_ref, bf16[1280,3072]{1,0:T(8,128)(2,1)} %get-tuple-element.49.rest_0_, ...), custom_call_target="tpu_custom_call" | custom-call | tf_op jit(solution)/shard_map/project/pallas_call | solution.py:254
  146.7 3.9 %project.3 = (bf16[2,128,384]{2,1,0:T(8,128)(2,1)S(1)}, bf16[2,128,384]{2,1,0:T(8,128)(2,1)S(1)}) custom-call(f32[4,2560]{1,0:T(4,128)S(1)} %copy-done.2, bf16[8,128,768]{2,1,0:T(8,128)(2,1)S(1)} %all-to-all-done.1.own_ref, bf16[8,128,768]{2,1,0:T(8,128)(2,1)S(1)} %collective-permute-done.12.peer_ref, bf16[80,3072]{1,0:T(8,128)(2,1)S(1)} %collective-permute-done.13.rest_0_, ...), custom_call_target="tpu_custom_call" | custom-call | tf_op jit(solution)/shard_map/project/pallas_call | solution.py:254
  152.3 2.6 %merge.1 = (bf16[128,5120]{1,0:T(8,128)(2,1)}, bf16[128,5120]{1,0:T(8,128)(2,1)}) custom-call(s32[17]{0:T(128)S(1)} %copy-done.3, bf16[2,128,2304]{2,1,0:T(8,128)(2,1)S(1)} %get-tuple-element.57.refs_0_, bf16[2,128,384]{2,1,0:T(8,128)(2,1)S(1)} %get-tuple-element.61.refs_1_, bf16[2,128,2304]{2,1,0:T(8,128)(2,1)S(1)} %collective-permute-done.16.refs_2_, ...), custom_call_target="tpu_custom_call" | custom-call | tf_op jit(solution)/shard_map/merge/pallas_call | solution.py:290
  (46 shorter events, 14.5 us)
Async XLA Ops:
  0.6 29.8 %collective-permute-start = (bf16[320,3072]{1,0:T(8,128)(2,1)}, bf16[320,3072]{1,0:T(8,128)(2,1)S(1)}, u32[]{:S(2)}, u32[]{:S(2)}) collective-permute-start(bf16[320,3072]{1,0:T(8,128)(2,1)} %bitcast.20), channel_id=1, source_target_pairs={{0,16},{8,28},{1,17},{9,29},{2,18},{10,30},{3,19},{11,31},{16,4},{... | collective-permute-start | bytes 5898248 | tf_op jit(solution)/shard_map/ppermute | solution.py:46
  5.3 25.1 %collective-permute-start.1 = (bf16[160,3072]{1,0:T(8,128)(2,1)S(1)}, bf16[160,3072]{1,0:T(8,128)(2,1)}, u32[]{:S(2)}, u32[]{:S(2)}) collective-permute-start(bf16[160,3072]{1,0:T(8,128)(2,1)S(1)} %slice.25), channel_id=1, source_target_pairs={{0,32},{8,40},{1,33},{9,41},{2,34},{10,42},{3,35},{11,43},{16,48},... | collective-permute-start | bytes 2949128 | tf_op jit(solution)/shard_map/ppermute | solution.py:46
  6.7 23.8 %collective-permute-start.2 = (bf16[160,3072]{1,0:T(8,128)(2,1)S(1)}, bf16[160,3072]{1,0:T(8,128)(2,1)}, u32[]{:S(2)}, u32[]{:S(2)}) collective-permute-start(bf16[160,3072]{1,0:T(8,128)(2,1)S(1)} %slice.25), channel_id=1, source_target_pairs={{0,96},{8,104},{1,97},{9,105},{2,98},{10,106},{3,99},{11,107},{16,... | collective-permute-start | bytes 2949128 | tf_op jit(solution)/shard_map/ppermute | solution.py:46
  8.2 7.3 %collective-permute-start.3 = (s32[1]{0:T(128)}, s32[1]{0:T(128)}, u32[]{:S(2)}, u32[]{:S(2)}) collective-permute-start(s32[1]{0:T(128)} %param.23), channel_id=1, source_target_pairs={{0,8},{8,0},{1,9},{9,1},{2,10},{10,2},{3,11},{11,3},{16,24},{24,16... | collective-permute-start | bytes 20 | tf_op jit(solution)/shard_map/ppermute | solution.py:46
  30.5 60.1 %all-to-all-start = ((bf16[8,128,2304]{2,1,0:T(8,128)(2,1)}), bf16[8,128,2304]{2,1,0:T(8,128)(2,1)}, u32[]{:S(2)}, u32[]{:S(2)}) async-start(bf16[8,128,2304]{2,1,0:T(8,128)(2,1)} %norm_pack.1), calls=%async_computation | async-start | bytes 9437184 | tf_op jit(solution)/shard_map/all_to_all | solution.py:323
  36.8 22.5 %collective-permute-start.5 = (bf16[160,3072]{1,0:T(8,128)(2,1)S(1)}, bf16[160,3072]{1,0:T(8,128)(2,1)S(1)}, u32[]{:S(2)}, u32[]{:S(2)}) collective-permute-start(bf16[160,3072]{1,0:T(8,128)(2,1)S(1)} %slice.20), channel_id=1, source_target_pairs={{0,96},{8,104},{1,97},{9,105},{2,98},{10,106},{3,99},{11,107},{16,... | collective-permute-start | bytes 2949128 | tf_op jit(solution)/shard_map/ppermute | solution.py:46
  39.4 27.0 %collective-permute-start.4 = (bf16[160,3072]{1,0:T(8,128)(2,1)S(1)}, bf16[160,3072]{1,0:T(8,128)(2,1)S(1)}, u32[]{:S(2)}, u32[]{:S(2)}) collective-permute-start(bf16[160,3072]{1,0:T(8,128)(2,1)S(1)} %slice.20), channel_id=1, source_target_pairs={{0,32},{8,40},{1,33},{9,41},{2,34},{10,42},{3,35},{11,43},{16,48},... | collective-permute-start | bytes 2949128 | tf_op jit(solution)/shard_map/ppermute | solution.py:46
  40.7 42.8 %collective-permute-start.6 = (bf16[160,3072]{1,0:T(8,128)(2,1)}, bf16[160,3072]{1,0:T(8,128)(2,1)S(1)}, u32[]{:S(2)}, u32[]{:S(2)}) collective-permute-start(bf16[160,3072]{1,0:T(8,128)(2,1)} %collective-permute-done.1.rest_1_), channel_id=1, source_target_pairs={{0,32},{8,40},{1,33},{9,41},{2,34},{10,42},{3,35},{11,43},{16,48},... | collective-permute-start | bytes 2949128 | tf_op jit(solution)/shard_map/ppermute | solution.py:46
  59.2 5.6 %copy-start.5 = (bf16[160,3072]{1,0:T(8,128)(2,1)}, bf16[160,3072]{1,0:T(8,128)(2,1)S(1)}, u32[]{:S(2)}) copy-start(bf16[160,3072]{1,0:T(8,128)(2,1)S(1)} %collective-permute-done.5.rest_4_) | copy-start | bytes 2949124
  59.2 25.2 %collective-permute-start.7 = (bf16[160,3072]{1,0:T(8,128)(2,1)S(1)}, bf16[160,3072]{1,0:T(8,128)(2,1)}, u32[]{:S(2)}, u32[]{:S(2)}) collective-permute-start(bf16[160,3072]{1,0:T(8,128)(2,1)S(1)} %collective-permute-done.5.rest_4_), channel_id=1, source_target_pairs={{0,96},{8,104},{1,97},{9,105},{2,98},{10,106},{3,99},{11,107},{16,... | collective-permute-start | bytes 2949128 | tf_op jit(solution)/shard_map/ppermute | solution.py:46
  63.6 1.3 copy-start.4
  64.9 60.8 %collective-permute-start.11 = (bf16[240,3072]{1,0:T(8,128)(2,1)}, bf16[240,3072]{1,0:T(8,128)(2,1)}, u32[]{:S(2)}, u32[]{:S(2)}) collective-permute-start(bf16[240,3072]{1,0:T(8,128)(2,1)} %pad_maximum_fusion), channel_id=1, source_target_pairs={{0,96},{8,104},{1,97},{9,105},{2,98},{10,106},{3,99},{11,107},{16,... | collective-permute-start | bytes 4423688 | tf_op jit(solution)/shard_map/ppermute | solution.py:46
  65.0 60.7 %collective-permute-start.9 = (bf16[240,3072]{1,0:T(8,128)(2,1)}, bf16[240,3072]{1,0:T(8,128)(2,1)}, u32[]{:S(2)}, u32[]{:S(2)}) collective-permute-start(bf16[240,3072]{1,0:T(8,128)(2,1)} %slice.22), channel_id=1, source_target_pairs={{0,32},{8,40},{1,33},{9,41},{2,34},{10,42},{3,35},{11,43},{16,48},... | collective-permute-start | bytes 4423688 | tf_op jit(solution)/shard_map/ppermute | solution.py:46
  101.6 24.9 %all-to-all-start.1 = ((bf16[8,128,768]{2,1,0:T(8,128)(2,1)}), bf16[8,128,768]{2,1,0:T(8,128)(2,1)S(1)}, u32[]{:S(2)}, u32[]{:S(2)}) async-start(bf16[8,128,768]{2,1,0:T(8,128)(2,1)} %attend.1), calls=%async_computation.1 | async-start | bytes 3145728 | tf_op jit(solution)/shard_map/all_to_all | solution.py:323
  106.1 17.9 %collective-permute-start.10 = (bf16[80,3072]{1,0:T(8,128)(2,1)}, bf16[80,3072]{1,0:T(8,128)(2,1)S(1)}, u32[]{:S(2)}, u32[]{:S(2)}) collective-permute-start(bf16[80,3072]{1,0:T(8,128)(2,1)} %get-tuple-element.64), channel_id=1, source_target_pairs={{0,96},{8,104},{1,97},{9,105},{2,98},{10,106},{3,99},{11,107},{16,... | collective-permute-start | bytes 1474568 | tf_op jit(solution)/shard_map/ppermute | solution.py:46
  108.6 17.0 %collective-permute-start.8 = (bf16[80,3072]{1,0:T(8,128)(2,1)}, bf16[80,3072]{1,0:T(8,128)(2,1)}, u32[]{:S(2)}, u32[]{:S(2)}) collective-permute-start(bf16[80,3072]{1,0:T(8,128)(2,1)} %copy-done.4), channel_id=1, source_target_pairs={{0,32},{8,40},{1,33},{9,41},{2,34},{10,42},{3,35},{11,43},{16,48},... | collective-permute-start | bytes 1474568 | tf_op jit(solution)/shard_map/ppermute | solution.py:46
  124.0 1.6 %copy-start = (bf16[80,3072]{1,0:T(8,128)(2,1)}, bf16[80,3072]{1,0:T(8,128)(2,1)S(1)}, u32[]{:S(2)}) copy-start(bf16[80,3072]{1,0:T(8,128)(2,1)S(1)} %collective-permute-done.10.rest_4_) | copy-start | bytes 1474564
  126.5 6.6 %collective-permute-start.12 = (bf16[8,128,768]{2,1,0:T(8,128)(2,1)S(1)}, bf16[8,128,768]{2,1,0:T(8,128)(2,1)S(1)}, u32[]{:S(2)}, u32[]{:S(2)}) collective-permute-start(bf16[8,128,768]{2,1,0:T(8,128)(2,1)S(1)} %all-to-all-done.1.own_ref), channel_id=1, source_target_pairs={{0,8},{8,0},{1,9},{9,1},{2,10},{10,2},{3,11},{11,3},{16,24},{24,16... | collective-permute-start | bytes 4718600 | tf_op jit(solution)/shard_map/ppermute | solution.py:46
  128.2 18.5 %collective-permute-start.15 = (bf16[160,3072]{1,0:T(8,128)(2,1)}, bf16[160,3072]{1,0:T(8,128)(2,1)S(1)}, u32[]{:S(2)}, u32[]{:S(2)}) collective-permute-start(bf16[160,3072]{1,0:T(8,128)(2,1)} %collective-permute-done.7.rest_6_), channel_id=1, source_target_pairs={{0,16},{8,28},{1,17},{9,29},{2,18},{10,30},{3,19},{11,31},{16,4},{... | collective-permute-start | bytes 2949128 | tf_op jit(solution)/shard_map/ppermute | solution.py:46
  130.4 16.2 %collective-permute-start.13 = (bf16[80,3072]{1,0:T(8,128)(2,1)}, bf16[80,3072]{1,0:T(8,128)(2,1)S(1)}, u32[]{:S(2)}, u32[]{:S(2)}) collective-permute-start(bf16[80,3072]{1,0:T(8,128)(2,1)} %collective-permute-done.8.rest_2_), channel_id=1, source_target_pairs={{0,32},{8,40},{1,33},{9,41},{2,34},{10,42},{3,35},{11,43},{16,48},... | collective-permute-start | bytes 1474568 | tf_op jit(solution)/shard_map/ppermute | solution.py:46
  130.4 16.2 %collective-permute-start.14 = (bf16[80,3072]{1,0:T(8,128)(2,1)}, bf16[80,3072]{1,0:T(8,128)(2,1)S(1)}, u32[]{:S(2)}, u32[]{:S(2)}) collective-permute-start(bf16[80,3072]{1,0:T(8,128)(2,1)} %copy-done), channel_id=1, source_target_pairs={{0,96},{8,104},{1,97},{9,105},{2,98},{10,106},{3,99},{11,107},{16,... | collective-permute-start | bytes 1474568 | tf_op jit(solution)/shard_map/ppermute | solution.py:46
  146.6 5.7 %copy-start.3 = (s32[17]{0:T(128)S(1)}, s32[17]{0:T(128)}, u32[]{:S(2)}) copy-start(s32[17]{0:T(128)} %stack.71.info_ref) | copy-start | bytes 208
  146.6 5.6 %collective-permute-start.16 = (bf16[2,128,2304]{2,1,0:T(8,128)(2,1)S(1)}, bf16[2,128,2304]{2,1,0:T(8,128)(2,1)S(1)}, u32[]{:S(2)}, u32[]{:S(2)}) collective-permute-start(bf16[2,128,2304]{2,1,0:T(8,128)(2,1)S(1)} %get-tuple-element.62), channel_id=1, source_target_pairs={{0,8},{8,0},{1,9},{9,1},{2,10},{10,2},{3,11},{11,3},{16,24},{24,16... | collective-permute-start | bytes 3538952 | tf_op jit(solution)/shard_map/ppermute | solution.py:46
  150.6 1.6 %collective-permute-start.17 = (bf16[2,128,384]{2,1,0:T(8,128)(2,1)S(1)}, bf16[2,128,384]{2,1,0:T(8,128)(2,1)S(1)}, u32[]{:S(2)}, u32[]{:S(2)}) collective-permute-start(bf16[2,128,384]{2,1,0:T(8,128)(2,1)S(1)} %get-tuple-element.63), channel_id=1, source_target_pairs={{0,8},{8,0},{1,9},{9,1},{2,10},{10,2},{3,11},{11,3},{16,24},{24,16... | collective-permute-start | bytes 589832 | tf_op jit(solution)/shard_map/ppermute | solution.py:46
  (4 other events, 3.7 us)

commit v4 on v3

--- a/solution.py
+++ b/solution.py
@@ -174,13 +174,14 @@
     n = len(weights)
     total = sum(a.shape[0] for a in weights)
     anywhere = pl.BlockSpec(memory_space=pl.ANY)
-    vmem = pl.BlockSpec(memory_space=pltpu.VMEM)
+    depth = weights[0].shape[1]
     return pl.pallas_call(
         functools.partial(prepare_body, n),
+        grid=(1,),
         in_specs=[pl.BlockSpec(memory_space=pltpu.SMEM)] * 2 + [anywhere] * (2 + n),
-        out_specs=[vmem, vmem],
+        out_specs=[pl.BlockSpec((8, 8 * PIECE), lambda i: (0, 0)), pl.BlockSpec((total, depth), lambda i: (0, 0))],
         out_shape=[
-            jax.ShapeDtypeStruct((4, 8 * PIECE), F32),
+            jax.ShapeDtypeStruct((2048, 8 * PIECE), F32),
             jax.ShapeDtypeStruct((total, weights[0].shape[1]), BF16),
         ],
         scratch_shapes=[
@@ -198,14 +199,15 @@
     return -(-n // unit) * unit
 
 
-def project_body(n, first, ready_rows, plan, gates_ref, own_ref, peer_ref, *rest):
+def project_body(n, first, ready_rows, plan, gates_any, own_ref, peer_ref, *rest):
     ready = rest[0] if ready_rows else None
     rest = rest[1:] if ready_rows else rest
     weights = rest[:n]
-    mine_ref, send_ref, x, w, w_sem = rest[n:]
+    mine_ref, send_ref, x, w, gates_own, w_sem, g_sem = rest[n:]
     groups, tokens, _ = own_ref.shape
     heads = own_ref.shape[2] // (2 * HD)
 
+    gates_ref = gates_any if ready_rows else gates_own
     at, w_copies = 0, []
     for i, (which, start, rows) in enumerate(plan):
         piece = weights[which].at[pl.ds(start, rows), :]
@@ -213,6 +215,10 @@
         at += rows
     for c in w_copies:
         c.start()
+    gates_copy = None
+    if not ready_rows:
+        gates_copy = pltpu.make_async_copy(gates_any.at[pl.ds(0, 8), :], gates_own, g_sem)
+        gates_copy.start()
 
     for who, ref in enumerate((own_ref, peer_ref)):
         for g in range(groups):
@@ -236,9 +242,15 @@
 
     if ready_rows:
         part(ready, 0)
+    else:
+        gates_copy.wait()
     for c in w_copies:
         c.wait()
     part(w, ready_rows)
+
+
+def whole(a):
+    return pl.BlockSpec(a.shape, lambda i: (0,) * len(a.shape))
 
 
 def project(first, own, peer, gates, ready, weights, plan=None):
@@ -249,17 +261,21 @@
     ready_rows = 0 if ready is None else ready.shape[0]
     depth = weights[0].shape[1]
     hbm = pl.BlockSpec(memory_space=pltpu.HBM)
-    vmem = pl.BlockSpec(memory_space=pltpu.VMEM)
     half = jax.ShapeDtypeStruct((2, tokens, round_up(ready_rows + rows, HD)), BF16)
     return pl.pallas_call(
         functools.partial(project_body, n, first, ready_rows, plan),
-        in_specs=[vmem] * (3 if ready is None else 4) + [hbm] * n,
-        out_specs=[vmem, vmem],
+        grid=(1,),
+        in_specs=[hbm if ready is None else pl.BlockSpec((8, gates.shape[1]), lambda i: (0, 0))]
+        + [whole(a) for a in ((own, peer) if ready is None else (own, peer, ready))]
+        + [hbm] * n,
+        out_specs=[whole(half), whole(half)],
         out_shape=[half, half],
         scratch_shapes=[
             pltpu.VMEM((4 * tokens, depth), BF16),
             pltpu.VMEM((rows, depth), BF16),
+            pltpu.VMEM((8, gates.shape[1]), F32),
             pltpu.SemaphoreType.DMA((len(plan),)),
+            pltpu.SemaphoreType.DMA,
         ],
         compiler_params=pltpu.CompilerParams(vmem_limit_bytes=36 * MIB),
         cost_estimate=NO_COST,
@@ -329,9 +345,9 @@
     info = jnp.stack([jnp.asarray(v, jnp.int32) for v in (*source, core, *block)])
 
     weight = out_weight.T
-    half = PIECE // 2
+    early = 160
     near = move(weight, beside())
-    w1 = weight[:half]
+    w1 = weight[:early]
     a1 = move(w1, up)
     b1 = move(w1, down)
     peer_time = move(time_index, swap)
@@ -344,16 +360,16 @@
     )
 
     received = exchange(packed)
-    w2 = weight[half:]
+    w2 = weight[early:]
     a2 = move(w2, up)
     b2 = move(w2, down)
     c1 = move(a1, up)
     c2 = move(b2, down)
-    quarter = half // 2
+    quarter = PIECE // 4
     near_a1 = move(near[:quarter], up)
     near_a2 = move(near[quarter:], up)
-    near_b1 = move(near[quarter:half], down)
-    near_b2 = move(jnp.concatenate([near[:quarter], near[half:]]), down)
+    near_b1 = move(near[quarter:early], down)
+    near_b2 = move(jnp.concatenate([near[:quarter], near[early:]]), down)
     received, a2, b2, c1, c2 = lax.optimization_barrier((received, a2, b2, c1, c2))
 
     attn = attend(received, 0, 3)
@@ -375,7 +391,7 @@
         gates,
         here,
         (near, near_a1, near_a2, near_b1, near_b2),
-        [(0, 0, PIECE), (1, 0, quarter), (2, 0, PIECE - quarter), (4, 0, quarter), (3, 0, quarter), (4, quarter, half)],
+        [(0, 0, PIECE), (1, 0, quarter), (2, 0, PIECE - quarter), (4, 0, quarter), (3, 0, early - quarter), (4, quarter, PIECE - early)],
     )
     mine_a, sent_a, near_c1, near_c2, near_c3 = lax.optimization_barrier((mine_a, sent_a, near_c1, near_c2, near_c3))
     got_a = move(sent_a, swap)

time: 155 us -> 155 us (level)
    unnamed x16 -> x14, local copies, waits for them, and re-layouts: 3.75 us -> 3.01 us
where the time goes in v4:
time: 155 us; the launch traced here: 154 us
  waiting for transfers between devices  66.2 us (43%)
  Pallas kernels  42.5 us (27%)
  starting transfers between devices  33.2 us (21%)
  local copies, waits for them, and re-layouts  8.3 us (5%)
  other arithmetic  2.56 us (2%)
    ppermute x18, waiting for transfers between devices, move(): return lax.ppermute(a, ('fsdp', 'seq'), perm)  59.2 us
    ppermute x18, starting transfers between devices, move(): return lax.ppermute(a, ('fsdp', 'seq'), perm)  23.8 us
    pallas_call x2, Pallas kernels, project(): pl.pallas_call(functools.partial(project_body, n, first, ready_rows, plan...  15.6 us
    pallas_call x1, Pallas kernels, attend(): pl.pallas_call(attn_body, grid=(width // (6 * HD),), in_specs=[pl.BlockSp...  11.1 us
    all_to_all x2, starting transfers between devices, exchange(): return lax.all_to_all(a, 'seq', split_axis=0, concat_axis=0, tiled=True)  9.48 us
    pallas_call x1, Pallas kernels, prepare(): pl.pallas_call(functools.partial(prepare_body, n), grid=(1,), in_specs=[p...  7.42 us
    all_to_all x2, waiting for transfers between devices, exchange(): return lax.all_to_all(a, 'seq', split_axis=0, concat_axis=0, tiled=True)  6.95 us
    pallas_call x1, Pallas kernels, norm_pack(): pl.pallas_call(norm_body, grid=(tokens // rows,), in_specs=[wide] * 6 + [...  5.81 us
  transfers between devices with their start and end apart: 20, of which 8 were waited for; matrix products, arithmetic and copies ran while one was open for 5% of the time, Pallas kernels for 26%

profile of v4, /device:TPU:1, one launch (start us, length us, event | category | flops | bytes accessed | tf_op | source)
XLA Modules:
  0.0 154.2 jit_solution(16664062753143580287)
XLA Ops:
  0.6 3.4 %collective-permute-start = (bf16[320,3072]{1,0:T(8,128)(2,1)}, bf16[320,3072]{1,0:T(8,128)(2,1)S(1)}, u32[]{:S(2)}, u32[]{:S(2)}) collective-permute-start(bf16[320,3072]{1,0:T(8,128)(2,1)} %bitcast.20), channel_id=1, source_target_pairs={{0,16},{8,28},{1,17},{9,29},{2,18},{10,30},{3,19},{11,31},{16,4},{... | collective-permute-start | bytes 5898248 | tf_op jit(solution)/shard_map/ppermute | solution.py:46
  5.3 1.4 collective-permute-start.1
  6.7 1.5 collective-permute-start.2
  9.0 5.8 %norm_pack.1 = bf16[8,128,2304]{2,1,0:T(8,128)(2,1)} custom-call(bf16[128,3072]{1,0:T(8,128)(2,1)} %q_ref.1, bf16[128,3072]{1,0:T(8,128)(2,1)} %qd_ref.1, bf16[128,3072]{1,0:T(8,128)(2,1)} %k_ref.1, bf16[128,3072]{1,0:T(8,128)(2,1)} %kd_ref.1, bf16[128,3072]{1,0:T(8,128)(2,1)} %v_ref.1, bf16[128,3072]{1,0:T(8,128)(2,1)} %vd_ref.1, f32[1,3072]{1,0:T(1,128)} %bitcast.24, ...), custom_call_target="tpu_custom_call" | custom-call | tf_op jit(solution)/shard_map/norm_pack/pallas_call | solution.py:81
  16.7 13.7 %collective-permute-done.1.rest_1_ = bf16[160,3072]{1,0:T(8,128)(2,1)} collective-permute-done((bf16[160,3072]{1,0:T(8,128)(2,1)S(1)}, bf16[160,3072]{1,0:T(8,128)(2,1)}, u32[]{:S(2)}, u32[]{:S(2)}) %collective-permute-start.1) | collective-permute-done | bytes 983072 | tf_op jit(solution)/shard_map/ppermute | solution.py:46
  30.5 5.0 %all-to-all-start = ((bf16[8,128,2304]{2,1,0:T(8,128)(2,1)}), bf16[8,128,2304]{2,1,0:T(8,128)(2,1)}, u32[]{:S(2)}, u32[]{:S(2)}) async-start(bf16[8,128,2304]{2,1,0:T(8,128)(2,1)} %norm_pack.1), calls=%async_computation | async-start | bytes 9437184 | tf_op jit(solution)/shard_map/all_to_all | solution.py:339
  36.8 2.6 %collective-permute-start.5 = (bf16[160,3072]{1,0:T(8,128)(2,1)S(1)}, bf16[160,3072]{1,0:T(8,128)(2,1)S(1)}, u32[]{:S(2)}, u32[]{:S(2)}) collective-permute-start(bf16[160,3072]{1,0:T(8,128)(2,1)S(1)} %slice.20), channel_id=1, source_target_pairs={{0,96},{8,104},{1,97},{9,105},{2,98},{10,106},{3,99},{11,107},{16,... | collective-permute-start | bytes 2949128 | tf_op jit(solution)/shard_map/ppermute | solution.py:46
  40.7 18.6 %collective-permute-done.5.rest_4_ = bf16[160,3072]{1,0:T(8,128)(2,1)S(1)} collective-permute-done((bf16[160,3072]{1,0:T(8,128)(2,1)S(1)}, bf16[160,3072]{1,0:T(8,128)(2,1)S(1)}, u32[]{:S(2)}, u32[]{:S(2)}) %collective-permute-start.5) | collective-permute-done | bytes 983072 | tf_op jit(solution)/shard_map/ppermute | solution.py:46
  59.2 3.5 %collective-permute-start.7 = (bf16[160,3072]{1,0:T(8,128)(2,1)S(1)}, bf16[160,3072]{1,0:T(8,128)(2,1)}, u32[]{:S(2)}, u32[]{:S(2)}) collective-permute-start(bf16[160,3072]{1,0:T(8,128)(2,1)S(1)} %collective-permute-done.5.rest_4_), channel_id=1, source_target_pairs={{0,96},{8,104},{1,97},{9,105},{2,98},{10,106},{3,99},{11,107},{16,... | collective-permute-start | bytes 2949128 | tf_op jit(solution)/shard_map/ppermute | solution.py:46
  64.9 1.4 collective-permute-start.9
  67.3 16.2 %collective-permute-done.6.rest_5_ = bf16[160,3072]{1,0:T(8,128)(2,1)S(1)} collective-permute-done((bf16[160,3072]{1,0:T(8,128)(2,1)}, bf16[160,3072]{1,0:T(8,128)(2,1)S(1)}, u32[]{:S(2)}, u32[]{:S(2)}) %collective-permute-start.6) | collective-permute-done | bytes 983072 | tf_op jit(solution)/shard_map/ppermute | solution.py:46
  84.5 6.1 %all-to-all-done.in_ref = bf16[8,128,2304]{2,1,0:T(8,128)(2,1)} async-done(((bf16[8,128,2304]{2,1,0:T(8,128)(2,1)}), bf16[8,128,2304]{2,1,0:T(8,128)(2,1)}, u32[]{:S(2)}, u32[]{:S(2)}) %all-to-all-start) | async-done | bytes 4718624 | tf_op jit(solution)/shard_map/all_to_all | solution.py:339
  90.6 11.1 %attend.1 = bf16[8,128,768]{2,1,0:T(8,128)(2,1)} custom-call(bf16[8,128,2304]{2,1,0:T(8,128)(2,1)} %all-to-all-done.in_ref), custom_call_target="tpu_custom_call" | custom-call | tf_op jit(solution)/shard_map/attend/pallas_call | solution.py:130
  101.7 4.4 %all-to-all-start.1 = ((bf16[8,128,768]{2,1,0:T(8,128)(2,1)}), bf16[8,128,768]{2,1,0:T(8,128)(2,1)S(1)}, u32[]{:S(2)}, u32[]{:S(2)}) async-start(bf16[8,128,768]{2,1,0:T(8,128)(2,1)} %attend.1), calls=%async_computation.1 | async-start | bytes 3145728 | tf_op jit(solution)/shard_map/all_to_all | solution.py:339
  106.1 2.5 %collective-permute-start.10 = (bf16[80,3072]{1,0:T(8,128)(2,1)}, bf16[80,3072]{1,0:T(8,128)(2,1)S(1)}, u32[]{:S(2)}, u32[]{:S(2)}) collective-permute-start(bf16[80,3072]{1,0:T(8,128)(2,1)} %get-tuple-element.64), channel_id=1, source_target_pairs={{0,96},{8,104},{1,97},{9,105},{2,98},{10,106},{3,99},{11,107},{16,... | collective-permute-start | bytes 1474568 | tf_op jit(solution)/shard_map/ppermute | solution.py:46
  108.7 7.4 %prepare.1 = (f32[2048,2560]{1,0:T(8,128)}, bf16[1280,3072]{1,0:T(8,128)(2,1)}) custom-call(s32[2]{0:T(128)} %pad_add_fusion.times_ref, s32[17]{0:T(128)} %stack.71.info_ref, f32[64,5120]{1,0:T(8,128)} %gate_hbm.1, f32[64,5120]{1,0:T(8,128)} %gate_dot_hbm.1, bf16[320,3072]{1,0:T(8,128)(2,1)} %bitcast.23, bf16[160,3072]{1,0:T(8,128)(2,1)} %collective-permute-done.1.rest_1_, ...), custom_call_target="tpu_custom_call" | custom-call | tf_op jit(solution)/shard_map/prepare/pallas_call | solution.py:178
  116.1 7.9 %collective-permute-done.10.rest_4_ = bf16[80,3072]{1,0:T(8,128)(2,1)S(1)} collective-permute-done((bf16[80,3072]{1,0:T(8,128)(2,1)}, bf16[80,3072]{1,0:T(8,128)(2,1)S(1)}, u32[]{:S(2)}, u32[]{:S(2)}) %collective-permute-start.10) | collective-permute-done | bytes 491552 | tf_op jit(solution)/shard_map/ppermute | solution.py:46
  124.0 1.6 %collective-permute-done.8.rest_2_ = bf16[80,3072]{1,0:T(8,128)(2,1)} collective-permute-done((bf16[80,3072]{1,0:T(8,128)(2,1)}, bf16[80,3072]{1,0:T(8,128)(2,1)}, u32[]{:S(2)}, u32[]{:S(2)}) %collective-permute-start.8) | collective-permute-done | bytes 491552 | tf_op jit(solution)/shard_map/ppermute | solution.py:46
  126.5 1.6 %collective-permute-start.12 = (bf16[8,128,768]{2,1,0:T(8,128)(2,1)S(1)}, bf16[8,128,768]{2,1,0:T(8,128)(2,1)S(1)}, u32[]{:S(2)}, u32[]{:S(2)}) collective-permute-start(bf16[8,128,768]{2,1,0:T(8,128)(2,1)S(1)} %all-to-all-done.1.own_ref), channel_id=1, source_target_pairs={{0,8},{8,0},{1,9},{9,1},{2,10},{10,2},{3,11},{11,3},{16,24},{24,16... | collective-permute-start | bytes 4718600 | tf_op jit(solution)/shard_map/ppermute | solution.py:46
  128.2 2.3 %collective-permute-start.15 = (bf16[160,3072]{1,0:T(8,128)(2,1)}, bf16[160,3072]{1,0:T(8,128)(2,1)S(1)}, u32[]{:S(2)}, u32[]{:S(2)}) collective-permute-start(bf16[160,3072]{1,0:T(8,128)(2,1)} %collective-permute-done.7.rest_6_), channel_id=1, source_target_pairs={{0,16},{8,28},{1,17},{9,29},{2,18},{10,30},{3,19},{11,31},{16,4},{... | collective-permute-start | bytes 2949128 | tf_op jit(solution)/shard_map/ppermute | solution.py:46
  130.5 2.7 %collective-permute-start.14 = (bf16[80,3072]{1,0:T(8,128)(2,1)}, bf16[80,3072]{1,0:T(8,128)(2,1)S(1)}, u32[]{:S(2)}, u32[]{:S(2)}) collective-permute-start(bf16[80,3072]{1,0:T(8,128)(2,1)} %copy-done), channel_id=1, source_target_pairs={{0,96},{8,104},{1,97},{9,105},{2,98},{10,106},{3,99},{11,107},{16,... | collective-permute-start | bytes 1474568 | tf_op jit(solution)/shard_map/ppermute | solution.py:46
  134.2 11.7 %project.2 = (bf16[2,128,2304]{2,1,0:T(8,128)(2,1)S(1)}, bf16[2,128,2304]{2,1,0:T(8,128)(2,1)S(1)}) custom-call(f32[2048,2560]{1,0:T(8,128)} %get-tuple-element.47.gates_any, bf16[8,128,768]{2,1,0:T(8,128)(2,1)S(1)} %all-to-all-done.1.own_ref, bf16[8,128,768]{2,1,0:T(8,128)(2,1)S(1)} %collective-permute-done.12.peer_ref, ...), custom_call_target="tpu_custom_call" | custom-call | tf_op jit(solution)/shard_map/project/pallas_call | solution.py:265
  146.0 3.9 %project.3 = (bf16[2,128,384]{2,1,0:T(8,128)(2,1)S(1)}, bf16[2,128,384]{2,1,0:T(8,128)(2,1)S(1)}) custom-call(f32[2048,2560]{1,0:T(8,128)} %get-tuple-element.47.gates_any, bf16[8,128,768]{2,1,0:T(8,128)(2,1)S(1)} %all-to-all-done.1.own_ref, bf16[8,128,768]{2,1,0:T(8,128)(2,1)S(1)} %collective-permute-done.12.peer_ref, ...), custom_call_target="tpu_custom_call" | custom-call | tf_op jit(solution)/shard_map/project/pallas_call | solution.py:265
  151.6 2.6 %merge.1 = (bf16[128,5120]{1,0:T(8,128)(2,1)}, bf16[128,5120]{1,0:T(8,128)(2,1)}) custom-call(s32[17]{0:T(128)S(1)} %copy-done.2, bf16[2,128,2304]{2,1,0:T(8,128)(2,1)S(1)} %get-tuple-element.57.refs_0_, bf16[2,128,384]{2,1,0:T(8,128)(2,1)S(1)} %get-tuple-element.61.refs_1_, bf16[2,128,2304]{2,1,0:T(8,128)(2,1)S(1)} %collective-permute-done.16.refs_2_, ...), custom_call_target="tpu_custom_call" | custom-call | tf_op jit(solution)/shard_map/merge/pallas_call | solution.py:306
  (44 shorter events, 13.7 us)
Async XLA Ops:
  0.6 29.8 %collective-permute-start = (bf16[320,3072]{1,0:T(8,128)(2,1)}, bf16[320,3072]{1,0:T(8,128)(2,1)S(1)}, u32[]{:S(2)}, u32[]{:S(2)}) collective-permute-start(bf16[320,3072]{1,0:T(8,128)(2,1)} %bitcast.20), channel_id=1, source_target_pairs={{0,16},{8,28},{1,17},{9,29},{2,18},{10,30},{3,19},{11,31},{16,4},{... | collective-permute-start | bytes 5898248 | tf_op jit(solution)/shard_map/ppermute | solution.py:46
  5.3 25.1 %collective-permute-start.1 = (bf16[160,3072]{1,0:T(8,128)(2,1)S(1)}, bf16[160,3072]{1,0:T(8,128)(2,1)}, u32[]{:S(2)}, u32[]{:S(2)}) collective-permute-start(bf16[160,3072]{1,0:T(8,128)(2,1)S(1)} %slice.25), channel_id=1, source_target_pairs={{0,32},{8,40},{1,33},{9,41},{2,34},{10,42},{3,35},{11,43},{16,48},... | collective-permute-start | bytes 2949128 | tf_op jit(solution)/shard_map/ppermute | solution.py:46
  6.7 23.8 %collective-permute-start.2 = (bf16[160,3072]{1,0:T(8,128)(2,1)S(1)}, bf16[160,3072]{1,0:T(8,128)(2,1)}, u32[]{:S(2)}, u32[]{:S(2)}) collective-permute-start(bf16[160,3072]{1,0:T(8,128)(2,1)S(1)} %slice.25), channel_id=1, source_target_pairs={{0,96},{8,104},{1,97},{9,105},{2,98},{10,106},{3,99},{11,107},{16,... | collective-permute-start | bytes 2949128 | tf_op jit(solution)/shard_map/ppermute | solution.py:46
  8.2 7.2 %collective-permute-start.3 = (s32[1]{0:T(128)}, s32[1]{0:T(128)}, u32[]{:S(2)}, u32[]{:S(2)}) collective-permute-start(s32[1]{0:T(128)} %param.23), channel_id=1, source_target_pairs={{0,8},{8,0},{1,9},{9,1},{2,10},{10,2},{3,11},{11,3},{16,24},{24,16... | collective-permute-start | bytes 20 | tf_op jit(solution)/shard_map/ppermute | solution.py:46
  30.5 60.1 %all-to-all-start = ((bf16[8,128,2304]{2,1,0:T(8,128)(2,1)}), bf16[8,128,2304]{2,1,0:T(8,128)(2,1)}, u32[]{:S(2)}, u32[]{:S(2)}) async-start(bf16[8,128,2304]{2,1,0:T(8,128)(2,1)} %norm_pack.1), calls=%async_computation | async-start | bytes 9437184 | tf_op jit(solution)/shard_map/all_to_all | solution.py:339
  36.8 22.5 %collective-permute-start.5 = (bf16[160,3072]{1,0:T(8,128)(2,1)S(1)}, bf16[160,3072]{1,0:T(8,128)(2,1)S(1)}, u32[]{:S(2)}, u32[]{:S(2)}) collective-permute-start(bf16[160,3072]{1,0:T(8,128)(2,1)S(1)} %slice.20), channel_id=1, source_target_pairs={{0,96},{8,104},{1,97},{9,105},{2,98},{10,106},{3,99},{11,107},{16,... | collective-permute-start | bytes 2949128 | tf_op jit(solution)/shard_map/ppermute | solution.py:46
  39.4 27.0 %collective-permute-start.4 = (bf16[160,3072]{1,0:T(8,128)(2,1)S(1)}, bf16[160,3072]{1,0:T(8,128)(2,1)S(1)}, u32[]{:S(2)}, u32[]{:S(2)}) collective-permute-start(bf16[160,3072]{1,0:T(8,128)(2,1)S(1)} %slice.20), channel_id=1, source_target_pairs={{0,32},{8,40},{1,33},{9,41},{2,34},{10,42},{3,35},{11,43},{16,48},... | collective-permute-start | bytes 2949128 | tf_op jit(solution)/shard_map/ppermute | solution.py:46
  40.7 42.9 %collective-permute-start.6 = (bf16[160,3072]{1,0:T(8,128)(2,1)}, bf16[160,3072]{1,0:T(8,128)(2,1)S(1)}, u32[]{:S(2)}, u32[]{:S(2)}) collective-permute-start(bf16[160,3072]{1,0:T(8,128)(2,1)} %collective-permute-done.1.rest_1_), channel_id=1, source_target_pairs={{0,32},{8,40},{1,33},{9,41},{2,34},{10,42},{3,35},{11,43},{16,48},... | collective-permute-start | bytes 2949128 | tf_op jit(solution)/shard_map/ppermute | solution.py:46
  59.2 5.6 %copy-start.4 = (bf16[160,3072]{1,0:T(8,128)(2,1)}, bf16[160,3072]{1,0:T(8,128)(2,1)S(1)}, u32[]{:S(2)}) copy-start(bf16[160,3072]{1,0:T(8,128)(2,1)S(1)} %collective-permute-done.5.rest_4_) | copy-start | bytes 2949124
  59.2 25.3 %collective-permute-start.7 = (bf16[160,3072]{1,0:T(8,128)(2,1)S(1)}, bf16[160,3072]{1,0:T(8,128)(2,1)}, u32[]{:S(2)}, u32[]{:S(2)}) collective-permute-start(bf16[160,3072]{1,0:T(8,128)(2,1)S(1)} %collective-permute-done.5.rest_4_), channel_id=1, source_target_pairs={{0,96},{8,104},{1,97},{9,105},{2,98},{10,106},{3,99},{11,107},{16,... | collective-permute-start | bytes 2949128 | tf_op jit(solution)/shard_map/ppermute | solution.py:46
  63.6 1.3 copy-start.3
  64.9 60.8 %collective-permute-start.11 = (bf16[240,3072]{1,0:T(8,128)(2,1)}, bf16[240,3072]{1,0:T(8,128)(2,1)}, u32[]{:S(2)}, u32[]{:S(2)}) collective-permute-start(bf16[240,3072]{1,0:T(8,128)(2,1)} %pad_maximum_fusion), channel_id=1, source_target_pairs={{0,96},{8,104},{1,97},{9,105},{2,98},{10,106},{3,99},{11,107},{16,... | collective-permute-start | bytes 4423688 | tf_op jit(solution)/shard_map/ppermute | solution.py:46
  64.9 60.7 %collective-permute-start.9 = (bf16[240,3072]{1,0:T(8,128)(2,1)}, bf16[240,3072]{1,0:T(8,128)(2,1)}, u32[]{:S(2)}, u32[]{:S(2)}) collective-permute-start(bf16[240,3072]{1,0:T(8,128)(2,1)} %slice.22), channel_id=1, source_target_pairs={{0,32},{8,40},{1,33},{9,41},{2,34},{10,42},{3,35},{11,43},{16,48},... | collective-permute-start | bytes 4423688 | tf_op jit(solution)/shard_map/ppermute | solution.py:46
  101.7 24.9 %all-to-all-start.1 = ((bf16[8,128,768]{2,1,0:T(8,128)(2,1)}), bf16[8,128,768]{2,1,0:T(8,128)(2,1)S(1)}, u32[]{:S(2)}, u32[]{:S(2)}) async-start(bf16[8,128,768]{2,1,0:T(8,128)(2,1)} %attend.1), calls=%async_computation.1 | async-start | bytes 3145728 | tf_op jit(solution)/shard_map/all_to_all | solution.py:339
  106.1 17.9 %collective-permute-start.10 = (bf16[80,3072]{1,0:T(8,128)(2,1)}, bf16[80,3072]{1,0:T(8,128)(2,1)S(1)}, u32[]{:S(2)}, u32[]{:S(2)}) collective-permute-start(bf16[80,3072]{1,0:T(8,128)(2,1)} %get-tuple-element.64), channel_id=1, source_target_pairs={{0,96},{8,104},{1,97},{9,105},{2,98},{10,106},{3,99},{11,107},{16,... | collective-permute-start | bytes 1474568 | tf_op jit(solution)/shard_map/ppermute | solution.py:46
  108.7 17.0 %collective-permute-start.8 = (bf16[80,3072]{1,0:T(8,128)(2,1)}, bf16[80,3072]{1,0:T(8,128)(2,1)}, u32[]{:S(2)}, u32[]{:S(2)}) collective-permute-start(bf16[80,3072]{1,0:T(8,128)(2,1)} %copy-done.3), channel_id=1, source_target_pairs={{0,32},{8,40},{1,33},{9,41},{2,34},{10,42},{3,35},{11,43},{16,48},... | collective-permute-start | bytes 1474568 | tf_op jit(solution)/shard_map/ppermute | solution.py:46
  124.0 1.6 %copy-start = (bf16[80,3072]{1,0:T(8,128)(2,1)}, bf16[80,3072]{1,0:T(8,128)(2,1)S(1)}, u32[]{:S(2)}) copy-start(bf16[80,3072]{1,0:T(8,128)(2,1)S(1)} %collective-permute-done.10.rest_4_) | copy-start | bytes 1474564
  126.5 6.6 %collective-permute-start.12 = (bf16[8,128,768]{2,1,0:T(8,128)(2,1)S(1)}, bf16[8,128,768]{2,1,0:T(8,128)(2,1)S(1)}, u32[]{:S(2)}, u32[]{:S(2)}) collective-permute-start(bf16[8,128,768]{2,1,0:T(8,128)(2,1)S(1)} %all-to-all-done.1.own_ref), channel_id=1, source_target_pairs={{0,8},{8,0},{1,9},{9,1},{2,10},{10,2},{3,11},{11,3},{16,24},{24,16... | collective-permute-start | bytes 4718600 | tf_op jit(solution)/shard_map/ppermute | solution.py:46
  128.2 17.7 %collective-permute-start.15 = (bf16[160,3072]{1,0:T(8,128)(2,1)}, bf16[160,3072]{1,0:T(8,128)(2,1)S(1)}, u32[]{:S(2)}, u32[]{:S(2)}) collective-permute-start(bf16[160,3072]{1,0:T(8,128)(2,1)} %collective-permute-done.7.rest_6_), channel_id=1, source_target_pairs={{0,16},{8,28},{1,17},{9,29},{2,18},{10,30},{3,19},{11,31},{16,4},{... | collective-permute-start | bytes 2949128 | tf_op jit(solution)/shard_map/ppermute | solution.py:46
  130.4 15.4 %collective-permute-start.13 = (bf16[80,3072]{1,0:T(8,128)(2,1)}, bf16[80,3072]{1,0:T(8,128)(2,1)S(1)}, u32[]{:S(2)}, u32[]{:S(2)}) collective-permute-start(bf16[80,3072]{1,0:T(8,128)(2,1)} %collective-permute-done.8.rest_2_), channel_id=1, source_target_pairs={{0,32},{8,40},{1,33},{9,41},{2,34},{10,42},{3,35},{11,43},{16,48},... | collective-permute-start | bytes 1474568 | tf_op jit(solution)/shard_map/ppermute | solution.py:46
  130.5 15.4 %collective-permute-start.14 = (bf16[80,3072]{1,0:T(8,128)(2,1)}, bf16[80,3072]{1,0:T(8,128)(2,1)S(1)}, u32[]{:S(2)}, u32[]{:S(2)}) collective-permute-start(bf16[80,3072]{1,0:T(8,128)(2,1)} %copy-done), channel_id=1, source_target_pairs={{0,96},{8,104},{1,97},{9,105},{2,98},{10,106},{3,99},{11,107},{16,... | collective-permute-start | bytes 1474568 | tf_op jit(solution)/shard_map/ppermute | solution.py:46
  145.9 5.7 %copy-start.2 = (s32[17]{0:T(128)S(1)}, s32[17]{0:T(128)}, u32[]{:S(2)}) copy-start(s32[17]{0:T(128)} %stack.71.info_ref) | copy-start | bytes 208
  145.9 5.7 %collective-permute-start.16 = (bf16[2,128,2304]{2,1,0:T(8,128)(2,1)S(1)}, bf16[2,128,2304]{2,1,0:T(8,128)(2,1)S(1)}, u32[]{:S(2)}, u32[]{:S(2)}) collective-permute-start(bf16[2,128,2304]{2,1,0:T(8,128)(2,1)S(1)} %get-tuple-element.62), channel_id=1, source_target_pairs={{0,8},{8,0},{1,9},{9,1},{2,10},{10,2},{3,11},{11,3},{16,24},{24,16... | collective-permute-start | bytes 3538952 | tf_op jit(solution)/shard_map/ppermute | solution.py:46
  149.9 1.6 %collective-permute-start.17 = (bf16[2,128,384]{2,1,0:T(8,128)(2,1)S(1)}, bf16[2,128,384]{2,1,0:T(8,128)(2,1)S(1)}, u32[]{:S(2)}, u32[]{:S(2)}) collective-permute-start(bf16[2,128,384]{2,1,0:T(8,128)(2,1)S(1)} %get-tuple-element.63), channel_id=1, source_target_pairs={{0,8},{8,0},{1,9},{9,1},{2,10},{10,2},{3,11},{11,3},{16,24},{24,16... | collective-permute-start | bytes 589832 | tf_op jit(solution)/shard_map/ppermute | solution.py:46
  (3 other events, 3.0 us)

commit v5 on v4

--- a/solution.py
+++ b/solution.py
@@ -375,9 +375,8 @@
     attn = attend(received, 0, 3)
     own = exchange(attn)
     gates, here = prepare(times, info, gate_table, gate_dot_table, (weight, a1, a2, b1, b2, c1, c2))
-    own, near_a1, near_a2, near_b1, near_b2, gates, here, c2 = lax.optimization_barrier(
-        (own, near_a1, near_a2, near_b1, near_b2, gates, here, c2)
-    )
+    own, near_a2, near_b2, gates, here, c2 = lax.optimization_barrier((own, near_a2, near_b2, gates, here, c2))
+    own, near_a1, near_b1 = lax.optimization_barrier((own, near_a1, near_b1))
 
     peer = move(own, swap)
     near_c1 = move(near_a1, up)

time: 155 us -> 153 us (0.987)
    ppermute x18, waiting for transfers between devices: 59.2 us -> 49.5 us  [move(): return lax.ppermute(a, ('fsdp', 'seq'), perm)]
    all_to_all x2, waiting for transfers between devices: 6.95 us -> 16.4 us  [exchange(): return lax.all_to_all(a, 'seq', split_axis=0, concat_axis=0, tiled=True)]
  transfers between devices with their start and end apart: 20 -> 20, of which waited for: 8 -> 6; matrix products, arithmetic and copies ran while one was open for 5% -> 5% of each run, Pallas kernels for 26% -> 26%
where the time goes in v5:
time: 153 us
  waiting for transfers between devices  66 us (43%)
  Pallas kernels  42.1 us (28%)
  starting transfers between devices  33.3 us (22%)
  local copies, waits for them, and re-layouts  7.29 us (5%)
  other arithmetic  2.56 us (2%)
    ppermute x18, waiting for transfers between devices, move(): return lax.ppermute(a, ('fsdp', 'seq'), perm)  49.5 us
    ppermute x18, starting transfers between devices, move(): return lax.ppermute(a, ('fsdp', 'seq'), perm)  23.8 us
    all_to_all x2, waiting for transfers between devices, exchange(): return lax.all_to_all(a, 'seq', split_axis=0, concat_axis=0, tiled=True)  16.4 us
    pallas_call x2, Pallas kernels, project(): pl.pallas_call(functools.partial(project_body, n, first, ready_rows, plan...  15.3 us
    pallas_call x1, Pallas kernels, attend(): pl.pallas_call(attn_body, grid=(width // (6 * HD),), in_specs=[pl.BlockSp...  11 us
    all_to_all x2, starting transfers between devices, exchange(): return lax.all_to_all(a, 'seq', split_axis=0, concat_axis=0, tiled=True)  9.48 us
    pallas_call x1, Pallas kernels, prepare(): pl.pallas_call(functools.partial(prepare_body, n), grid=(1,), in_specs=[p...  7.39 us
    pallas_call x1, Pallas kernels, norm_pack(): pl.pallas_call(norm_body, grid=(tokens // rows,), in_specs=[wide] * 6 + [...  5.85 us
  transfers between devices with their start and end apart: 20, of which 6 were waited for; matrix products, arithmetic and copies ran while one was open for 5% of the time, Pallas kernels for 26%

profile of v5, /device:TPU:1, one launch (start us, length us, event | category | flops | bytes accessed | tf_op | source)
XLA Modules:
  0.0 152.7 jit_solution(514143095304693561)
XLA Ops:
  0.6 3.4 %collective-permute-start = (bf16[320,3072]{1,0:T(8,128)(2,1)}, bf16[320,3072]{1,0:T(8,128)(2,1)S(1)}, u32[]{:S(2)}, u32[]{:S(2)}) collective-permute-start(bf16[320,3072]{1,0:T(8,128)(2,1)} %bitcast.20), channel_id=1, source_target_pairs={{0,16},{8,28},{1,17},{9,29},{2,18},{10,30},{3,19},{11,31},{16,4},{... | collective-permute-start | bytes 5898248 | tf_op jit(solution)/shard_map/ppermute | solution.py:46
  4.0 1.3 slice.25
  5.3 1.4 collective-permute-start.1
  6.7 1.5 collective-permute-start.2
  9.0 5.9 %norm_pack.1 = bf16[8,128,2304]{2,1,0:T(8,128)(2,1)} custom-call(bf16[128,3072]{1,0:T(8,128)(2,1)} %q_ref.1, bf16[128,3072]{1,0:T(8,128)(2,1)} %qd_ref.1, bf16[128,3072]{1,0:T(8,128)(2,1)} %k_ref.1, bf16[128,3072]{1,0:T(8,128)(2,1)} %kd_ref.1, bf16[128,3072]{1,0:T(8,128)(2,1)} %v_ref.1, bf16[128,3072]{1,0:T(8,128)(2,1)} %vd_ref.1, f32[1,3072]{1,0:T(1,128)} %bitcast.24, ...), custom_call_target="tpu_custom_call" | custom-call | tf_op jit(solution)/shard_map/norm_pack/pallas_call | solution.py:81
  16.8 13.6 %collective-permute-done.1.rest_1_ = bf16[160,3072]{1,0:T(8,128)(2,1)} collective-permute-done((bf16[160,3072]{1,0:T(8,128)(2,1)S(1)}, bf16[160,3072]{1,0:T(8,128)(2,1)}, u32[]{:S(2)}, u32[]{:S(2)}) %collective-permute-start.1) | collective-permute-done | bytes 983072 | tf_op jit(solution)/shard_map/ppermute | solution.py:46
  30.5 5.0 %all-to-all-start = ((bf16[8,128,2304]{2,1,0:T(8,128)(2,1)}), bf16[8,128,2304]{2,1,0:T(8,128)(2,1)}, u32[]{:S(2)}, u32[]{:S(2)}) async-start(bf16[8,128,2304]{2,1,0:T(8,128)(2,1)} %norm_pack.1), calls=%async_computation | async-start | bytes 9437184 | tf_op jit(solution)/shard_map/all_to_all | solution.py:339
  36.8 2.6 %collective-permute-start.5 = (bf16[160,3072]{1,0:T(8,128)(2,1)S(1)}, bf16[160,3072]{1,0:T(8,128)(2,1)S(1)}, u32[]{:S(2)}, u32[]{:S(2)}) collective-permute-start(bf16[160,3072]{1,0:T(8,128)(2,1)S(1)} %slice.20), channel_id=1, source_target_pairs={{0,96},{8,104},{1,97},{9,105},{2,98},{10,106},{3,99},{11,107},{16,... | collective-permute-start | bytes 2949128 | tf_op jit(solution)/shard_map/ppermute | solution.py:46
  40.6 18.6 %collective-permute-done.5.rest_4_ = bf16[160,3072]{1,0:T(8,128)(2,1)S(1)} collective-permute-done((bf16[160,3072]{1,0:T(8,128)(2,1)S(1)}, bf16[160,3072]{1,0:T(8,128)(2,1)S(1)}, u32[]{:S(2)}, u32[]{:S(2)}) %collective-permute-start.5) | collective-permute-done | bytes 983072 | tf_op jit(solution)/shard_map/ppermute | solution.py:46
  59.2 3.5 %collective-permute-start.7 = (bf16[160,3072]{1,0:T(8,128)(2,1)S(1)}, bf16[160,3072]{1,0:T(8,128)(2,1)}, u32[]{:S(2)}, u32[]{:S(2)}) collective-permute-start(bf16[160,3072]{1,0:T(8,128)(2,1)S(1)} %collective-permute-done.5.rest_4_), channel_id=1, source_target_pairs={{0,96},{8,104},{1,97},{9,105},{2,98},{10,106},{3,99},{11,107},{16,... | collective-permute-start | bytes 2949128 | tf_op jit(solution)/shard_map/ppermute | solution.py:46
  64.9 1.4 collective-permute-start.8
  67.3 16.2 %collective-permute-done.6.rest_5_ = bf16[160,3072]{1,0:T(8,128)(2,1)S(1)} collective-permute-done((bf16[160,3072]{1,0:T(8,128)(2,1)}, bf16[160,3072]{1,0:T(8,128)(2,1)S(1)}, u32[]{:S(2)}, u32[]{:S(2)}) %collective-permute-start.6) | collective-permute-done | bytes 983072 | tf_op jit(solution)/shard_map/ppermute | solution.py:46
  84.5 6.1 %all-to-all-done.in_ref = bf16[8,128,2304]{2,1,0:T(8,128)(2,1)} async-done(((bf16[8,128,2304]{2,1,0:T(8,128)(2,1)}), bf16[8,128,2304]{2,1,0:T(8,128)(2,1)}, u32[]{:S(2)}, u32[]{:S(2)}) %all-to-all-start) | async-done | bytes 4718624 | tf_op jit(solution)/shard_map/all_to_all | solution.py:339
  90.6 11.0 %attend.1 = bf16[8,128,768]{2,1,0:T(8,128)(2,1)} custom-call(bf16[8,128,2304]{2,1,0:T(8,128)(2,1)} %all-to-all-done.in_ref), custom_call_target="tpu_custom_call" | custom-call | tf_op jit(solution)/shard_map/attend/pallas_call | solution.py:130
  101.6 4.4 %all-to-all-start.1 = ((bf16[8,128,768]{2,1,0:T(8,128)(2,1)}), bf16[8,128,768]{2,1,0:T(8,128)(2,1)S(1)}, u32[]{:S(2)}, u32[]{:S(2)}) async-start(bf16[8,128,768]{2,1,0:T(8,128)(2,1)} %attend.1), calls=%async_computation.1 | async-start | bytes 3145728 | tf_op jit(solution)/shard_map/all_to_all | solution.py:339
  107.1 1.6 %collective-permute-start.11 = (bf16[80,3072]{1,0:T(8,128)(2,1)}, bf16[80,3072]{1,0:T(8,128)(2,1)}, u32[]{:S(2)}, u32[]{:S(2)}) collective-permute-start(bf16[80,3072]{1,0:T(8,128)(2,1)} %get-tuple-element.66), channel_id=1, source_target_pairs={{0,96},{8,104},{1,97},{9,105},{2,98},{10,106},{3,99},{11,107},{16,... | collective-permute-start | bytes 1474568 | tf_op jit(solution)/shard_map/ppermute | solution.py:46
  108.7 7.4 %prepare.1 = (f32[2048,2560]{1,0:T(8,128)}, bf16[1280,3072]{1,0:T(8,128)(2,1)}) custom-call(s32[2]{0:T(128)} %pad_add_fusion.times_ref, s32[17]{0:T(128)} %stack.71.info_ref, f32[64,5120]{1,0:T(8,128)} %gate_hbm.1, f32[64,5120]{1,0:T(8,128)} %gate_dot_hbm.1, bf16[320,3072]{1,0:T(8,128)(2,1)} %bitcast.23, bf16[160,3072]{1,0:T(8,128)(2,1)} %collective-permute-done.1.rest_1_, ...), custom_call_target="tpu_custom_call" | custom-call | tf_op jit(solution)/shard_map/prepare/pallas_call | solution.py:178
  116.1 10.3 %all-to-all-done.1.own_ref = bf16[8,128,768]{2,1,0:T(8,128)(2,1)S(1)} async-done(((bf16[8,128,768]{2,1,0:T(8,128)(2,1)}), bf16[8,128,768]{2,1,0:T(8,128)(2,1)S(1)}, u32[]{:S(2)}, u32[]{:S(2)}) %all-to-all-start.1) | async-done | bytes 1572896 | tf_op jit(solution)/shard_map/all_to_all | solution.py:339
  126.5 1.6 %collective-permute-start.12 = (bf16[8,128,768]{2,1,0:T(8,128)(2,1)S(1)}, bf16[8,128,768]{2,1,0:T(8,128)(2,1)S(1)}, u32[]{:S(2)}, u32[]{:S(2)}) collective-permute-start(bf16[8,128,768]{2,1,0:T(8,128)(2,1)S(1)} %all-to-all-done.1.own_ref), channel_id=1, source_target_pairs={{0,8},{8,0},{1,9},{9,1},{2,10},{10,2},{3,11},{11,3},{16,24},{24,16... | collective-permute-start | bytes 4718600 | tf_op jit(solution)/shard_map/ppermute | solution.py:46
  128.1 2.3 %collective-permute-start.15 = (bf16[160,3072]{1,0:T(8,128)(2,1)}, bf16[160,3072]{1,0:T(8,128)(2,1)S(1)}, u32[]{:S(2)}, u32[]{:S(2)}) collective-permute-start(bf16[160,3072]{1,0:T(8,128)(2,1)} %collective-permute-done.7.rest_6_), channel_id=1, source_target_pairs={{0,16},{8,28},{1,17},{9,29},{2,18},{10,30},{3,19},{11,31},{16,4},{... | collective-permute-start | bytes 2949128 | tf_op jit(solution)/shard_map/ppermute | solution.py:46
  130.4 2.6 %collective-permute-start.14 = (bf16[80,3072]{1,0:T(8,128)(2,1)}, bf16[80,3072]{1,0:T(8,128)(2,1)S(1)}, u32[]{:S(2)}, u32[]{:S(2)}) collective-permute-start(bf16[80,3072]{1,0:T(8,128)(2,1)} %collective-permute-done.11.rest_4_), channel_id=1, source_target_pairs={{0,96},{8,104},{1,97},{9,105},{2,98},{10,106},{3,99},{11,107},{16,... | collective-permute-start | bytes 1474568 | tf_op jit(solution)/shard_map/ppermute | solution.py:46
  133.0 11.4 %project.2 = (bf16[2,128,2304]{2,1,0:T(8,128)(2,1)S(1)}, bf16[2,128,2304]{2,1,0:T(8,128)(2,1)S(1)}) custom-call(f32[2048,2560]{1,0:T(8,128)} %get-tuple-element.48.gates_any, bf16[8,128,768]{2,1,0:T(8,128)(2,1)S(1)} %all-to-all-done.1.own_ref, bf16[8,128,768]{2,1,0:T(8,128)(2,1)S(1)} %collective-permute-done.12.peer_ref, ...), custom_call_target="tpu_custom_call" | custom-call | tf_op jit(solution)/shard_map/project/pallas_call | solution.py:265
  144.5 3.9 %project.3 = (bf16[2,128,384]{2,1,0:T(8,128)(2,1)S(1)}, bf16[2,128,384]{2,1,0:T(8,128)(2,1)S(1)}) custom-call(f32[2048,2560]{1,0:T(8,128)} %get-tuple-element.48.gates_any, bf16[8,128,768]{2,1,0:T(8,128)(2,1)S(1)} %all-to-all-done.1.own_ref, bf16[8,128,768]{2,1,0:T(8,128)(2,1)S(1)} %collective-permute-done.12.peer_ref, ...), custom_call_target="tpu_custom_call" | custom-call | tf_op jit(solution)/shard_map/project/pallas_call | solution.py:265
  150.1 2.6 %merge.1 = (bf16[128,5120]{1,0:T(8,128)(2,1)}, bf16[128,5120]{1,0:T(8,128)(2,1)}) custom-call(s32[17]{0:T(128)S(1)} %copy-done, bf16[2,128,2304]{2,1,0:T(8,128)(2,1)S(1)} %get-tuple-element.59.refs_0_, bf16[2,128,384]{2,1,0:T(8,128)(2,1)S(1)} %get-tuple-element.63.refs_1_, bf16[2,128,2304]{2,1,0:T(8,128)(2,1)S(1)} %collective-permute-done.16.refs_2_, ...), custom_call_target="tpu_custom_call" | custom-call | tf_op jit(solution)/shard_map/merge/pallas_call | solution.py:306
  (40 shorter events, 11.6 us)
Async XLA Ops:
  0.6 29.8 %collective-permute-start = (bf16[320,3072]{1,0:T(8,128)(2,1)}, bf16[320,3072]{1,0:T(8,128)(2,1)S(1)}, u32[]{:S(2)}, u32[]{:S(2)}) collective-permute-start(bf16[320,3072]{1,0:T(8,128)(2,1)} %bitcast.20), channel_id=1, source_target_pairs={{0,16},{8,28},{1,17},{9,29},{2,18},{10,30},{3,19},{11,31},{16,4},{... | collective-permute-start | bytes 5898248 | tf_op jit(solution)/shard_map/ppermute | solution.py:46
  5.3 25.1 %collective-permute-start.1 = (bf16[160,3072]{1,0:T(8,128)(2,1)S(1)}, bf16[160,3072]{1,0:T(8,128)(2,1)}, u32[]{:S(2)}, u32[]{:S(2)}) collective-permute-start(bf16[160,3072]{1,0:T(8,128)(2,1)S(1)} %slice.25), channel_id=1, source_target_pairs={{0,32},{8,40},{1,33},{9,41},{2,34},{10,42},{3,35},{11,43},{16,48},... | collective-permute-start | bytes 2949128 | tf_op jit(solution)/shard_map/ppermute | solution.py:46
  6.7 23.8 %collective-permute-start.2 = (bf16[160,3072]{1,0:T(8,128)(2,1)S(1)}, bf16[160,3072]{1,0:T(8,128)(2,1)}, u32[]{:S(2)}, u32[]{:S(2)}) collective-permute-start(bf16[160,3072]{1,0:T(8,128)(2,1)S(1)} %slice.25), channel_id=1, source_target_pairs={{0,96},{8,104},{1,97},{9,105},{2,98},{10,106},{3,99},{11,107},{16,... | collective-permute-start | bytes 2949128 | tf_op jit(solution)/shard_map/ppermute | solution.py:46
  8.2 7.3 %collective-permute-start.3 = (s32[1]{0:T(128)}, s32[1]{0:T(128)}, u32[]{:S(2)}, u32[]{:S(2)}) collective-permute-start(s32[1]{0:T(128)} %param.23), channel_id=1, source_target_pairs={{0,8},{8,0},{1,9},{9,1},{2,10},{10,2},{3,11},{11,3},{16,24},{24,16... | collective-permute-start | bytes 20 | tf_op jit(solution)/shard_map/ppermute | solution.py:46
  30.5 60.1 %all-to-all-start = ((bf16[8,128,2304]{2,1,0:T(8,128)(2,1)}), bf16[8,128,2304]{2,1,0:T(8,128)(2,1)}, u32[]{:S(2)}, u32[]{:S(2)}) async-start(bf16[8,128,2304]{2,1,0:T(8,128)(2,1)} %norm_pack.1), calls=%async_computation | async-start | bytes 9437184 | tf_op jit(solution)/shard_map/all_to_all | solution.py:339
  36.8 22.5 %collective-permute-start.5 = (bf16[160,3072]{1,0:T(8,128)(2,1)S(1)}, bf16[160,3072]{1,0:T(8,128)(2,1)S(1)}, u32[]{:S(2)}, u32[]{:S(2)}) collective-permute-start(bf16[160,3072]{1,0:T(8,128)(2,1)S(1)} %slice.20), channel_id=1, source_target_pairs={{0,96},{8,104},{1,97},{9,105},{2,98},{10,106},{3,99},{11,107},{16,... | collective-permute-start | bytes 2949128 | tf_op jit(solution)/shard_map/ppermute | solution.py:46
  39.4 27.0 %collective-permute-start.4 = (bf16[160,3072]{1,0:T(8,128)(2,1)S(1)}, bf16[160,3072]{1,0:T(8,128)(2,1)S(1)}, u32[]{:S(2)}, u32[]{:S(2)}) collective-permute-start(bf16[160,3072]{1,0:T(8,128)(2,1)S(1)} %slice.20), channel_id=1, source_target_pairs={{0,32},{8,40},{1,33},{9,41},{2,34},{10,42},{3,35},{11,43},{16,48},... | collective-permute-start | bytes 2949128 | tf_op jit(solution)/shard_map/ppermute | solution.py:46
  40.6 42.9 %collective-permute-start.6 = (bf16[160,3072]{1,0:T(8,128)(2,1)}, bf16[160,3072]{1,0:T(8,128)(2,1)S(1)}, u32[]{:S(2)}, u32[]{:S(2)}) collective-permute-start(bf16[160,3072]{1,0:T(8,128)(2,1)} %collective-permute-done.1.rest_1_), channel_id=1, source_target_pairs={{0,32},{8,40},{1,33},{9,41},{2,34},{10,42},{3,35},{11,43},{16,48},... | collective-permute-start | bytes 2949128 | tf_op jit(solution)/shard_map/ppermute | solution.py:46
  59.2 5.6 %copy-start.2 = (bf16[160,3072]{1,0:T(8,128)(2,1)}, bf16[160,3072]{1,0:T(8,128)(2,1)S(1)}, u32[]{:S(2)}) copy-start(bf16[160,3072]{1,0:T(8,128)(2,1)S(1)} %collective-permute-done.5.rest_4_) | copy-start | bytes 2949124
  59.2 25.3 %collective-permute-start.7 = (bf16[160,3072]{1,0:T(8,128)(2,1)S(1)}, bf16[160,3072]{1,0:T(8,128)(2,1)}, u32[]{:S(2)}, u32[]{:S(2)}) collective-permute-start(bf16[160,3072]{1,0:T(8,128)(2,1)S(1)} %collective-permute-done.5.rest_4_), channel_id=1, source_target_pairs={{0,96},{8,104},{1,97},{9,105},{2,98},{10,106},{3,99},{11,107},{16,... | collective-permute-start | bytes 2949128 | tf_op jit(solution)/shard_map/ppermute | solution.py:46
  63.6 1.3 copy-start.1
  64.9 51.3 %collective-permute-start.9 = (bf16[240,3072]{1,0:T(8,128)(2,1)}, bf16[240,3072]{1,0:T(8,128)(2,1)}, u32[]{:S(2)}, u32[]{:S(2)}) collective-permute-start(bf16[240,3072]{1,0:T(8,128)(2,1)} %pad_maximum_fusion), channel_id=1, source_target_pairs={{0,96},{8,104},{1,97},{9,105},{2,98},{10,106},{3,99},{11,107},{16,... | collective-permute-start | bytes 4423688 | tf_op jit(solution)/shard_map/ppermute | solution.py:46
  64.9 51.2 %collective-permute-start.8 = (bf16[240,3072]{1,0:T(8,128)(2,1)}, bf16[240,3072]{1,0:T(8,128)(2,1)}, u32[]{:S(2)}, u32[]{:S(2)}) collective-permute-start(bf16[240,3072]{1,0:T(8,128)(2,1)} %slice.21), channel_id=1, source_target_pairs={{0,32},{8,40},{1,33},{9,41},{2,34},{10,42},{3,35},{11,43},{16,48},... | collective-permute-start | bytes 4423688 | tf_op jit(solution)/shard_map/ppermute | solution.py:46
  83.5 1.0 copy-start.4
  101.6 24.9 %all-to-all-start.1 = ((bf16[8,128,768]{2,1,0:T(8,128)(2,1)}), bf16[8,128,768]{2,1,0:T(8,128)(2,1)S(1)}, u32[]{:S(2)}, u32[]{:S(2)}) async-start(bf16[8,128,768]{2,1,0:T(8,128)(2,1)} %attend.1), calls=%async_computation.1 | async-start | bytes 3145728 | tf_op jit(solution)/shard_map/all_to_all | solution.py:339
  106.1 20.4 %collective-permute-start.10 = (bf16[80,3072]{1,0:T(8,128)(2,1)}, bf16[80,3072]{1,0:T(8,128)(2,1)}, u32[]{:S(2)}, u32[]{:S(2)}) collective-permute-start(bf16[80,3072]{1,0:T(8,128)(2,1)} %copy-done.1), channel_id=1, source_target_pairs={{0,32},{8,40},{1,33},{9,41},{2,34},{10,42},{3,35},{11,43},{16,48},... | collective-permute-start | bytes 1474568 | tf_op jit(solution)/shard_map/ppermute | solution.py:46
  107.1 19.4 %collective-permute-start.11 = (bf16[80,3072]{1,0:T(8,128)(2,1)}, bf16[80,3072]{1,0:T(8,128)(2,1)}, u32[]{:S(2)}, u32[]{:S(2)}) collective-permute-start(bf16[80,3072]{1,0:T(8,128)(2,1)} %get-tuple-element.66), channel_id=1, source_target_pairs={{0,96},{8,104},{1,97},{9,105},{2,98},{10,106},{3,99},{11,107},{16,... | collective-permute-start | bytes 1474568 | tf_op jit(solution)/shard_map/ppermute | solution.py:46
  126.5 6.5 %collective-permute-start.12 = (bf16[8,128,768]{2,1,0:T(8,128)(2,1)S(1)}, bf16[8,128,768]{2,1,0:T(8,128)(2,1)S(1)}, u32[]{:S(2)}, u32[]{:S(2)}) collective-permute-start(bf16[8,128,768]{2,1,0:T(8,128)(2,1)S(1)} %all-to-all-done.1.own_ref), channel_id=1, source_target_pairs={{0,8},{8,0},{1,9},{9,1},{2,10},{10,2},{3,11},{11,3},{16,24},{24,16... | collective-permute-start | bytes 4718600 | tf_op jit(solution)/shard_map/ppermute | solution.py:46
  128.1 16.4 %collective-permute-start.15 = (bf16[160,3072]{1,0:T(8,128)(2,1)}, bf16[160,3072]{1,0:T(8,128)(2,1)S(1)}, u32[]{:S(2)}, u32[]{:S(2)}) collective-permute-start(bf16[160,3072]{1,0:T(8,128)(2,1)} %collective-permute-done.7.rest_6_), channel_id=1, source_target_pairs={{0,16},{8,28},{1,17},{9,29},{2,18},{10,30},{3,19},{11,31},{16,4},{... | collective-permute-start | bytes 2949128 | tf_op jit(solution)/shard_map/ppermute | solution.py:46
  130.3 14.1 %collective-permute-start.13 = (bf16[80,3072]{1,0:T(8,128)(2,1)}, bf16[80,3072]{1,0:T(8,128)(2,1)S(1)}, u32[]{:S(2)}, u32[]{:S(2)}) collective-permute-start(bf16[80,3072]{1,0:T(8,128)(2,1)} %collective-permute-done.10.rest_2_), channel_id=1, source_target_pairs={{0,32},{8,40},{1,33},{9,41},{2,34},{10,42},{3,35},{11,43},{16,48},... | collective-permute-start | bytes 1474568 | tf_op jit(solution)/shard_map/ppermute | solution.py:46
  130.4 14.0 %collective-permute-start.14 = (bf16[80,3072]{1,0:T(8,128)(2,1)}, bf16[80,3072]{1,0:T(8,128)(2,1)S(1)}, u32[]{:S(2)}, u32[]{:S(2)}) collective-permute-start(bf16[80,3072]{1,0:T(8,128)(2,1)} %collective-permute-done.11.rest_4_), channel_id=1, source_target_pairs={{0,96},{8,104},{1,97},{9,105},{2,98},{10,106},{3,99},{11,107},{16,... | collective-permute-start | bytes 1474568 | tf_op jit(solution)/shard_map/ppermute | solution.py:46
  144.4 5.7 %copy-start = (s32[17]{0:T(128)S(1)}, s32[17]{0:T(128)}, u32[]{:S(2)}) copy-start(s32[17]{0:T(128)} %stack.71.info_ref) | copy-start | bytes 208
  144.4 5.7 %collective-permute-start.16 = (bf16[2,128,2304]{2,1,0:T(8,128)(2,1)S(1)}, bf16[2,128,2304]{2,1,0:T(8,128)(2,1)S(1)}, u32[]{:S(2)}, u32[]{:S(2)}) collective-permute-start(bf16[2,128,2304]{2,1,0:T(8,128)(2,1)S(1)} %get-tuple-element.64), channel_id=1, source_target_pairs={{0,8},{8,0},{1,9},{9,1},{2,10},{10,2},{3,11},{11,3},{16,24},{24,16... | collective-permute-start | bytes 3538952 | tf_op jit(solution)/shard_map/ppermute | solution.py:46
  148.5 1.6 %collective-permute-start.17 = (bf16[2,128,384]{2,1,0:T(8,128)(2,1)S(1)}, bf16[2,128,384]{2,1,0:T(8,128)(2,1)S(1)}, u32[]{:S(2)}, u32[]{:S(2)}) collective-permute-start(bf16[2,128,384]{2,1,0:T(8,128)(2,1)S(1)} %get-tuple-element.65), channel_id=1, source_target_pairs={{0,8},{8,0},{1,9},{9,1},{2,10},{10,2},{3,11},{11,3},{16,24},{24,16... | collective-permute-start | bytes 589832 | tf_op jit(solution)/shard_map/ppermute | solution.py:46
  (1 other events, 0.9 us)

commit v6 on v5

--- a/solution.py
+++ b/solution.py
@@ -284,30 +284,38 @@
 
 
 def merge_body(spots, info_ref, *refs):
-    parts = (len(refs) - 2) // 2
-    out_refs = refs[2 * parts :]
+    parts = (len(refs) - 4) // 2
+    out_hbm = refs[2 * parts : 2 * parts + 2]
+    outs, sem = refs[2 * parts + 2 :]
     first = info_ref[8] == 0
-    for i, (part, at) in enumerate(spots):
-        own_ref, got_ref = refs[part], refs[parts + part]
-        cols = 2 * PIECE
-        column = pl.multiple_of(info_ref[9 + i] * cols, cols)
-        here = slice(at * PIECE, (at + 1) * PIECE)
-        for t in range(2):
+    copies = []
+    for t in range(2):
+        for i, (part, at) in enumerate(spots):
+            own_ref, got_ref = refs[part], refs[parts + part]
+            cols = 2 * PIECE
+            column = pl.multiple_of(info_ref[9 + i] * cols, cols)
+            here = slice(at * PIECE, (at + 1) * PIECE)
             own, got = own_ref[t, :, here], got_ref[t, :, here]
             low = jnp.where(first, own, got)
             high = jnp.where(first, got, own)
-            out_refs[t][:, pl.ds(column, cols)] = jnp.concatenate([low, high], axis=1)
+            outs[t, :, pl.ds(column, cols)] = jnp.concatenate([low, high], axis=1)
+        copies.append(pltpu.make_async_copy(outs.at[t], out_hbm[t], sem.at[t]))
+        copies[t].start()
+    for c in copies:
+        c.wait()
 
 
 def merge(info, spots, owns, gots, width):
     tokens = owns[0].shape[1]
     vmem = pl.BlockSpec(memory_space=pltpu.VMEM)
+    anywhere = pl.BlockSpec(memory_space=pl.ANY)
     out = jax.ShapeDtypeStruct((tokens, width), BF16)
     return pl.pallas_call(
         functools.partial(merge_body, spots),
         in_specs=[pl.BlockSpec(memory_space=pltpu.SMEM)] + [vmem] * (2 * len(owns)),
-        out_specs=[vmem, vmem],
+        out_specs=[anywhere, anywhere],
         out_shape=[out, out],
+        scratch_shapes=[pltpu.VMEM((2, tokens, width), BF16), pltpu.SemaphoreType.DMA((2,))],
         compiler_params=pltpu.CompilerParams(vmem_limit_bytes=12 * MIB),
         cost_estimate=NO_COST,
         name="merge",

time: 153 us -> 153 us (level)
  no operation moved by 1% of the time
where the time goes in v6:
time: 153 us
  waiting for transfers between devices  66 us (43%)
  Pallas kernels  41.9 us (27%)
  starting transfers between devices  33.3 us (22%)
  local copies, waits for them, and re-layouts  7.29 us (5%)
  other arithmetic  2.56 us (2%)
  between operations  1.59 us (1%)
    ppermute x18, waiting for transfers between devices, move(): return lax.ppermute(a, ('fsdp', 'seq'), perm)  49.5 us
    ppermute x18, starting transfers between devices, move(): return lax.ppermute(a, ('fsdp', 'seq'), perm)  23.8 us
    all_to_all x2, waiting for transfers between devices, exchange(): return lax.all_to_all(a, 'seq', split_axis=0, concat_axis=0, tiled=True)  16.4 us
    pallas_call x2, Pallas kernels, project(): pl.pallas_call(functools.partial(project_body, n, first, ready_rows, plan...  15.3 us
    pallas_call x1, Pallas kernels, attend(): pl.pallas_call(attn_body, grid=(width // (6 * HD),), in_specs=[pl.BlockSp...  11 us
    all_to_all x2, starting transfers between devices, exchange(): return lax.all_to_all(a, 'seq', split_axis=0, concat_axis=0, tiled=True)  9.48 us
    pallas_call x1, Pallas kernels, prepare(): pl.pallas_call(functools.partial(prepare_body, n), grid=(1,), in_specs=[p...  7.39 us
    pallas_call x1, Pallas kernels, norm_pack(): pl.pallas_call(norm_body, grid=(tokens // rows,), in_specs=[wide] * 6 + [...  5.85 us
  transfers between devices with their start and end apart: 20, of which 6 were waited for; matrix products, arithmetic and copies ran while one was open for 5% of the time, Pallas kernels for 26%

profile of v6, /device:TPU:1, one launch (start us, length us, event | category | flops | bytes accessed | tf_op | source)
XLA Modules:
  0.0 152.7 jit_solution(3649836533059614967)
XLA Ops:
  0.6 3.4 %collective-permute-start = (bf16[320,3072]{1,0:T(8,128)(2,1)}, bf16[320,3072]{1,0:T(8,128)(2,1)S(1)}, u32[]{:S(2)}, u32[]{:S(2)}) collective-permute-start(bf16[320,3072]{1,0:T(8,128)(2,1)} %bitcast.20), channel_id=1, source_target_pairs={{0,16},{8,28},{1,17},{9,29},{2,18},{10,30},{3,19},{11,31},{16,4},{... | collective-permute-start | bytes 5898248 | tf_op jit(solution)/shard_map/ppermute | solution.py:46
  4.0 1.3 slice.25
  5.3 1.4 collective-permute-start.1
  6.7 1.5 collective-permute-start.2
  9.0 5.9 %norm_pack.1 = bf16[8,128,2304]{2,1,0:T(8,128)(2,1)} custom-call(bf16[128,3072]{1,0:T(8,128)(2,1)} %q_ref.1, bf16[128,3072]{1,0:T(8,128)(2,1)} %qd_ref.1, bf16[128,3072]{1,0:T(8,128)(2,1)} %k_ref.1, bf16[128,3072]{1,0:T(8,128)(2,1)} %kd_ref.1, bf16[128,3072]{1,0:T(8,128)(2,1)} %v_ref.1, bf16[128,3072]{1,0:T(8,128)(2,1)} %vd_ref.1, f32[1,3072]{1,0:T(1,128)} %bitcast.24, ...), custom_call_target="tpu_custom_call" | custom-call | tf_op jit(solution)/shard_map/norm_pack/pallas_call | solution.py:81
  16.8 13.6 %collective-permute-done.1.rest_1_ = bf16[160,3072]{1,0:T(8,128)(2,1)} collective-permute-done((bf16[160,3072]{1,0:T(8,128)(2,1)S(1)}, bf16[160,3072]{1,0:T(8,128)(2,1)}, u32[]{:S(2)}, u32[]{:S(2)}) %collective-permute-start.1) | collective-permute-done | bytes 983072 | tf_op jit(solution)/shard_map/ppermute | solution.py:46
  30.5 5.0 %all-to-all-start = ((bf16[8,128,2304]{2,1,0:T(8,128)(2,1)}), bf16[8,128,2304]{2,1,0:T(8,128)(2,1)}, u32[]{:S(2)}, u32[]{:S(2)}) async-start(bf16[8,128,2304]{2,1,0:T(8,128)(2,1)} %norm_pack.1), calls=%async_computation | async-start | bytes 9437184 | tf_op jit(solution)/shard_map/all_to_all | solution.py:347
  36.8 2.6 %collective-permute-start.5 = (bf16[160,3072]{1,0:T(8,128)(2,1)S(1)}, bf16[160,3072]{1,0:T(8,128)(2,1)S(1)}, u32[]{:S(2)}, u32[]{:S(2)}) collective-permute-start(bf16[160,3072]{1,0:T(8,128)(2,1)S(1)} %slice.20), channel_id=1, source_target_pairs={{0,96},{8,104},{1,97},{9,105},{2,98},{10,106},{3,99},{11,107},{16,... | collective-permute-start | bytes 2949128 | tf_op jit(solution)/shard_map/ppermute | solution.py:46
  40.6 18.6 %collective-permute-done.5.rest_4_ = bf16[160,3072]{1,0:T(8,128)(2,1)S(1)} collective-permute-done((bf16[160,3072]{1,0:T(8,128)(2,1)S(1)}, bf16[160,3072]{1,0:T(8,128)(2,1)S(1)}, u32[]{:S(2)}, u32[]{:S(2)}) %collective-permute-start.5) | collective-permute-done | bytes 983072 | tf_op jit(solution)/shard_map/ppermute | solution.py:46
  59.2 3.5 %collective-permute-start.7 = (bf16[160,3072]{1,0:T(8,128)(2,1)S(1)}, bf16[160,3072]{1,0:T(8,128)(2,1)}, u32[]{:S(2)}, u32[]{:S(2)}) collective-permute-start(bf16[160,3072]{1,0:T(8,128)(2,1)S(1)} %collective-permute-done.5.rest_4_), channel_id=1, source_target_pairs={{0,96},{8,104},{1,97},{9,105},{2,98},{10,106},{3,99},{11,107},{16,... | collective-permute-start | bytes 2949128 | tf_op jit(solution)/shard_map/ppermute | solution.py:46
  64.9 1.4 collective-permute-start.8
  67.3 16.2 %collective-permute-done.6.rest_5_ = bf16[160,3072]{1,0:T(8,128)(2,1)S(1)} collective-permute-done((bf16[160,3072]{1,0:T(8,128)(2,1)}, bf16[160,3072]{1,0:T(8,128)(2,1)S(1)}, u32[]{:S(2)}, u32[]{:S(2)}) %collective-permute-start.6) | collective-permute-done | bytes 983072 | tf_op jit(solution)/shard_map/ppermute | solution.py:46
  84.5 6.1 %all-to-all-done.in_ref = bf16[8,128,2304]{2,1,0:T(8,128)(2,1)} async-done(((bf16[8,128,2304]{2,1,0:T(8,128)(2,1)}), bf16[8,128,2304]{2,1,0:T(8,128)(2,1)}, u32[]{:S(2)}, u32[]{:S(2)}) %all-to-all-start) | async-done | bytes 4718624 | tf_op jit(solution)/shard_map/all_to_all | solution.py:347
  90.6 11.0 %attend.1 = bf16[8,128,768]{2,1,0:T(8,128)(2,1)} custom-call(bf16[8,128,2304]{2,1,0:T(8,128)(2,1)} %all-to-all-done.in_ref), custom_call_target="tpu_custom_call" | custom-call | tf_op jit(solution)/shard_map/attend/pallas_call | solution.py:130
  101.6 4.4 %all-to-all-start.1 = ((bf16[8,128,768]{2,1,0:T(8,128)(2,1)}), bf16[8,128,768]{2,1,0:T(8,128)(2,1)S(1)}, u32[]{:S(2)}, u32[]{:S(2)}) async-start(bf16[8,128,768]{2,1,0:T(8,128)(2,1)} %attend.1), calls=%async_computation.1 | async-start | bytes 3145728 | tf_op jit(solution)/shard_map/all_to_all | solution.py:347
  107.1 1.6 %collective-permute-start.11 = (bf16[80,3072]{1,0:T(8,128)(2,1)}, bf16[80,3072]{1,0:T(8,128)(2,1)}, u32[]{:S(2)}, u32[]{:S(2)}) collective-permute-start(bf16[80,3072]{1,0:T(8,128)(2,1)} %get-tuple-element.66), channel_id=1, source_target_pairs={{0,96},{8,104},{1,97},{9,105},{2,98},{10,106},{3,99},{11,107},{16,... | collective-permute-start | bytes 1474568 | tf_op jit(solution)/shard_map/ppermute | solution.py:46
  108.7 7.4 %prepare.1 = (f32[2048,2560]{1,0:T(8,128)}, bf16[1280,3072]{1,0:T(8,128)(2,1)}) custom-call(s32[2]{0:T(128)} %pad_add_fusion.times_ref, s32[17]{0:T(128)} %stack.71.info_ref, f32[64,5120]{1,0:T(8,128)} %gate_hbm.1, f32[64,5120]{1,0:T(8,128)} %gate_dot_hbm.1, bf16[320,3072]{1,0:T(8,128)(2,1)} %bitcast.23, bf16[160,3072]{1,0:T(8,128)(2,1)} %collective-permute-done.1.rest_1_, ...), custom_call_target="tpu_custom_call" | custom-call | tf_op jit(solution)/shard_map/prepare/pallas_call | solution.py:178
  116.1 10.3 %all-to-all-done.1.own_ref = bf16[8,128,768]{2,1,0:T(8,128)(2,1)S(1)} async-done(((bf16[8,128,768]{2,1,0:T(8,128)(2,1)}), bf16[8,128,768]{2,1,0:T(8,128)(2,1)S(1)}, u32[]{:S(2)}, u32[]{:S(2)}) %all-to-all-start.1) | async-done | bytes 1572896 | tf_op jit(solution)/shard_map/all_to_all | solution.py:347
  126.5 1.6 %collective-permute-start.12 = (bf16[8,128,768]{2,1,0:T(8,128)(2,1)S(1)}, bf16[8,128,768]{2,1,0:T(8,128)(2,1)S(1)}, u32[]{:S(2)}, u32[]{:S(2)}) collective-permute-start(bf16[8,128,768]{2,1,0:T(8,128)(2,1)S(1)} %all-to-all-done.1.own_ref), channel_id=1, source_target_pairs={{0,8},{8,0},{1,9},{9,1},{2,10},{10,2},{3,11},{11,3},{16,24},{24,16... | collective-permute-start | bytes 4718600 | tf_op jit(solution)/shard_map/ppermute | solution.py:46
  128.1 2.3 %collective-permute-start.15 = (bf16[160,3072]{1,0:T(8,128)(2,1)}, bf16[160,3072]{1,0:T(8,128)(2,1)S(1)}, u32[]{:S(2)}, u32[]{:S(2)}) collective-permute-start(bf16[160,3072]{1,0:T(8,128)(2,1)} %collective-permute-done.7.rest_6_), channel_id=1, source_target_pairs={{0,16},{8,28},{1,17},{9,29},{2,18},{10,30},{3,19},{11,31},{16,4},{... | collective-permute-start | bytes 2949128 | tf_op jit(solution)/shard_map/ppermute | solution.py:46
  130.4 2.6 %collective-permute-start.14 = (bf16[80,3072]{1,0:T(8,128)(2,1)}, bf16[80,3072]{1,0:T(8,128)(2,1)S(1)}, u32[]{:S(2)}, u32[]{:S(2)}) collective-permute-start(bf16[80,3072]{1,0:T(8,128)(2,1)} %collective-permute-done.11.rest_4_), channel_id=1, source_target_pairs={{0,96},{8,104},{1,97},{9,105},{2,98},{10,106},{3,99},{11,107},{16,... | collective-permute-start | bytes 1474568 | tf_op jit(solution)/shard_map/ppermute | solution.py:46
  133.0 11.4 %project.2 = (bf16[2,128,2304]{2,1,0:T(8,128)(2,1)S(1)}, bf16[2,128,2304]{2,1,0:T(8,128)(2,1)S(1)}) custom-call(f32[2048,2560]{1,0:T(8,128)} %get-tuple-element.48.gates_any, bf16[8,128,768]{2,1,0:T(8,128)(2,1)S(1)} %all-to-all-done.1.own_ref, bf16[8,128,768]{2,1,0:T(8,128)(2,1)S(1)} %collective-permute-done.12.peer_ref, ...), custom_call_target="tpu_custom_call" | custom-call | tf_op jit(solution)/shard_map/project/pallas_call | solution.py:265
  144.5 3.9 %project.3 = (bf16[2,128,384]{2,1,0:T(8,128)(2,1)S(1)}, bf16[2,128,384]{2,1,0:T(8,128)(2,1)S(1)}) custom-call(f32[2048,2560]{1,0:T(8,128)} %get-tuple-element.48.gates_any, bf16[8,128,768]{2,1,0:T(8,128)(2,1)S(1)} %all-to-all-done.1.own_ref, bf16[8,128,768]{2,1,0:T(8,128)(2,1)S(1)} %collective-permute-done.12.peer_ref, ...), custom_call_target="tpu_custom_call" | custom-call | tf_op jit(solution)/shard_map/project/pallas_call | solution.py:265
  150.1 2.4 %merge.1 = (bf16[128,5120]{1,0:T(8,128)(2,1)}, bf16[128,5120]{1,0:T(8,128)(2,1)}) custom-call(s32[17]{0:T(128)S(1)} %copy-done, bf16[2,128,2304]{2,1,0:T(8,128)(2,1)S(1)} %get-tuple-element.59.refs_0_, bf16[2,128,384]{2,1,0:T(8,128)(2,1)S(1)} %get-tuple-element.63.refs_1_, bf16[2,128,2304]{2,1,0:T(8,128)(2,1)S(1)} %collective-permute-done.16.refs_2_, ...), custom_call_target="tpu_custom_call" | custom-call | tf_op jit(solution)/shard_map/merge/pallas_call | solution.py:313
  (40 shorter events, 11.6 us)
Async XLA Ops:
  0.6 29.8 %collective-permute-start = (bf16[320,3072]{1,0:T(8,128)(2,1)}, bf16[320,3072]{1,0:T(8,128)(2,1)S(1)}, u32[]{:S(2)}, u32[]{:S(2)}) collective-permute-start(bf16[320,3072]{1,0:T(8,128)(2,1)} %bitcast.20), channel_id=1, source_target_pairs={{0,16},{8,28},{1,17},{9,29},{2,18},{10,30},{3,19},{11,31},{16,4},{... | collective-permute-start | bytes 5898248 | tf_op jit(solution)/shard_map/ppermute | solution.py:46
  5.3 25.1 %collective-permute-start.1 = (bf16[160,3072]{1,0:T(8,128)(2,1)S(1)}, bf16[160,3072]{1,0:T(8,128)(2,1)}, u32[]{:S(2)}, u32[]{:S(2)}) collective-permute-start(bf16[160,3072]{1,0:T(8,128)(2,1)S(1)} %slice.25), channel_id=1, source_target_pairs={{0,32},{8,40},{1,33},{9,41},{2,34},{10,42},{3,35},{11,43},{16,48},... | collective-permute-start | bytes 2949128 | tf_op jit(solution)/shard_map/ppermute | solution.py:46
  6.7 23.8 %collective-permute-start.2 = (bf16[160,3072]{1,0:T(8,128)(2,1)S(1)}, bf16[160,3072]{1,0:T(8,128)(2,1)}, u32[]{:S(2)}, u32[]{:S(2)}) collective-permute-start(bf16[160,3072]{1,0:T(8,128)(2,1)S(1)} %slice.25), channel_id=1, source_target_pairs={{0,96},{8,104},{1,97},{9,105},{2,98},{10,106},{3,99},{11,107},{16,... | collective-permute-start | bytes 2949128 | tf_op jit(solution)/shard_map/ppermute | solution.py:46
  8.2 7.3 %collective-permute-start.3 = (s32[1]{0:T(128)}, s32[1]{0:T(128)}, u32[]{:S(2)}, u32[]{:S(2)}) collective-permute-start(s32[1]{0:T(128)} %param.23), channel_id=1, source_target_pairs={{0,8},{8,0},{1,9},{9,1},{2,10},{10,2},{3,11},{11,3},{16,24},{24,16... | collective-permute-start | bytes 20 | tf_op jit(solution)/shard_map/ppermute | solution.py:46
  30.5 60.1 %all-to-all-start = ((bf16[8,128,2304]{2,1,0:T(8,128)(2,1)}), bf16[8,128,2304]{2,1,0:T(8,128)(2,1)}, u32[]{:S(2)}, u32[]{:S(2)}) async-start(bf16[8,128,2304]{2,1,0:T(8,128)(2,1)} %norm_pack.1), calls=%async_computation | async-start | bytes 9437184 | tf_op jit(solution)/shard_map/all_to_all | solution.py:347
  36.8 22.5 %collective-permute-start.5 = (bf16[160,3072]{1,0:T(8,128)(2,1)S(1)}, bf16[160,3072]{1,0:T(8,128)(2,1)S(1)}, u32[]{:S(2)}, u32[]{:S(2)}) collective-permute-start(bf16[160,3072]{1,0:T(8,128)(2,1)S(1)} %slice.20), channel_id=1, source_target_pairs={{0,96},{8,104},{1,97},{9,105},{2,98},{10,106},{3,99},{11,107},{16,... | collective-permute-start | bytes 2949128 | tf_op jit(solution)/shard_map/ppermute | solution.py:46
  39.4 27.0 %collective-permute-start.4 = (bf16[160,3072]{1,0:T(8,128)(2,1)S(1)}, bf16[160,3072]{1,0:T(8,128)(2,1)S(1)}, u32[]{:S(2)}, u32[]{:S(2)}) collective-permute-start(bf16[160,3072]{1,0:T(8,128)(2,1)S(1)} %slice.20), channel_id=1, source_target_pairs={{0,32},{8,40},{1,33},{9,41},{2,34},{10,42},{3,35},{11,43},{16,48},... | collective-permute-start | bytes 2949128 | tf_op jit(solution)/shard_map/ppermute | solution.py:46
  40.6 42.9 %collective-permute-start.6 = (bf16[160,3072]{1,0:T(8,128)(2,1)}, bf16[160,3072]{1,0:T(8,128)(2,1)S(1)}, u32[]{:S(2)}, u32[]{:S(2)}) collective-permute-start(bf16[160,3072]{1,0:T(8,128)(2,1)} %collective-permute-done.1.rest_1_), channel_id=1, source_target_pairs={{0,32},{8,40},{1,33},{9,41},{2,34},{10,42},{3,35},{11,43},{16,48},... | collective-permute-start | bytes 2949128 | tf_op jit(solution)/shard_map/ppermute | solution.py:46
  59.2 5.6 %copy-start.2 = (bf16[160,3072]{1,0:T(8,128)(2,1)}, bf16[160,3072]{1,0:T(8,128)(2,1)S(1)}, u32[]{:S(2)}) copy-start(bf16[160,3072]{1,0:T(8,128)(2,1)S(1)} %collective-permute-done.5.rest_4_) | copy-start | bytes 2949124
  59.2 25.3 %collective-permute-start.7 = (bf16[160,3072]{1,0:T(8,128)(2,1)S(1)}, bf16[160,3072]{1,0:T(8,128)(2,1)}, u32[]{:S(2)}, u32[]{:S(2)}) collective-permute-start(bf16[160,3072]{1,0:T(8,128)(2,1)S(1)} %collective-permute-done.5.rest_4_), channel_id=1, source_target_pairs={{0,96},{8,104},{1,97},{9,105},{2,98},{10,106},{3,99},{11,107},{16,... | collective-permute-start | bytes 2949128 | tf_op jit(solution)/shard_map/ppermute | solution.py:46
  63.6 1.3 copy-start.1
  64.9 51.3 %collective-permute-start.9 = (bf16[240,3072]{1,0:T(8,128)(2,1)}, bf16[240,3072]{1,0:T(8,128)(2,1)}, u32[]{:S(2)}, u32[]{:S(2)}) collective-permute-start(bf16[240,3072]{1,0:T(8,128)(2,1)} %pad_maximum_fusion), channel_id=1, source_target_pairs={{0,96},{8,104},{1,97},{9,105},{2,98},{10,106},{3,99},{11,107},{16,... | collective-permute-start | bytes 4423688 | tf_op jit(solution)/shard_map/ppermute | solution.py:46
  64.9 51.2 %collective-permute-start.8 = (bf16[240,3072]{1,0:T(8,128)(2,1)}, bf16[240,3072]{1,0:T(8,128)(2,1)}, u32[]{:S(2)}, u32[]{:S(2)}) collective-permute-start(bf16[240,3072]{1,0:T(8,128)(2,1)} %slice.21), channel_id=1, source_target_pairs={{0,32},{8,40},{1,33},{9,41},{2,34},{10,42},{3,35},{11,43},{16,48},... | collective-permute-start | bytes 4423688 | tf_op jit(solution)/shard_map/ppermute | solution.py:46
  83.5 1.0 copy-start.4
  101.6 24.9 %all-to-all-start.1 = ((bf16[8,128,768]{2,1,0:T(8,128)(2,1)}), bf16[8,128,768]{2,1,0:T(8,128)(2,1)S(1)}, u32[]{:S(2)}, u32[]{:S(2)}) async-start(bf16[8,128,768]{2,1,0:T(8,128)(2,1)} %attend.1), calls=%async_computation.1 | async-start | bytes 3145728 | tf_op jit(solution)/shard_map/all_to_all | solution.py:347
  106.1 20.4 %collective-permute-start.10 = (bf16[80,3072]{1,0:T(8,128)(2,1)}, bf16[80,3072]{1,0:T(8,128)(2,1)}, u32[]{:S(2)}, u32[]{:S(2)}) collective-permute-start(bf16[80,3072]{1,0:T(8,128)(2,1)} %copy-done.1), channel_id=1, source_target_pairs={{0,32},{8,40},{1,33},{9,41},{2,34},{10,42},{3,35},{11,43},{16,48},... | collective-permute-start | bytes 1474568 | tf_op jit(solution)/shard_map/ppermute | solution.py:46
  107.1 19.4 %collective-permute-start.11 = (bf16[80,3072]{1,0:T(8,128)(2,1)}, bf16[80,3072]{1,0:T(8,128)(2,1)}, u32[]{:S(2)}, u32[]{:S(2)}) collective-permute-start(bf16[80,3072]{1,0:T(8,128)(2,1)} %get-tuple-element.66), channel_id=1, source_target_pairs={{0,96},{8,104},{1,97},{9,105},{2,98},{10,106},{3,99},{11,107},{16,... | collective-permute-start | bytes 1474568 | tf_op jit(solution)/shard_map/ppermute | solution.py:46
  126.5 6.5 %collective-permute-start.12 = (bf16[8,128,768]{2,1,0:T(8,128)(2,1)S(1)}, bf16[8,128,768]{2,1,0:T(8,128)(2,1)S(1)}, u32[]{:S(2)}, u32[]{:S(2)}) collective-permute-start(bf16[8,128,768]{2,1,0:T(8,128)(2,1)S(1)} %all-to-all-done.1.own_ref), channel_id=1, source_target_pairs={{0,8},{8,0},{1,9},{9,1},{2,10},{10,2},{3,11},{11,3},{16,24},{24,16... | collective-permute-start | bytes 4718600 | tf_op jit(solution)/shard_map/ppermute | solution.py:46
  128.1 16.4 %collective-permute-start.15 = (bf16[160,3072]{1,0:T(8,128)(2,1)}, bf16[160,3072]{1,0:T(8,128)(2,1)S(1)}, u32[]{:S(2)}, u32[]{:S(2)}) collective-permute-start(bf16[160,3072]{1,0:T(8,128)(2,1)} %collective-permute-done.7.rest_6_), channel_id=1, source_target_pairs={{0,16},{8,28},{1,17},{9,29},{2,18},{10,30},{3,19},{11,31},{16,4},{... | collective-permute-start | bytes 2949128 | tf_op jit(solution)/shard_map/ppermute | solution.py:46
  130.3 14.1 %collective-permute-start.13 = (bf16[80,3072]{1,0:T(8,128)(2,1)}, bf16[80,3072]{1,0:T(8,128)(2,1)S(1)}, u32[]{:S(2)}, u32[]{:S(2)}) collective-permute-start(bf16[80,3072]{1,0:T(8,128)(2,1)} %collective-permute-done.10.rest_2_), channel_id=1, source_target_pairs={{0,32},{8,40},{1,33},{9,41},{2,34},{10,42},{3,35},{11,43},{16,48},... | collective-permute-start | bytes 1474568 | tf_op jit(solution)/shard_map/ppermute | solution.py:46
  130.4 14.0 %collective-permute-start.14 = (bf16[80,3072]{1,0:T(8,128)(2,1)}, bf16[80,3072]{1,0:T(8,128)(2,1)S(1)}, u32[]{:S(2)}, u32[]{:S(2)}) collective-permute-start(bf16[80,3072]{1,0:T(8,128)(2,1)} %collective-permute-done.11.rest_4_), channel_id=1, source_target_pairs={{0,96},{8,104},{1,97},{9,105},{2,98},{10,106},{3,99},{11,107},{16,... | collective-permute-start | bytes 1474568 | tf_op jit(solution)/shard_map/ppermute | solution.py:46
  144.4 5.7 %copy-start = (s32[17]{0:T(128)S(1)}, s32[17]{0:T(128)}, u32[]{:S(2)}) copy-start(s32[17]{0:T(128)} %stack.71.info_ref) | copy-start | bytes 208
  144.4 5.7 %collective-permute-start.16 = (bf16[2,128,2304]{2,1,0:T(8,128)(2,1)S(1)}, bf16[2,128,2304]{2,1,0:T(8,128)(2,1)S(1)}, u32[]{:S(2)}, u32[]{:S(2)}) collective-permute-start(bf16[2,128,2304]{2,1,0:T(8,128)(2,1)S(1)} %get-tuple-element.64), channel_id=1, source_target_pairs={{0,8},{8,0},{1,9},{9,1},{2,10},{10,2},{3,11},{11,3},{16,24},{24,16... | collective-permute-start | bytes 3538952 | tf_op jit(solution)/shard_map/ppermute | solution.py:46
  148.5 1.6 %collective-permute-start.17 = (bf16[2,128,384]{2,1,0:T(8,128)(2,1)S(1)}, bf16[2,128,384]{2,1,0:T(8,128)(2,1)S(1)}, u32[]{:S(2)}, u32[]{:S(2)}) collective-permute-start(bf16[2,128,384]{2,1,0:T(8,128)(2,1)S(1)} %get-tuple-element.65), channel_id=1, source_target_pairs={{0,8},{8,0},{1,9},{9,1},{2,10},{10,2},{3,11},{11,3},{16,24},{24,16... | collective-permute-start | bytes 589832 | tf_op jit(solution)/shard_map/ppermute | solution.py:46
  (1 other events, 0.9 us)

commit v7 on v6

--- a/solution.py
+++ b/solution.py
@@ -135,7 +135,7 @@
         out_specs=pl.BlockSpec((groups, tokens, 2 * HD), lambda h: (0, 0, first + h)),
         out_shape=jax.ShapeDtypeStruct((groups, tokens, heads * 2 * HD), BF16),
         input_output_aliases={} if earlier is None else {1: 0},
-        compiler_params=pltpu.CompilerParams(vmem_limit_bytes=VMEM_ALL),
+        compiler_params=pltpu.CompilerParams(vmem_limit_bytes=VMEM_ALL - 3 * MIB // 2),
         cost_estimate=NO_COST,
         name="attend",
     )(packed, *(() if earlier is None else (earlier,)))

time: 153 us -> 153 us (level)
  no operation moved by 1% of the time
where the time goes in v7:
time: 153 us
  waiting for transfers between devices  66 us (43%)
  Pallas kernels  41.9 us (27%)
  starting transfers between devices  33.3 us (22%)
  local copies, waits for them, and re-layouts  7.29 us (5%)
  other arithmetic  2.56 us (2%)
  between operations  1.59 us (1%)
    ppermute x18, waiting for transfers between devices, move(): return lax.ppermute(a, ('fsdp', 'seq'), perm)  49.5 us
    ppermute x18, starting transfers between devices, move(): return lax.ppermute(a, ('fsdp', 'seq'), perm)  23.8 us
    all_to_all x2, waiting for transfers between devices, exchange(): return lax.all_to_all(a, 'seq', split_axis=0, concat_axis=0, tiled=True)  16.4 us
    pallas_call x2, Pallas kernels, project(): pl.pallas_call(functools.partial(project_body, n, first, ready_rows, plan...  15.3 us
    pallas_call x1, Pallas kernels, attend(): pl.pallas_call(attn_body, grid=(width // (6 * HD),), in_specs=[pl.BlockSp...  11 us
    all_to_all x2, starting transfers between devices, exchange(): return lax.all_to_all(a, 'seq', split_axis=0, concat_axis=0, tiled=True)  9.48 us
    pallas_call x1, Pallas kernels, prepare(): pl.pallas_call(functools.partial(prepare_body, n), grid=(1,), in_specs=[p...  7.39 us
    pallas_call x1, Pallas kernels, norm_pack(): pl.pallas_call(norm_body, grid=(tokens // rows,), in_specs=[wide] * 6 + [...  5.85 us
  transfers between devices with their start and end apart: 20, of which 6 were waited for; matrix products, arithmetic and copies ran while one was open for 5% of the time, Pallas kernels for 26%

profile of v7, /device:TPU:1, one launch (start us, length us, event | category | flops | bytes accessed | tf_op | source)
XLA Modules:
  0.0 152.7 jit_solution(3649836533059614967)
XLA Ops:
  0.6 3.4 %collective-permute-start = (bf16[320,3072]{1,0:T(8,128)(2,1)}, bf16[320,3072]{1,0:T(8,128)(2,1)S(1)}, u32[]{:S(2)}, u32[]{:S(2)}) collective-permute-start(bf16[320,3072]{1,0:T(8,128)(2,1)} %bitcast.20), channel_id=1, source_target_pairs={{0,16},{8,28},{1,17},{9,29},{2,18},{10,30},{3,19},{11,31},{16,4},{... | collective-permute-start | bytes 5898248 | tf_op jit(solution)/shard_map/ppermute | solution.py:46
  4.0 1.3 slice.25
  5.3 1.4 collective-permute-start.1
  6.7 1.5 collective-permute-start.2
  9.0 5.9 %norm_pack.1 = bf16[8,128,2304]{2,1,0:T(8,128)(2,1)} custom-call(bf16[128,3072]{1,0:T(8,128)(2,1)} %q_ref.1, bf16[128,3072]{1,0:T(8,128)(2,1)} %qd_ref.1, bf16[128,3072]{1,0:T(8,128)(2,1)} %k_ref.1, bf16[128,3072]{1,0:T(8,128)(2,1)} %kd_ref.1, bf16[128,3072]{1,0:T(8,128)(2,1)} %v_ref.1, bf16[128,3072]{1,0:T(8,128)(2,1)} %vd_ref.1, f32[1,3072]{1,0:T(1,128)} %bitcast.24, ...), custom_call_target="tpu_custom_call" | custom-call | tf_op jit(solution)/shard_map/norm_pack/pallas_call | solution.py:81
  16.8 13.6 %collective-permute-done.1.rest_1_ = bf16[160,3072]{1,0:T(8,128)(2,1)} collective-permute-done((bf16[160,3072]{1,0:T(8,128)(2,1)S(1)}, bf16[160,3072]{1,0:T(8,128)(2,1)}, u32[]{:S(2)}, u32[]{:S(2)}) %collective-permute-start.1) | collective-permute-done | bytes 983072 | tf_op jit(solution)/shard_map/ppermute | solution.py:46
  30.5 5.0 %all-to-all-start = ((bf16[8,128,2304]{2,1,0:T(8,128)(2,1)}), bf16[8,128,2304]{2,1,0:T(8,128)(2,1)}, u32[]{:S(2)}, u32[]{:S(2)}) async-start(bf16[8,128,2304]{2,1,0:T(8,128)(2,1)} %norm_pack.1), calls=%async_computation | async-start | bytes 9437184 | tf_op jit(solution)/shard_map/all_to_all | solution.py:347
  36.8 2.6 %collective-permute-start.5 = (bf16[160,3072]{1,0:T(8,128)(2,1)S(1)}, bf16[160,3072]{1,0:T(8,128)(2,1)S(1)}, u32[]{:S(2)}, u32[]{:S(2)}) collective-permute-start(bf16[160,3072]{1,0:T(8,128)(2,1)S(1)} %slice.20), channel_id=1, source_target_pairs={{0,96},{8,104},{1,97},{9,105},{2,98},{10,106},{3,99},{11,107},{16,... | collective-permute-start | bytes 2949128 | tf_op jit(solution)/shard_map/ppermute | solution.py:46
  40.6 18.6 %collective-permute-done.5.rest_4_ = bf16[160,3072]{1,0:T(8,128)(2,1)S(1)} collective-permute-done((bf16[160,3072]{1,0:T(8,128)(2,1)S(1)}, bf16[160,3072]{1,0:T(8,128)(2,1)S(1)}, u32[]{:S(2)}, u32[]{:S(2)}) %collective-permute-start.5) | collective-permute-done | bytes 983072 | tf_op jit(solution)/shard_map/ppermute | solution.py:46
  59.2 3.5 %collective-permute-start.7 = (bf16[160,3072]{1,0:T(8,128)(2,1)S(1)}, bf16[160,3072]{1,0:T(8,128)(2,1)}, u32[]{:S(2)}, u32[]{:S(2)}) collective-permute-start(bf16[160,3072]{1,0:T(8,128)(2,1)S(1)} %collective-permute-done.5.rest_4_), channel_id=1, source_target_pairs={{0,96},{8,104},{1,97},{9,105},{2,98},{10,106},{3,99},{11,107},{16,... | collective-permute-start | bytes 2949128 | tf_op jit(solution)/shard_map/ppermute | solution.py:46
  64.9 1.4 collective-permute-start.8
  67.3 16.2 %collective-permute-done.6.rest_5_ = bf16[160,3072]{1,0:T(8,128)(2,1)S(1)} collective-permute-done((bf16[160,3072]{1,0:T(8,128)(2,1)}, bf16[160,3072]{1,0:T(8,128)(2,1)S(1)}, u32[]{:S(2)}, u32[]{:S(2)}) %collective-permute-start.6) | collective-permute-done | bytes 983072 | tf_op jit(solution)/shard_map/ppermute | solution.py:46
  84.5 6.1 %all-to-all-done.in_ref = bf16[8,128,2304]{2,1,0:T(8,128)(2,1)} async-done(((bf16[8,128,2304]{2,1,0:T(8,128)(2,1)}), bf16[8,128,2304]{2,1,0:T(8,128)(2,1)}, u32[]{:S(2)}, u32[]{:S(2)}) %all-to-all-start) | async-done | bytes 4718624 | tf_op jit(solution)/shard_map/all_to_all | solution.py:347
  90.6 11.0 %attend.1 = bf16[8,128,768]{2,1,0:T(8,128)(2,1)} custom-call(bf16[8,128,2304]{2,1,0:T(8,128)(2,1)} %all-to-all-done.in_ref), custom_call_target="tpu_custom_call" | custom-call | tf_op jit(solution)/shard_map/attend/pallas_call | solution.py:130
  101.6 4.4 %all-to-all-start.1 = ((bf16[8,128,768]{2,1,0:T(8,128)(2,1)}), bf16[8,128,768]{2,1,0:T(8,128)(2,1)S(1)}, u32[]{:S(2)}, u32[]{:S(2)}) async-start(bf16[8,128,768]{2,1,0:T(8,128)(2,1)} %attend.1), calls=%async_computation.1 | async-start | bytes 3145728 | tf_op jit(solution)/shard_map/all_to_all | solution.py:347
  107.1 1.6 %collective-permute-start.11 = (bf16[80,3072]{1,0:T(8,128)(2,1)}, bf16[80,3072]{1,0:T(8,128)(2,1)}, u32[]{:S(2)}, u32[]{:S(2)}) collective-permute-start(bf16[80,3072]{1,0:T(8,128)(2,1)} %get-tuple-element.66), channel_id=1, source_target_pairs={{0,96},{8,104},{1,97},{9,105},{2,98},{10,106},{3,99},{11,107},{16,... | collective-permute-start | bytes 1474568 | tf_op jit(solution)/shard_map/ppermute | solution.py:46
  108.7 7.4 %prepare.1 = (f32[2048,2560]{1,0:T(8,128)}, bf16[1280,3072]{1,0:T(8,128)(2,1)}) custom-call(s32[2]{0:T(128)} %pad_add_fusion.times_ref, s32[17]{0:T(128)} %stack.71.info_ref, f32[64,5120]{1,0:T(8,128)} %gate_hbm.1, f32[64,5120]{1,0:T(8,128)} %gate_dot_hbm.1, bf16[320,3072]{1,0:T(8,128)(2,1)} %bitcast.23, bf16[160,3072]{1,0:T(8,128)(2,1)} %collective-permute-done.1.rest_1_, ...), custom_call_target="tpu_custom_call" | custom-call | tf_op jit(solution)/shard_map/prepare/pallas_call | solution.py:178
  116.1 10.3 %all-to-all-done.1.own_ref = bf16[8,128,768]{2,1,0:T(8,128)(2,1)S(1)} async-done(((bf16[8,128,768]{2,1,0:T(8,128)(2,1)}), bf16[8,128,768]{2,1,0:T(8,128)(2,1)S(1)}, u32[]{:S(2)}, u32[]{:S(2)}) %all-to-all-start.1) | async-done | bytes 1572896 | tf_op jit(solution)/shard_map/all_to_all | solution.py:347
  126.5 1.6 %collective-permute-start.12 = (bf16[8,128,768]{2,1,0:T(8,128)(2,1)S(1)}, bf16[8,128,768]{2,1,0:T(8,128)(2,1)S(1)}, u32[]{:S(2)}, u32[]{:S(2)}) collective-permute-start(bf16[8,128,768]{2,1,0:T(8,128)(2,1)S(1)} %all-to-all-done.1.own_ref), channel_id=1, source_target_pairs={{0,8},{8,0},{1,9},{9,1},{2,10},{10,2},{3,11},{11,3},{16,24},{24,16... | collective-permute-start | bytes 4718600 | tf_op jit(solution)/shard_map/ppermute | solution.py:46
  128.1 2.3 %collective-permute-start.15 = (bf16[160,3072]{1,0:T(8,128)(2,1)}, bf16[160,3072]{1,0:T(8,128)(2,1)S(1)}, u32[]{:S(2)}, u32[]{:S(2)}) collective-permute-start(bf16[160,3072]{1,0:T(8,128)(2,1)} %collective-permute-done.7.rest_6_), channel_id=1, source_target_pairs={{0,16},{8,28},{1,17},{9,29},{2,18},{10,30},{3,19},{11,31},{16,4},{... | collective-permute-start | bytes 2949128 | tf_op jit(solution)/shard_map/ppermute | solution.py:46
  130.4 2.6 %collective-permute-start.14 = (bf16[80,3072]{1,0:T(8,128)(2,1)}, bf16[80,3072]{1,0:T(8,128)(2,1)S(1)}, u32[]{:S(2)}, u32[]{:S(2)}) collective-permute-start(bf16[80,3072]{1,0:T(8,128)(2,1)} %collective-permute-done.11.rest_4_), channel_id=1, source_target_pairs={{0,96},{8,104},{1,97},{9,105},{2,98},{10,106},{3,99},{11,107},{16,... | collective-permute-start | bytes 1474568 | tf_op jit(solution)/shard_map/ppermute | solution.py:46
  133.0 11.4 %project.2 = (bf16[2,128,2304]{2,1,0:T(8,128)(2,1)S(1)}, bf16[2,128,2304]{2,1,0:T(8,128)(2,1)S(1)}) custom-call(f32[2048,2560]{1,0:T(8,128)} %get-tuple-element.48.gates_any, bf16[8,128,768]{2,1,0:T(8,128)(2,1)S(1)} %all-to-all-done.1.own_ref, bf16[8,128,768]{2,1,0:T(8,128)(2,1)S(1)} %collective-permute-done.12.peer_ref, ...), custom_call_target="tpu_custom_call" | custom-call | tf_op jit(solution)/shard_map/project/pallas_call | solution.py:265
  144.5 3.9 %project.3 = (bf16[2,128,384]{2,1,0:T(8,128)(2,1)S(1)}, bf16[2,128,384]{2,1,0:T(8,128)(2,1)S(1)}) custom-call(f32[2048,2560]{1,0:T(8,128)} %get-tuple-element.48.gates_any, bf16[8,128,768]{2,1,0:T(8,128)(2,1)S(1)} %all-to-all-done.1.own_ref, bf16[8,128,768]{2,1,0:T(8,128)(2,1)S(1)} %collective-permute-done.12.peer_ref, ...), custom_call_target="tpu_custom_call" | custom-call | tf_op jit(solution)/shard_map/project/pallas_call | solution.py:265
  150.1 2.4 %merge.1 = (bf16[128,5120]{1,0:T(8,128)(2,1)}, bf16[128,5120]{1,0:T(8,128)(2,1)}) custom-call(s32[17]{0:T(128)S(1)} %copy-done, bf16[2,128,2304]{2,1,0:T(8,128)(2,1)S(1)} %get-tuple-element.59.refs_0_, bf16[2,128,384]{2,1,0:T(8,128)(2,1)S(1)} %get-tuple-element.63.refs_1_, bf16[2,128,2304]{2,1,0:T(8,128)(2,1)S(1)} %collective-permute-done.16.refs_2_, ...), custom_call_target="tpu_custom_call" | custom-call | tf_op jit(solution)/shard_map/merge/pallas_call | solution.py:313
  (40 shorter events, 11.6 us)
Async XLA Ops:
  0.6 29.8 %collective-permute-start = (bf16[320,3072]{1,0:T(8,128)(2,1)}, bf16[320,3072]{1,0:T(8,128)(2,1)S(1)}, u32[]{:S(2)}, u32[]{:S(2)}) collective-permute-start(bf16[320,3072]{1,0:T(8,128)(2,1)} %bitcast.20), channel_id=1, source_target_pairs={{0,16},{8,28},{1,17},{9,29},{2,18},{10,30},{3,19},{11,31},{16,4},{... | collective-permute-start | bytes 5898248 | tf_op jit(solution)/shard_map/ppermute | solution.py:46
  5.3 25.1 %collective-permute-start.1 = (bf16[160,3072]{1,0:T(8,128)(2,1)S(1)}, bf16[160,3072]{1,0:T(8,128)(2,1)}, u32[]{:S(2)}, u32[]{:S(2)}) collective-permute-start(bf16[160,3072]{1,0:T(8,128)(2,1)S(1)} %slice.25), channel_id=1, source_target_pairs={{0,32},{8,40},{1,33},{9,41},{2,34},{10,42},{3,35},{11,43},{16,48},... | collective-permute-start | bytes 2949128 | tf_op jit(solution)/shard_map/ppermute | solution.py:46
  6.7 23.8 %collective-permute-start.2 = (bf16[160,3072]{1,0:T(8,128)(2,1)S(1)}, bf16[160,3072]{1,0:T(8,128)(2,1)}, u32[]{:S(2)}, u32[]{:S(2)}) collective-permute-start(bf16[160,3072]{1,0:T(8,128)(2,1)S(1)} %slice.25), channel_id=1, source_target_pairs={{0,96},{8,104},{1,97},{9,105},{2,98},{10,106},{3,99},{11,107},{16,... | collective-permute-start | bytes 2949128 | tf_op jit(solution)/shard_map/ppermute | solution.py:46
  8.2 7.3 %collective-permute-start.3 = (s32[1]{0:T(128)}, s32[1]{0:T(128)}, u32[]{:S(2)}, u32[]{:S(2)}) collective-permute-start(s32[1]{0:T(128)} %param.23), channel_id=1, source_target_pairs={{0,8},{8,0},{1,9},{9,1},{2,10},{10,2},{3,11},{11,3},{16,24},{24,16... | collective-permute-start | bytes 20 | tf_op jit(solution)/shard_map/ppermute | solution.py:46
  30.5 60.1 %all-to-all-start = ((bf16[8,128,2304]{2,1,0:T(8,128)(2,1)}), bf16[8,128,2304]{2,1,0:T(8,128)(2,1)}, u32[]{:S(2)}, u32[]{:S(2)}) async-start(bf16[8,128,2304]{2,1,0:T(8,128)(2,1)} %norm_pack.1), calls=%async_computation | async-start | bytes 9437184 | tf_op jit(solution)/shard_map/all_to_all | solution.py:347
  36.8 22.5 %collective-permute-start.5 = (bf16[160,3072]{1,0:T(8,128)(2,1)S(1)}, bf16[160,3072]{1,0:T(8,128)(2,1)S(1)}, u32[]{:S(2)}, u32[]{:S(2)}) collective-permute-start(bf16[160,3072]{1,0:T(8,128)(2,1)S(1)} %slice.20), channel_id=1, source_target_pairs={{0,96},{8,104},{1,97},{9,105},{2,98},{10,106},{3,99},{11,107},{16,... | collective-permute-start | bytes 2949128 | tf_op jit(solution)/shard_map/ppermute | solution.py:46
  39.4 27.0 %collective-permute-start.4 = (bf16[160,3072]{1,0:T(8,128)(2,1)S(1)}, bf16[160,3072]{1,0:T(8,128)(2,1)S(1)}, u32[]{:S(2)}, u32[]{:S(2)}) collective-permute-start(bf16[160,3072]{1,0:T(8,128)(2,1)S(1)} %slice.20), channel_id=1, source_target_pairs={{0,32},{8,40},{1,33},{9,41},{2,34},{10,42},{3,35},{11,43},{16,48},... | collective-permute-start | bytes 2949128 | tf_op jit(solution)/shard_map/ppermute | solution.py:46
  40.6 42.9 %collective-permute-start.6 = (bf16[160,3072]{1,0:T(8,128)(2,1)}, bf16[160,3072]{1,0:T(8,128)(2,1)S(1)}, u32[]{:S(2)}, u32[]{:S(2)}) collective-permute-start(bf16[160,3072]{1,0:T(8,128)(2,1)} %collective-permute-done.1.rest_1_), channel_id=1, source_target_pairs={{0,32},{8,40},{1,33},{9,41},{2,34},{10,42},{3,35},{11,43},{16,48},... | collective-permute-start | bytes 2949128 | tf_op jit(solution)/shard_map/ppermute | solution.py:46
  59.2 5.6 %copy-start.2 = (bf16[160,3072]{1,0:T(8,128)(2,1)}, bf16[160,3072]{1,0:T(8,128)(2,1)S(1)}, u32[]{:S(2)}) copy-start(bf16[160,3072]{1,0:T(8,128)(2,1)S(1)} %collective-permute-done.5.rest_4_) | copy-start | bytes 2949124
  59.2 25.3 %collective-permute-start.7 = (bf16[160,3072]{1,0:T(8,128)(2,1)S(1)}, bf16[160,3072]{1,0:T(8,128)(2,1)}, u32[]{:S(2)}, u32[]{:S(2)}) collective-permute-start(bf16[160,3072]{1,0:T(8,128)(2,1)S(1)} %collective-permute-done.5.rest_4_), channel_id=1, source_target_pairs={{0,96},{8,104},{1,97},{9,105},{2,98},{10,106},{3,99},{11,107},{16,... | collective-permute-start | bytes 2949128 | tf_op jit(solution)/shard_map/ppermute | solution.py:46
  63.6 1.3 copy-start.1
  64.9 51.3 %collective-permute-start.9 = (bf16[240,3072]{1,0:T(8,128)(2,1)}, bf16[240,3072]{1,0:T(8,128)(2,1)}, u32[]{:S(2)}, u32[]{:S(2)}) collective-permute-start(bf16[240,3072]{1,0:T(8,128)(2,1)} %pad_maximum_fusion), channel_id=1, source_target_pairs={{0,96},{8,104},{1,97},{9,105},{2,98},{10,106},{3,99},{11,107},{16,... | collective-permute-start | bytes 4423688 | tf_op jit(solution)/shard_map/ppermute | solution.py:46
  64.9 51.2 %collective-permute-start.8 = (bf16[240,3072]{1,0:T(8,128)(2,1)}, bf16[240,3072]{1,0:T(8,128)(2,1)}, u32[]{:S(2)}, u32[]{:S(2)}) collective-permute-start(bf16[240,3072]{1,0:T(8,128)(2,1)} %slice.21), channel_id=1, source_target_pairs={{0,32},{8,40},{1,33},{9,41},{2,34},{10,42},{3,35},{11,43},{16,48},... | collective-permute-start | bytes 4423688 | tf_op jit(solution)/shard_map/ppermute | solution.py:46
  83.5 1.0 copy-start.4
  101.6 24.9 %all-to-all-start.1 = ((bf16[8,128,768]{2,1,0:T(8,128)(2,1)}), bf16[8,128,768]{2,1,0:T(8,128)(2,1)S(1)}, u32[]{:S(2)}, u32[]{:S(2)}) async-start(bf16[8,128,768]{2,1,0:T(8,128)(2,1)} %attend.1), calls=%async_computation.1 | async-start | bytes 3145728 | tf_op jit(solution)/shard_map/all_to_all | solution.py:347
  106.1 20.4 %collective-permute-start.10 = (bf16[80,3072]{1,0:T(8,128)(2,1)}, bf16[80,3072]{1,0:T(8,128)(2,1)}, u32[]{:S(2)}, u32[]{:S(2)}) collective-permute-start(bf16[80,3072]{1,0:T(8,128)(2,1)} %copy-done.1), channel_id=1, source_target_pairs={{0,32},{8,40},{1,33},{9,41},{2,34},{10,42},{3,35},{11,43},{16,48},... | collective-permute-start | bytes 1474568 | tf_op jit(solution)/shard_map/ppermute | solution.py:46
  107.1 19.4 %collective-permute-start.11 = (bf16[80,3072]{1,0:T(8,128)(2,1)}, bf16[80,3072]{1,0:T(8,128)(2,1)}, u32[]{:S(2)}, u32[]{:S(2)}) collective-permute-start(bf16[80,3072]{1,0:T(8,128)(2,1)} %get-tuple-element.66), channel_id=1, source_target_pairs={{0,96},{8,104},{1,97},{9,105},{2,98},{10,106},{3,99},{11,107},{16,... | collective-permute-start | bytes 1474568 | tf_op jit(solution)/shard_map/ppermute | solution.py:46
  126.5 6.5 %collective-permute-start.12 = (bf16[8,128,768]{2,1,0:T(8,128)(2,1)S(1)}, bf16[8,128,768]{2,1,0:T(8,128)(2,1)S(1)}, u32[]{:S(2)}, u32[]{:S(2)}) collective-permute-start(bf16[8,128,768]{2,1,0:T(8,128)(2,1)S(1)} %all-to-all-done.1.own_ref), channel_id=1, source_target_pairs={{0,8},{8,0},{1,9},{9,1},{2,10},{10,2},{3,11},{11,3},{16,24},{24,16... | collective-permute-start | bytes 4718600 | tf_op jit(solution)/shard_map/ppermute | solution.py:46
  128.1 16.4 %collective-permute-start.15 = (bf16[160,3072]{1,0:T(8,128)(2,1)}, bf16[160,3072]{1,0:T(8,128)(2,1)S(1)}, u32[]{:S(2)}, u32[]{:S(2)}) collective-permute-start(bf16[160,3072]{1,0:T(8,128)(2,1)} %collective-permute-done.7.rest_6_), channel_id=1, source_target_pairs={{0,16},{8,28},{1,17},{9,29},{2,18},{10,30},{3,19},{11,31},{16,4},{... | collective-permute-start | bytes 2949128 | tf_op jit(solution)/shard_map/ppermute | solution.py:46
  130.3 14.1 %collective-permute-start.13 = (bf16[80,3072]{1,0:T(8,128)(2,1)}, bf16[80,3072]{1,0:T(8,128)(2,1)S(1)}, u32[]{:S(2)}, u32[]{:S(2)}) collective-permute-start(bf16[80,3072]{1,0:T(8,128)(2,1)} %collective-permute-done.10.rest_2_), channel_id=1, source_target_pairs={{0,32},{8,40},{1,33},{9,41},{2,34},{10,42},{3,35},{11,43},{16,48},... | collective-permute-start | bytes 1474568 | tf_op jit(solution)/shard_map/ppermute | solution.py:46
  130.4 14.0 %collective-permute-start.14 = (bf16[80,3072]{1,0:T(8,128)(2,1)}, bf16[80,3072]{1,0:T(8,128)(2,1)S(1)}, u32[]{:S(2)}, u32[]{:S(2)}) collective-permute-start(bf16[80,3072]{1,0:T(8,128)(2,1)} %collective-permute-done.11.rest_4_), channel_id=1, source_target_pairs={{0,96},{8,104},{1,97},{9,105},{2,98},{10,106},{3,99},{11,107},{16,... | collective-permute-start | bytes 1474568 | tf_op jit(solution)/shard_map/ppermute | solution.py:46
  144.4 5.7 %copy-start = (s32[17]{0:T(128)S(1)}, s32[17]{0:T(128)}, u32[]{:S(2)}) copy-start(s32[17]{0:T(128)} %stack.71.info_ref) | copy-start | bytes 208
  144.4 5.7 %collective-permute-start.16 = (bf16[2,128,2304]{2,1,0:T(8,128)(2,1)S(1)}, bf16[2,128,2304]{2,1,0:T(8,128)(2,1)S(1)}, u32[]{:S(2)}, u32[]{:S(2)}) collective-permute-start(bf16[2,128,2304]{2,1,0:T(8,128)(2,1)S(1)} %get-tuple-element.64), channel_id=1, source_target_pairs={{0,8},{8,0},{1,9},{9,1},{2,10},{10,2},{3,11},{11,3},{16,24},{24,16... | collective-permute-start | bytes 3538952 | tf_op jit(solution)/shard_map/ppermute | solution.py:46
  148.5 1.6 %collective-permute-start.17 = (bf16[2,128,384]{2,1,0:T(8,128)(2,1)S(1)}, bf16[2,128,384]{2,1,0:T(8,128)(2,1)S(1)}, u32[]{:S(2)}, u32[]{:S(2)}) collective-permute-start(bf16[2,128,384]{2,1,0:T(8,128)(2,1)S(1)} %get-tuple-element.65), channel_id=1, source_target_pairs={{0,8},{8,0},{1,9},{9,1},{2,10},{10,2},{3,11},{11,3},{16,24},{24,16... | collective-permute-start | bytes 589832 | tf_op jit(solution)/shard_map/ppermute | solution.py:46
  (1 other events, 0.9 us)
